TPU v7x, 128 devices: a whole 4x4x4 slice. The times are simulated.
128 devices in a mesh: blk: 4 (over x_lo, core), shard: 32 (over z, y, x_hi).
Axes of the slice: x: 4 (x_hi: 2, x_lo: 2; x = x_hi * 2 + x_lo), y: 4, z: 4, core: 2. Of those that a mesh axis runs over, the one named last changes fastest.
Arguments:
- embeddings: bfloat16 [8, 512, 1024], P('blk', 'shard'), may hold values from -170 to 170
- centroids: bfloat16 [65536, 1024], P(('blk', 'shard')), may hold values from -6 to 6
- prices: int32 [65536], P(('blk', 'shard')), may hold values from 0 to 4095
Outputs:
- weights: float32 [8, 512, 65536], P(None, None, ('blk', 'shard'))
- centroid_sums: float32 [65536, 1024], P(('blk', 'shard'))
- loads: float32 [65536], P(('blk', 'shard'))
All inputs are finite; a program needn't handle non-finite values.
Results may differ from a plain program's by a relative error of at most 0.0035.
Values may be sent and summed in bfloat16 or wider, within the bound.
No kernel may reach another device: no remote copies, remote signals or barrier semaphores. Data moves between devices by JAX's collectives and lax.ppermute only.
A program may use at most 128 MiB of HBM per device.

v0:
```python
import math

import jax
import jax.numpy as jnp
from jax import lax
from jax.sharding import PartitionSpec as P


def passed_along(shard, axis, by):
    length = lax.axis_size(axis)
    return lax.ppermute(shard, axis, [(i, (i + by) % length) for i in range(length)])


def merge_stats(top, total):
    global_top = lax.pmax(top, ("blk", "shard"))
    scaled = total * jnp.exp(top - global_top)
    return (global_top, lax.psum(scaled, ("blk", "shard")))


def per_device(embeddings, centroids, prices):
    groups = lax.axis_size("blk")
    members = lax.axis_size("shard")
    here = lax.axis_index("blk")
    batch_group, rows_dev, width = embeddings.shape
    cent_dev = centroids.shape[0]
    rows_all = rows_dev * members
    total_cent = cent_dev * groups * members
    total_rows = batch_group * groups * rows_all
    scale = 1.0 / math.sqrt(width)
    bias = prices.astype(jnp.float32) / 1024.0
    top_all = jnp.zeros((groups, batch_group, rows_all), jnp.float32)
    total_all = jnp.zeros((groups, batch_group, rows_all), jnp.float32)
    kept_rows = []
    kept_scores = []
    moving = embeddings
    for step in range(groups):
        home = (here - step) % groups
        block = lax.all_gather(moving, "shard", axis=1, tiled=True)
        scores = (
            jnp.einsum("mrd,kd->mrk", block, centroids, preferred_element_type=jnp.float32) * scale
            - bias
        )
        top = jnp.max(scores, axis=-1)
        top, total = (top, jnp.sum(jnp.exp(scores - top[..., None]), axis=-1))
        top_all = lax.dynamic_update_index_in_dim(top_all, top, home, 0)
        total_all = lax.dynamic_update_index_in_dim(total_all, total, home, 0)
        kept_rows.append(block)
        kept_scores.append(scores)
        if step + 1 < groups:
            moving = passed_along(moving, "blk", 1)
    top_all, total_all = merge_stats(top_all, total_all)
    lse_all = top_all + jnp.log(total_all)
    weight_all = jnp.zeros((groups, batch_group, rows_all, cent_dev), jnp.float32)
    sums = jnp.zeros((cent_dev, width), jnp.float32)
    load_sum = jnp.zeros((cent_dev,), jnp.float32)
    for step in range(groups):
        home = (here - step) % groups
        block = kept_rows[step]
        scores = kept_scores[step]
        lse_block = lax.dynamic_index_in_dim(lse_all, home, 0, keepdims=False)
        weight_block = float(total_cent) * jnp.exp(scores - lse_block[..., None])
        part_sums = jnp.einsum(
            "mrk,mrd->kd",
            weight_block.astype(jnp.bfloat16),
            block,
            preferred_element_type=jnp.float32,
        )
        weight_block, part_sums, part_load = (
            weight_block,
            part_sums,
            jnp.sum(weight_block, axis=(0, 1)),
        )
        weight_all = lax.dynamic_update_index_in_dim(weight_all, weight_block, home, 0)
        sums = sums + part_sums
        load_sum = load_sum + part_load
    weights = weight_all.reshape(groups * batch_group, rows_all, cent_dev)
    centroid_sums = sums / math.sqrt(total_rows)
    loads = load_sum / float(total_rows)
    return (weights, centroid_sums, loads)


def solution(mesh):
    placed = (P("blk", "shard", None), P(("blk", "shard"), None), P(("blk", "shard")))
    return jax.shard_map(
        per_device,
        mesh=mesh,
        in_specs=placed,
        out_specs=(P(None, None, ("blk", "shard")), P(("blk", "shard"), None), P(("blk", "shard"))),
        check_vma=False,
    )
```

profile of v0, /device:TPU:1, one launch (start us, length us, event | category | flops | bytes accessed | tf_op | source)
XLA Modules:
  0.0 479.1 jit_solution(8127377866435946485)
XLA Ops:
  7.2 0.7 all-gather.5.cloned.1.call-update
  8.0 2.7 collective-permute-start
  10.6 1.6 collective-permute-done
  12.3 0.6 copy-done.13
  13.0 2.3 collective-permute-start.1
  15.3 1.6 collective-permute-done.1
  17.0 0.6 copy-done.14
  17.6 2.3 collective-permute-start.2
  20.0 1.6 collective-permute-done.2
  21.6 0.6 copy-done.15
  22.3 0.7 convert_multiply_fusion
  23.0 61.0 %all-gather.5.cloned.1.call-done = bf16[2,512,1024]{2,1,0:T(8,128)(2,1)} async-done(((bf16[2,16,1024]{2,1,0:T(8,128)(2,1)}), bf16[2,512,1024]{2,1,0:T(8,128)(2,1)}) %all-gather.5.cloned.1.call-update) | async-done | bytes 2097168 | tf_op jit(solution)/shard_map/all_gather | solution.py:38
  84.0 2.9 fusion.36
  86.9 1.3 copy-done.1
  88.6 68.1 %all-gather.7.cloned.1.call-done = bf16[2,512,1024]{2,1,0:T(8,128)(2,1)} async-done(((bf16[2,16,1024]{2,1,0:T(8,128)(2,1)}), bf16[2,512,1024]{2,1,0:T(8,128)(2,1)}) %all-gather.7.cloned.1.call-update) | async-done | bytes 2097168 | tf_op jit(solution)/shard_map/all_gather | solution.py:38
  156.7 2.9 fusion.37
  159.6 1.4 copy-done.3
  161.0 0.3 exponential_reduce_fusion.2
  161.3 67.5 %all-gather.9.cloned.1.call-done = bf16[2,512,1024]{2,1,0:T(8,128)(2,1)} async-done(((bf16[2,16,1024]{2,1,0:T(8,128)(2,1)}), bf16[2,512,1024]{2,1,0:T(8,128)(2,1)}) %all-gather.9.cloned.1.call-update) | async-done | bytes 2097168 | tf_op jit(solution)/shard_map/all_gather | solution.py:38
  228.8 2.9 fusion.38
  231.7 1.3 copy-done.5
  233.0 0.3 exponential_reduce_fusion.1
  233.4 67.5 %all-gather.11.cloned.1.call-done = bf16[2,512,1024]{2,1,0:T(8,128)(2,1)} async-done(((bf16[2,16,1024]{2,1,0:T(8,128)(2,1)}), bf16[2,512,1024]{2,1,0:T(8,128)(2,1)}) %all-gather.11.cloned.1.call-update) | async-done | bytes 2097168 | tf_op jit(solution)/shard_map/all_gather | solution.py:38
  300.8 2.9 fusion.39
  304.0 65.0 %pmax.7 = f32[4,2,512]{2,1,0:T(2,128)S(1)} all-reduce(f32[4,2,512]{2,1,0:T(2,128)S(1)} %bitcast_dynamic-update-slice_fusion.4), channel_id=1, replica_groups=mesh['blk'=4,'shard'=32] {'blk','shard'}, use_global_device_ids=true, to_apply=%region_4.5 | all-reduce | flops 4096 | bytes 32768 | tf_op jit(solution)/shard_map/pmax | solution.py:15
  369.1 62.9 %psum.7 = f32[4,2,512]{2,1,0:T(2,128)S(1)} all-reduce(f32[4,2,512]{2,1,0:T(2,128)S(1)} %bitcast.85), channel_id=1, replica_groups=mesh['blk'=4,'shard'=32] {'blk','shard'}, use_global_device_ids=true, to_apply=%region_9.10 | all-reduce | flops 4096 | bytes 32768 | tf_op jit(solution)/shard_map/psum | solution.py:17
  432.0 4.3 fusion.7
  436.3 2.9 copy.8
  439.2 2.9 copy.9
  442.2 4.9 %fusion.1 = (f32[512]{0:T(512)S(1)}, f32[1,2,512,512]{2,3,1,0:T(8,128)}, f32[1,2,512,512]{2,3,1,0:T(8,128)}, f32[512]{0:T(512)S(1)}) fusion(f32[2,512,512]{1,2,0:T(8,128)} %copy-done.1, f32[2,512]{1,0:T(2,128)S(1)} %get-tuple-element.14, f32[2,512,512]{1,2,0:T(8,128)} %copy-done.3, f32[2,512]{1,0:T(2,128)S(1)} %get-tuple-element.13), kind=kLoop, calls=%fused_computation.16 | loop fusion | flops 3144704 | bytes 8400896 | tf_op jit(solution)/shard_map/reduce_sum | solution.py:71
  447.1 2.9 copy.6
  450.0 2.9 copy.7
  452.8 1.1 broadcast_in_dim.53
  453.9 0.5 copy-done.11
  454.7 1.3 copy-done.10
  456.3 1.3 copy-done.9
  457.9 1.3 copy-done.8
  459.5 0.6 add_multiply_fusion
  460.1 1.5 copy-done.6
  461.6 2.2 copy-done.18
  463.8 1.3 fusion.14
  465.1 0.3 copy-done.4
  465.4 0.6 copy-done.17
  466.1 1.3 fusion.16
  467.6 0.6 copy-done.16
  468.3 1.3 fusion.18
  469.6 0.3 copy-done.12
  469.9 2.7 fusion
  (48 shorter events, 2.3 us)
Async XLA Ops:
  7.2 76.8 %copy-start = (bf16[512,1024]{1,0:T(8,128)(2,1)S(1)}, bf16[512,1024]{1,0:T(8,128)(2,1)}, u32[]{:S(2)}) copy-start(bf16[512,1024]{1,0:T(8,128)(2,1)} %param.4) | copy-start | bytes 3145732
  7.2 76.8 %all-gather.5.cloned.1.call-start = ((), (), s32[]{:S(2)}) async-start(), calls=%async_computation | async-start | bytes 2162688 | tf_op jit(solution)/shard_map/all_gather | solution.py:38
  7.9 148.8 %all-gather.7.cloned.1.call-start = ((), (), s32[]{:S(2)}) async-start(), calls=%async_computation.1 | async-start | bytes 2162688 | tf_op jit(solution)/shard_map/all_gather | solution.py:38
  8.0 4.3 collective-permute-start
  12.3 0.6 copy-start.13
  12.9 215.9 %all-gather.9.cloned.1.call-start = ((), (), s32[]{:S(2)}) async-start(), calls=%async_computation.2 | async-start | bytes 2162688 | tf_op jit(solution)/shard_map/all_gather | solution.py:38
  13.0 4.0 collective-permute-start.1
  17.0 0.6 copy-start.14
  17.6 283.2 %all-gather.11.cloned.1.call-start = ((), (), s32[]{:S(2)}) async-start(), calls=%async_computation.3 | async-start | bytes 2162688 | tf_op jit(solution)/shard_map/all_gather | solution.py:38
  17.6 4.0 collective-permute-start.2
  21.6 0.6 copy-start.15
  86.9 1.3 copy-start.1
  159.6 1.4 copy-start.3
  231.7 1.3 copy-start.5
  452.8 1.6 copy-start.11
  454.4 1.6 copy-start.10
  456.0 1.6 copy-start.9
  457.6 1.6 copy-start.8
  459.2 2.4 copy-start.6
  459.2 4.6 copy-start.18
  459.5 7.9 %copy-start.7 = (f32[4,2,512,512]{3,2,1,0:T(8,128)}, f32[4,2,512,512]{3,2,1,0:T(8,128)S(1)}, u32[]{:S(2)}) copy-start(f32[4,2,512,512]{3,2,1,0:T(8,128)S(1)} %constant_dynamic-update-slice_fusion) | copy-start | bytes 25165828
  463.8 1.6 copy-start.4
  463.8 2.2 copy-start.17
  466.1 1.6 copy-start.2
  466.1 2.2 copy-start.16
  468.3 1.6 copy-start.12
Sparse Core Ops, SparseCore 0:
  11.1 72.8 all-gather.4
  87.7 68.9 all-gather.6
  159.8 68.9 all-gather.8
  231.8 68.9 all-gather.10
where the time goes:
time: 480 us; the launch traced here: 479 us
  waiting for transfers between devices  270 us (56%)
  blocking collectives  128 us (27%)
  local copies, waits for them, and re-layouts  30.1 us (6%)
  matrix products  18.1 us (4%)
  between operations  14 us (3%)
  other arithmetic  11.7 us (2%)
  starting transfers between devices  7.47 us (2%)
    all_gather x4, waiting for transfers between devices, per_device(): block = lax.all_gather(moving, 'shard', axis=1, tiled=True)  264 us
    pmax x1, blocking collectives, merge_stats(): global_top = lax.pmax(top, ('blk', 'shard'))  65 us
    psum x1, blocking collectives, merge_stats(): return (global_top, lax.psum(scaled, ('blk', 'shard')))  62.9 us
    unnamed x38, local copies, waits for them, and re-layouts  16.3 us
    broadcast_in_dim x4, local copies, waits for them, and re-layouts, per_device(): lax.dynamic_update_index_in_dim(weight_all, weight_block, home, 0)  11.6 us
    dot_general x4, matrix products, per_device(): jnp.einsum('mrd,kd->mrk', block, centroids, preferred_element_type=jnp.fl...  11.6 us
  transfers between devices with their start and end apart: 7, of which 7 were waited for; matrix products, arithmetic and copies ran while one was open for 2% of the time, Pallas kernels for 0%

commit v1 on v0

v1 whole, which is shorter than its diff:
```python
import functools
import math

import jax
import jax.numpy as jnp
from jax import lax
from jax.experimental import pallas as pl
from jax.experimental.pallas import tpu as pltpu
from jax.sharding import PartitionSpec as P

AXES = ("blk", "shard")
SIDE = 4
LANES = 128


def place_of(device):
    blk, shard = divmod(device, 32)
    return {"x": (shard & 1) * 2 + (blk >> 1), "y": (shard >> 1) & 3, "z": shard >> 3, "c": blk & 1}


def device_at(x, y, z, c):
    return ((x & 1) * 2 + c) * 32 + z * 8 + y * 2 + (x >> 1)


def along(axis0, axis1, by):
    pairs = []
    for device in range(128):
        place = place_of(device)
        axis = axis1 if place["c"] else axis0
        place[axis] = (place[axis] + by) % SIDE
        pairs.append((device, device_at(**place)))
    return pairs


def to_core(value):
    pairs = []
    for device in range(128):
        place = place_of(device)
        place["c"] = 1 - place["c"]
        pairs.append((device, device_at(**place)))
    return lax.ppermute(value, AXES, pairs)


def shift(value, axes, by):
    return lax.ppermute(value, AXES, along(*axes, by))


ORDERS = (("x", "y"), ("y", "z"), ("z", "x"))


def spread(value, axes, here):
    out = jnp.zeros((SIDE,) + value.shape, value.dtype)
    out = lax.dynamic_update_index_in_dim(out, value, here, 0)
    for by in (2, 1, -1):
        got = shift(value, axes, by)
        out = lax.dynamic_update_index_in_dim(out, got, (here - by) % SIDE, 0)
    return out.reshape((SIDE * value.shape[0],) + value.shape[1:])


def score_kernel(scale, rows_ref, cent_ref, bias_ref, score_ref, stat_ref):
    rows = rows_ref.shape[0]
    tiles = rows // LANES
    lane = lax.broadcasted_iota(jnp.int32, (LANES, LANES), 1)
    for t in range(tiles):
        part = pl.ds(t * LANES, LANES)
        score = (
            lax.dot_general(
                rows_ref[part, :],
                cent_ref[...],
                (((1,), (1,)), ((), ())),
                preferred_element_type=jnp.float32,
            )
            * scale
            - bias_ref[...]
        )
        score_ref[part, :] = score
        top = jnp.max(score, axis=1, keepdims=True)
        total = jnp.sum(jnp.exp(score - top), axis=1, keepdims=True)
        both = jnp.where(lane == 0, top, total)
        flat = both.T
        stat_ref[t : t + 1, :] = flat[0:1, :]
        stat_ref[tiles + t : tiles + t + 1, :] = flat[1:2, :]


def score_block(rows, centroids, bias, scale):
    count, width = rows.shape
    cent = centroids.shape[0]
    return pl.pallas_call(
        functools.partial(score_kernel, scale),
        out_shape=(
            jax.ShapeDtypeStruct((count, cent), jnp.float32),
            jax.ShapeDtypeStruct((2 * count // LANES, LANES), jnp.float32),
        ),
        in_specs=[pl.BlockSpec(memory_space=pltpu.VMEM)] * 3,
        out_specs=[pl.BlockSpec(memory_space=pltpu.VMEM)] * 2,
        compiler_params=pltpu.CompilerParams(vmem_limit_bytes=24 * 2**20),
        cost_estimate=pl.CostEstimate(
            flops=2 * count * width * cent,
            bytes_accessed=2 * width * (count + cent) + 4 * count * cent,
            transcendentals=count * cent,
        ),
        name="scores",
    )(rows, centroids, bias)


def weight_kernel(
    pieces, total_cent, total_rows, where_ref, stat_a, stat_b, *refs
):
    scores = refs[:pieces]
    blocks = refs[pieces : 2 * pieces]
    out_ref, sums_ref, loads_ref = refs[2 * pieces : 2 * pieces + 3]
    staged, rounded, lse, sems = refs[2 * pieces + 3 :]
    core = where_ref[0]
    tiles = stat_a.shape[1] // 2

    top = jnp.maximum(stat_a[:, :tiles, :], stat_b[:, :tiles, :])
    total = stat_a[:, tiles:, :] * jnp.exp(stat_a[:, :tiles, :] - top) + stat_b[
        :, tiles:, :
    ] * jnp.exp(stat_b[:, :tiles, :] - top)
    lse[...] = top + jnp.log(total)

    def copies(i, kind):
        slot = i % 2
        here = where_ref[1 + i]
        if kind == 0:
            return [
                pltpu.make_async_copy(
                    staged.at[slot].reshape(4, 2, 2, 2, 16, 512).at[:, :, x_lo, j],
                    out_ref.at[x_lo, 0, j, here],
                    sems.at[slot],
                )
                for x_lo in range(2)
                for j in range(2)
            ]
        return [
            pltpu.make_async_copy(
                staged.at[slot].reshape(4, 4, 2, 16, 512).at[:, :, j],
                out_ref.at[lax.rem(here, 2), 1, j, :, :, lax.div(here, 2)],
                sems.at[slot],
            )
            for j in range(2)
        ]

    def on_kind(i, act):
        kind = core if i < pieces // 2 else 1 - core
        for k in range(2):

            @pl.when(kind == k)
            def _(k=k):
                for copy in copies(i, k):
                    act(copy)

    load = jnp.zeros((8, loads_ref.shape[1]), jnp.float32)
    for i in range(pieces):
        slot = i % 2
        if i >= 2:
            on_kind(i - 2, lambda c: c.wait())
        kind = core if i < pieces // 2 else 1 - core
        index = kind * SIDE + where_ref[1 + i]
        norm = lse[index]
        for t in range(tiles):
            part = pl.ds(t * LANES, LANES)
            column = jnp.broadcast_to(norm[t : t + 1, :], (LANES, LANES)).T
            column = jnp.concatenate([column] * (scores[i].shape[1] // LANES), axis=1)
            weight = total_cent * jnp.exp(scores[i][part, :] - column)
            staged[slot, part, :] = weight
            load = load + jnp.sum(weight.reshape(LANES // 8, 8, weight.shape[1]), axis=0)
            rounded[part, :] = weight.astype(jnp.bfloat16)
        on_kind(i, lambda c: c.start())
        part_sums = lax.dot_general(
            rounded[...],
            blocks[i][...],
            (((0,), (0,)), ((), ())),
            preferred_element_type=jnp.float32,
        )
        if i == 0:
            sums_ref[...] = part_sums
        elif i + 1 < pieces:
            sums_ref[...] += part_sums
        else:
            sums_ref[...] = (sums_ref[...] + part_sums) * (1.0 / math.sqrt(total_rows))
    loads_ref[...] = jnp.sum(load, axis=0, keepdims=True) * (1.0 / total_rows)
    on_kind(pieces - 2, lambda c: c.wait())
    on_kind(pieces - 1, lambda c: c.wait())


def weight_all(where, stat_a, stat_b, scores, blocks, total_cent, total_rows):
    pieces = len(scores)
    count, cent = scores[0].shape
    width = blocks[0].shape[1]
    vmem = pl.BlockSpec(memory_space=pltpu.VMEM)
    out, sums, loads = pl.pallas_call(
        functools.partial(weight_kernel, pieces, float(total_cent), float(total_rows)),
        out_shape=(
            jax.ShapeDtypeStruct((2, 2, 2, 4, 4, 2, 16, cent), jnp.float32),
            jax.ShapeDtypeStruct((cent, width), jnp.float32),
            jax.ShapeDtypeStruct((1, cent), jnp.float32),
        ),
        in_specs=[pl.BlockSpec(memory_space=pltpu.SMEM)] + [vmem] * (2 + 2 * pieces),
        out_specs=(pl.BlockSpec(memory_space=pl.ANY), vmem, vmem),
        scratch_shapes=[
            pltpu.VMEM((2, count, cent), jnp.float32),
            pltpu.VMEM((count, cent), jnp.bfloat16),
            pltpu.VMEM((stat_a.shape[0], stat_a.shape[1] // 2, LANES), jnp.float32),
            pltpu.SemaphoreType.DMA((2,)),
        ],
        compiler_params=pltpu.CompilerParams(vmem_limit_bytes=48 * 2**20),
        name="weights",
    )(where, stat_a, stat_b, *scores, *blocks)
    return out, sums, loads


def merged(stats):
    half = stats[0].shape[1] // 2
    tops = [s[:, :half] for s in stats]
    top = functools.reduce(jnp.maximum, tops)
    total = sum(s[:, half:] * jnp.exp(t - top) for s, t in zip(stats, tops))
    return jnp.concatenate([top, total], axis=1)


def per_device(embeddings, centroids, prices):
    blk, shard = lax.axis_index("blk"), lax.axis_index("shard")
    core = blk % 2
    at = {"x": (shard % 2) * 2 + blk // 2, "y": (shard // 2) % 4, "z": shard // 8}
    here = [jnp.where(core == 0, at[a], at[b]) for a, b in ORDERS]
    width = embeddings.shape[2]
    cent = centroids.shape[0]
    scale = 1.0 / math.sqrt(width)
    bias = (prices.astype(jnp.float32) / 1024.0).reshape(1, cent)
    total_cent = cent * 128
    total_rows = embeddings.shape[0] * embeddings.shape[1] * 128

    block = embeddings.reshape(-1, width)
    block = spread(block, ORDERS[0], here[0])
    block = spread(block, ORDERS[1], here[1])
    mine, theirs = [block], [to_core(block)]
    steps = (0, 1, -1, 2)
    for by in steps[1:]:
        got = shift(block, ORDERS[2], by)
        mine.append(got)
        theirs.append(to_core(got))
    blocks = mine + theirs
    other = jnp.where(core == 0, at["x"], at["z"])
    last = [(here[2] - by) % SIDE for by in steps] + [(other - by) % SIDE for by in steps]

    scores, stats = [], None
    for i, rows in enumerate(blocks):
        score, stat = score_block(rows, centroids, bias, scale)
        scores.append(score)
        if stats is None:
            stats = jnp.zeros((8,) + stat.shape, jnp.float32)
        kind = core if i < SIDE else 1 - core
        stats = lax.dynamic_update_index_in_dim(stats, stat, kind * SIDE + last[i], 0)
    for axes in ORDERS:
        stats = merged([stats] + [shift(stats, axes, by) for by in (2, 1, -1)])
    where = jnp.stack([core] + last).astype(jnp.int32)
    out, sums, loads = weight_all(
        where, stats, to_core(stats), scores, blocks, total_cent, total_rows
    )
    return out.reshape(8, 512, cent), sums, loads.reshape(cent)


def solution(mesh):
    placed = (P("blk", "shard", None), P(AXES, None), P(AXES))
    return jax.shard_map(
        per_device,
        mesh=mesh,
        in_specs=placed,
        out_specs=(P(None, None, AXES), P(AXES, None), P(AXES)),
        check_vma=False,
    )
```

time: 480 us -> 125 us (0.26)
  waiting for transfers between devices: 270 us -> 28.6 us
  blocking collectives: 128 us -> 0 us
  starting transfers between devices: 7.47 us -> 45.2 us
  local copies, waits for them, and re-layouts: 30.1 us -> 7.43 us
  matrix products: 18.1 us -> 0 us
  other arithmetic: 11.7 us -> 29.2 us
  Pallas kernels: 0 us -> 13.1 us
  between operations: 14 us -> 0.91 us
    all_gather x4 -> x0, waiting for transfers between devices: 264 us -> none  [per_device(): block = lax.all_gather(moving, 'shard', axis=1, tiled=True)]
    pmax x1 -> x0, blocking collectives: 65 us -> none  [merge_stats(): global_top = lax.pmax(top, ('blk', 'shard'))]
    psum x1 -> x0, blocking collectives: 62.9 us -> none  [merge_stats(): return (global_top, lax.psum(scaled, ('blk', 'shard')))]
    ppermute x3 -> x23, starting transfers between devices: 7.31 us -> 45.2 us  [the longest x18 24.6 us: shift(): return lax.ppermute(value, AXES, along(*axes, by))]
    pallas_call x0 -> x8, other arithmetic: none -> 28.3 us  [score_block(): pl.pallas_call(functools.partial(score_kernel, scale), out_shape=(jax.Sha...]
    ppermute x3 -> x23, waiting for transfers between devices: 4.94 us -> 28.6 us  [the longest x18 27.8 us: shift(): return lax.ppermute(value, AXES, along(*axes, by))]
    dot_general x8 -> x0, matrix products: 18.1 us -> none  [the longest x4 11.6 us: per_device(): jnp.einsum('mrd,kd->mrk', block, centroids, preferred_element_type=jnp.fl...]
    unnamed x38 -> x8, local copies, waits for them, and re-layouts: 16.3 us -> 2.46 us
  transfers between devices with their start and end apart: 7 -> 23, of which waited for: 7 -> 13; matrix products, arithmetic and copies ran while one was open for 2% -> 24% of each run, Pallas kernels for 0% -> 0%
where the time goes in v1:
time: 125 us; the launch traced here: 124 us
  starting transfers between devices  45.2 us (36%)
  other arithmetic  29.2 us (23%)
  waiting for transfers between devices  28.6 us (23%)
  Pallas kernels  13.1 us (10%)
  local copies, waits for them, and re-layouts  7.43 us (6%)
    pallas_call x8, other arithmetic, score_block(): pl.pallas_call(functools.partial(score_kernel, scale), out_shape=(jax.Sha...  28.3 us
    ppermute x18, waiting for transfers between devices, shift(): return lax.ppermute(value, AXES, along(*axes, by))  27.8 us
    ppermute x18, starting transfers between devices, shift(): return lax.ppermute(value, AXES, along(*axes, by))  24.6 us
    ppermute x5, starting transfers between devices, to_core(): return lax.ppermute(value, AXES, pairs)  20.6 us
    pallas_call x1, Pallas kernels, weight_all(): pl.pallas_call(functools.partial(weight_kernel, pieces, float(total_cent)...  13.1 us
  transfers between devices with their start and end apart: 23, of which 13 were waited for; matrix products, arithmetic and copies ran while one was open for 24% of the time, Pallas kernels for 0%

profile of v1, /device:TPU:1, one launch (start us, length us, event | category | flops | bytes accessed | tf_op | source)
XLA Modules:
  0.0 124.4 jit_solution(13345143783674834062)
XLA Ops:
  0.6 3.6 %collective-permute-start.2 = (bf16[32,1024]{1,0:T(8,128)(2,1)}, bf16[32,1024]{1,0:T(8,128)(2,1)S(1)}, u32[]{:S(2)}, u32[]{:S(2)}) collective-permute-start(bf16[32,1024]{1,0:T(8,128)(2,1)} %bitcast.61), channel_id=1, source_target_pairs={{0,65},{1,64},{2,67},{3,66},{4,69},{5,68},{6,71},{7,70},{8,73},{9,... | collective-permute-start | bytes 196616 | tf_op jit(solution)/shard_map/ppermute | solution.py:45
  4.3 1.6 %collective-permute-start = (bf16[32,1024]{1,0:T(8,128)(2,1)}, bf16[32,1024]{1,0:T(8,128)(2,1)S(1)}, u32[]{:S(2)}, u32[]{:S(2)}) collective-permute-start(bf16[32,1024]{1,0:T(8,128)(2,1)} %bitcast.63), channel_id=1, source_target_pairs={{0,1},{1,0},{2,3},{3,2},{4,5},{5,4},{6,7},{7,6},{8,9},{9,8},{10,11... | collective-permute-start | bytes 196616 | tf_op jit(solution)/shard_map/ppermute | solution.py:45
  5.9 0.9 bitcast_dynamic-update-slice_fusion.7
  6.8 2.4 %collective-permute-done = bf16[32,1024]{1,0:T(8,128)(2,1)S(1)} collective-permute-done((bf16[32,1024]{1,0:T(8,128)(2,1)}, bf16[32,1024]{1,0:T(8,128)(2,1)S(1)}, u32[]{:S(2)}, u32[]{:S(2)}) %collective-permute-start) | collective-permute-done | bytes 65568 | tf_op jit(solution)/shard_map/ppermute | solution.py:45
  9.2 0.6 collective-permute-done.1
  9.8 3.7 %collective-permute-start.3 = (bf16[128,1024]{1,0:T(8,128)(2,1)S(1)}, bf16[128,1024]{1,0:T(8,128)(2,1)S(1)}, u32[]{:S(2)}, u32[]{:S(2)}) collective-permute-start(bf16[128,1024]{1,0:T(8,128)(2,1)S(1)} %bitcast.49), channel_id=1, source_target_pairs={{0,4},{1,5},{2,6},{3,7},{4,0},{5,1},{6,2},{7,3},{8,12},{9,13},{10,... | collective-permute-start | bytes 786440 | tf_op jit(solution)/shard_map/ppermute | solution.py:45
  14.0 1.0 collective-permute-start.4
  15.0 1.1 broadcast_in_dim.61
  16.1 0.7 bitcast_dynamic-update-slice_fusion.3
  16.8 0.8 collective-permute-done.3
  17.6 0.7 bitcast_dynamic-update-slice_fusion.2
  18.3 2.4 %collective-permute-done.4 = bf16[128,1024]{1,0:T(8,128)(2,1)S(1)} collective-permute-done((bf16[128,1024]{1,0:T(8,128)(2,1)S(1)}, bf16[128,1024]{1,0:T(8,128)(2,1)S(1)}, u32[]{:S(2)}, u32[]{:S(2)}) %collective-permute-start.4) | collective-permute-done | bytes 262176 | tf_op jit(solution)/shard_map/ppermute | solution.py:45
  20.7 0.7 bitcast_dynamic-update-slice_fusion.1
  21.4 0.7 bitcast_dynamic-update-slice_fusion
  22.1 1.1 collective-permute-start.6
  23.2 1.6 %collective-permute-start.7 = (bf16[512,1024]{1,0:T(8,128)(2,1)}, bf16[512,1024]{1,0:T(8,128)(2,1)}, u32[]{:S(2)}, u32[]{:S(2)}) collective-permute-start(bf16[512,1024]{1,0:T(8,128)(2,1)} %bitcast.19.refs_8_), channel_id=1, source_target_pairs={{0,24},{1,25},{2,26},{3,27},{4,28},{5,29},{6,30},{7,31},{8,0},{9,1... | collective-permute-start | bytes 3145736 | tf_op jit(solution)/shard_map/ppermute | solution.py:45
  24.8 1.4 %collective-permute-start.8 = (bf16[512,1024]{1,0:T(8,128)(2,1)}, bf16[512,1024]{1,0:T(8,128)(2,1)}, u32[]{:S(2)}, u32[]{:S(2)}) collective-permute-start(bf16[512,1024]{1,0:T(8,128)(2,1)} %bitcast.19.refs_8_), channel_id=1, source_target_pairs={{0,16},{1,17},{2,18},{3,19},{4,20},{5,21},{6,22},{7,23},{8,24},{9,... | collective-permute-start | bytes 3145736 | tf_op jit(solution)/shard_map/ppermute | solution.py:45
  26.2 4.5 %collective-permute-start.9 = (bf16[512,1024]{1,0:T(8,128)(2,1)}, bf16[512,1024]{1,0:T(8,128)(2,1)}, u32[]{:S(2)}, u32[]{:S(2)}) collective-permute-start(bf16[512,1024]{1,0:T(8,128)(2,1)} %bitcast.19.refs_8_), channel_id=1, source_target_pairs={{0,32},{1,33},{2,34},{3,35},{4,36},{5,37},{6,38},{7,39},{8,40},{9,... | collective-permute-start | bytes 3145736 | tf_op jit(solution)/shard_map/ppermute | solution.py:41
  30.7 6.9 %collective-permute-done.6.refs_9_ = bf16[512,1024]{1,0:T(8,128)(2,1)} collective-permute-done((bf16[512,1024]{1,0:T(8,128)(2,1)}, bf16[512,1024]{1,0:T(8,128)(2,1)}, u32[]{:S(2)}, u32[]{:S(2)}) %collective-permute-start.6) | collective-permute-done | bytes 1048608 | tf_op jit(solution)/shard_map/ppermute | solution.py:45
  37.6 4.3 %collective-permute-start.10 = (bf16[512,1024]{1,0:T(8,128)(2,1)}, bf16[512,1024]{1,0:T(8,128)(2,1)}, u32[]{:S(2)}, u32[]{:S(2)}) collective-permute-start(bf16[512,1024]{1,0:T(8,128)(2,1)} %collective-permute-done.6.refs_9_), channel_id=1, source_target_pairs={{0,32},{1,33},{2,34},{3,35},{4,36},{5,37},{6,38},{7,39},{8,40},{9,... | collective-permute-start | bytes 3145736 | tf_op jit(solution)/shard_map/ppermute | solution.py:41
  41.9 6.2 %collective-permute-done.7.refs_10_ = bf16[512,1024]{1,0:T(8,128)(2,1)} collective-permute-done((bf16[512,1024]{1,0:T(8,128)(2,1)}, bf16[512,1024]{1,0:T(8,128)(2,1)}, u32[]{:S(2)}, u32[]{:S(2)}) %collective-permute-start.7) | collective-permute-done | bytes 1048608 | tf_op jit(solution)/shard_map/ppermute | solution.py:45
  48.1 4.6 %collective-permute-start.11 = (bf16[512,1024]{1,0:T(8,128)(2,1)}, bf16[512,1024]{1,0:T(8,128)(2,1)}, u32[]{:S(2)}, u32[]{:S(2)}) collective-permute-start(bf16[512,1024]{1,0:T(8,128)(2,1)} %collective-permute-done.7.refs_10_), channel_id=1, source_target_pairs={{0,32},{1,33},{2,34},{3,35},{4,36},{5,37},{6,38},{7,39},{8,40},{9,... | collective-permute-start | bytes 3145736 | tf_op jit(solution)/shard_map/ppermute | solution.py:41
  52.7 1.9 %collective-permute-start.12 = (bf16[512,1024]{1,0:T(8,128)(2,1)}, bf16[512,1024]{1,0:T(8,128)(2,1)}, u32[]{:S(2)}, u32[]{:S(2)}) collective-permute-start(bf16[512,1024]{1,0:T(8,128)(2,1)} %collective-permute-done.8.refs_11_), channel_id=1, source_target_pairs={{0,32},{1,33},{2,34},{3,35},{4,36},{5,37},{6,38},{7,39},{8,40},{9,... | collective-permute-start | bytes 3145736 | tf_op jit(solution)/shard_map/ppermute | solution.py:41
  54.6 0.8 convert_multiply_fusion
  55.4 3.3 %scores.15 = (f32[8,8,128]{2,1,0:T(8,128)S(1)}, f32[512,512]{1,0:T(8,128)S(1)}) fusion(f32[8,8,128]{2,1,0:T(8,128)S(1)} %broadcast_in_dim.60, s32[]{:T(128)S(6)} %select_n.176, bf16[512,1024]{1,0:T(8,128)(2,1)} %bitcast.19.refs_8_, bf16[512,1024]{1,0:T(8,128)(2,1)} %param.4, f32[1,512]{1,0:T(1,128)S(1)} %bitcast.53), kind=kCustom, calls=%fused_computation.40 | custom fusion | flops 536870912 | bytes 3151876 | tf_op jit(solution)/shard_map/scores/pallas_call | solution.py:88
  58.6 3.0 %scores.14 = (f32[8,8,128]{2,1,0:T(8,128)S(1)}, f32[512,512]{1,0:T(8,128)S(1)}) fusion(f32[8,8,128]{2,1,0:T(8,128)S(1)} %get-tuple-element.51, s32[]{:T(128)S(6)} %select_n.177, bf16[512,1024]{1,0:T(8,128)(2,1)} %collective-permute-done.6.refs_9_, bf16[512,1024]{1,0:T(8,128)(2,1)S(1)} %copy-done.2, f32[1,512]{1,0:T(1,128)S(1)} %bitcast.54), kind=kCustom, calls=%fused_computation.39 | custom fusion | flops 536870912 | bytes 3151876 | tf_op jit(solution)/shard_map/scores/pallas_call | solution.py:88
  61.6 3.3 %scores.13 = (f32[8,8,128]{2,1,0:T(8,128)S(1)}, f32[512,512]{1,0:T(8,128)S(1)}) fusion(f32[8,8,128]{2,1,0:T(8,128)S(1)} %get-tuple-element.47, s32[]{:T(128)S(6)} %select_n.178, bf16[512,1024]{1,0:T(8,128)(2,1)} %collective-permute-done.7.refs_10_, bf16[512,1024]{1,0:T(8,128)(2,1)} %param.4, f32[1,512]{1,0:T(1,128)S(1)} %bitcast.55), kind=kCustom, calls=%fused_computation.38 | custom fusion | flops 536870912 | bytes 3151876 | tf_op jit(solution)/shard_map/scores/pallas_call | solution.py:88
  64.9 3.7 %scores.12 = (f32[8,8,128]{2,1,0:T(8,128)S(1)}, f32[512,512]{1,0:T(8,128)}) fusion(f32[8,8,128]{2,1,0:T(8,128)S(1)} %get-tuple-element.55, s32[]{:T(128)S(6)} %select_n.179, bf16[512,1024]{1,0:T(8,128)(2,1)} %collective-permute-done.8.refs_11_, bf16[512,1024]{1,0:T(8,128)(2,1)S(1)} %copy-done.3, f32[1,512]{1,0:T(1,128)S(1)} %bitcast.56), kind=kCustom, calls=%fused_computation.37 | custom fusion | flops 536870912 | bytes 3151876 | tf_op jit(solution)/shard_map/scores/pallas_call | solution.py:88
  68.6 3.7 %scores.11 = (f32[8,8,128]{2,1,0:T(8,128)S(1)}, f32[512,512]{1,0:T(8,128)}) fusion(f32[8,8,128]{2,1,0:T(8,128)S(1)} %get-tuple-element.43, s32[]{:T(128)S(6)} %select_n.180, bf16[512,1024]{1,0:T(8,128)(2,1)} %collective-permute-done.9.refs_12_, bf16[512,1024]{1,0:T(8,128)(2,1)S(1)} %copy-done.3, f32[1,512]{1,0:T(1,128)S(1)} %bitcast.57), kind=kCustom, calls=%fused_computation.36 | custom fusion | flops 536870912 | bytes 3151876 | tf_op jit(solution)/shard_map/scores/pallas_call | solution.py:88
  72.3 3.8 %scores.10 = (f32[8,8,128]{2,1,0:T(8,128)S(1)}, f32[512,512]{1,0:T(8,128)}) fusion(f32[8,8,128]{2,1,0:T(8,128)S(1)} %get-tuple-element.59, s32[]{:T(128)S(6)} %select_n.181, bf16[512,1024]{1,0:T(8,128)(2,1)} %collective-permute-done.10.refs_13_, bf16[512,1024]{1,0:T(8,128)(2,1)S(1)} %copy-done.3, f32[1,512]{1,0:T(1,128)S(1)} %bitcast.58), kind=kCustom, calls=%fused_computation.35 | custom fusion | flops 536870912 | bytes 3151876 | tf_op jit(solution)/shard_map/scores/pallas_call | solution.py:88
  76.1 3.8 %scores.9 = (f32[8,8,128]{2,1,0:T(8,128)S(1)}, f32[512,512]{1,0:T(8,128)}) fusion(f32[8,8,128]{2,1,0:T(8,128)S(1)} %get-tuple-element.63, s32[]{:T(128)S(6)} %select_n.182, bf16[512,1024]{1,0:T(8,128)(2,1)} %collective-permute-done.11.refs_14_, bf16[512,1024]{1,0:T(8,128)(2,1)S(1)} %copy-done.3, f32[1,512]{1,0:T(1,128)S(1)} %bitcast.59), kind=kCustom, calls=%fused_computation.34 | custom fusion | flops 536870912 | bytes 3151876 | tf_op jit(solution)/shard_map/scores/pallas_call | solution.py:88
  79.9 3.7 %scores.8 = (f32[8,8,128]{2,1,0:T(8,128)S(1)}, f32[512,512]{1,0:T(8,128)}) fusion(f32[8,8,128]{2,1,0:T(8,128)S(1)} %get-tuple-element.67, s32[]{:T(128)S(6)} %select_n.183, bf16[512,1024]{1,0:T(8,128)(2,1)} %collective-permute-done.12.refs_15_, bf16[512,1024]{1,0:T(8,128)(2,1)S(1)} %copy-done.3, f32[1,512]{1,0:T(1,128)S(1)} %bitcast.60), kind=kCustom, calls=%fused_computation.33 | custom fusion | flops 536870912 | bytes 3151876 | tf_op jit(solution)/shard_map/scores/pallas_call | solution.py:88
  83.6 0.9 collective-permute-start.15
  84.5 0.6 collective-permute-start.14
  85.1 1.8 %collective-permute-start.13 = (f32[8,8,128]{2,1,0:T(8,128)S(1)}, f32[8,8,128]{2,1,0:T(8,128)S(1)}, u32[]{:S(2)}, u32[]{:S(2)}) collective-permute-start(f32[8,8,128]{2,1,0:T(8,128)S(1)} %get-tuple-element.71), channel_id=1, source_target_pairs={{0,1},{1,0},{2,3},{3,2},{4,5},{5,4},{6,7},{7,6},{8,9},{9,8},{10,11... | collective-permute-start | bytes 98312 | tf_op jit(solution)/shard_map/ppermute | solution.py:45
  86.9 1.6 %collective-permute-done.14 = f32[8,8,128]{2,1,0:T(8,128)S(1)} collective-permute-done((f32[8,8,128]{2,1,0:T(8,128)S(1)}, f32[8,8,128]{2,1,0:T(8,128)S(1)}, u32[]{:S(2)}, u32[]{:S(2)}) %collective-permute-start.14) | collective-permute-done | bytes 32800 | tf_op jit(solution)/shard_map/ppermute | solution.py:45
  88.5 0.9 collective-permute-done.13
  89.4 1.6 %collective-permute-start.18 = (f32[8,8,128]{2,1,0:T(8,128)S(1)}, f32[8,8,128]{2,1,0:T(8,128)S(1)}, u32[]{:S(2)}, u32[]{:S(2)}) collective-permute-start(f32[8,8,128]{2,1,0:T(8,128)S(1)} %pad_maximum_fusion), channel_id=1, source_target_pairs={{0,6},{1,7},{2,0},{3,1},{4,2},{5,3},{6,4},{7,5},{8,14},{9,15},{10,... | collective-permute-start | bytes 98312 | tf_op jit(solution)/shard_map/ppermute | solution.py:45
  91.0 1.4 %collective-permute-start.16 = (f32[8,8,128]{2,1,0:T(8,128)S(1)}, f32[8,8,128]{2,1,0:T(8,128)S(1)}, u32[]{:S(2)}, u32[]{:S(2)}) collective-permute-start(f32[8,8,128]{2,1,0:T(8,128)S(1)} %pad_maximum_fusion), channel_id=1, source_target_pairs={{0,4},{1,5},{2,6},{3,7},{4,0},{5,1},{6,2},{7,3},{8,12},{9,13},{10,... | collective-permute-start | bytes 98312 | tf_op jit(solution)/shard_map/ppermute | solution.py:45
  92.5 2.6 %collective-permute-done.17 = f32[8,8,128]{2,1,0:T(8,128)S(1)} collective-permute-done((f32[8,8,128]{2,1,0:T(8,128)S(1)}, f32[8,8,128]{2,1,0:T(8,128)S(1)}, u32[]{:S(2)}, u32[]{:S(2)}) %collective-permute-start.17) | collective-permute-done | bytes 32800 | tf_op jit(solution)/shard_map/ppermute | solution.py:45
  95.4 2.6 %collective-permute-start.21 = (f32[8,8,128]{2,1,0:T(8,128)S(1)}, f32[8,8,128]{2,1,0:T(8,128)S(1)}, u32[]{:S(2)}, u32[]{:S(2)}) collective-permute-start(f32[8,8,128]{2,1,0:T(8,128)S(1)} %pad_maximum_fusion.1), channel_id=1, source_target_pairs={{0,24},{1,25},{2,26},{3,27},{4,28},{5,29},{6,30},{7,31},{8,0},{9,1... | collective-permute-start | bytes 98312 | tf_op jit(solution)/shard_map/ppermute | solution.py:45
  98.1 1.3 %collective-permute-start.19 = (f32[8,8,128]{2,1,0:T(8,128)S(1)}, f32[8,8,128]{2,1,0:T(8,128)S(1)}, u32[]{:S(2)}, u32[]{:S(2)}) collective-permute-start(f32[8,8,128]{2,1,0:T(8,128)S(1)} %pad_maximum_fusion.1), channel_id=1, source_target_pairs={{0,16},{1,17},{2,18},{3,19},{4,20},{5,21},{6,22},{7,23},{8,24},{9,... | collective-permute-start | bytes 98312 | tf_op jit(solution)/shard_map/ppermute | solution.py:45
  99.3 2.7 %collective-permute-done.20 = f32[8,8,128]{2,1,0:T(8,128)S(1)} collective-permute-done((f32[8,8,128]{2,1,0:T(8,128)S(1)}, f32[8,8,128]{2,1,0:T(8,128)S(1)}, u32[]{:S(2)}, u32[]{:S(2)}) %collective-permute-start.20) | collective-permute-done | bytes 32800 | tf_op jit(solution)/shard_map/ppermute | solution.py:45
  102.4 5.4 %collective-permute-start.22 = (f32[8,8,128]{2,1,0:T(8,128)S(1)}, f32[8,8,128]{2,1,0:T(8,128)S(1)}, u32[]{:S(2)}, u32[]{:S(2)}) collective-permute-start(f32[8,8,128]{2,1,0:T(8,128)S(1)} %pad_maximum_fusion.2.stat_a), channel_id=1, source_target_pairs={{0,32},{1,33},{2,34},{3,35},{4,36},{5,37},{6,38},{7,39},{8,40},{9,... | collective-permute-start | bytes 98312 | tf_op jit(solution)/shard_map/ppermute | solution.py:41
  107.9 0.8 collective-permute-done.22.stat_b
  108.7 1.2 copy-done
  109.9 1.2 copy-done.1
  111.1 13.1 %weights.1 = (f32[2,2,2,4,4,2,16,512]{7,6,5,4,3,2,1,0:T(8,128)}, f32[512,1024]{1,0:T(8,128)}, f32[1,512]{1,0:T(1,128)}) custom-call(s32[9]{0:T(128)S(1)} %stack.39.where_ref, f32[8,8,128]{2,1,0:T(8,128)S(1)} %pad_maximum_fusion.2.stat_a, f32[8,8,128]{2,1,0:T(8,128)S(1)} %collective-permute-done.22.stat_b, f32[512,512]{1,0:T(8,128)S(1)} %get-tuple-element.52.refs_0_, ...), custom_call_target="tpu_custom_call" | custom-call | tf_op jit(solution)/shard_map/weights/pallas_call | solution.py:192
  (34 shorter events, 1.5 us)
Async XLA Ops:
  0.6 58.0 %copy-start.2 = (bf16[512,1024]{1,0:T(8,128)(2,1)S(1)}, bf16[512,1024]{1,0:T(8,128)(2,1)}, u32[]{:S(2)}) copy-start(bf16[512,1024]{1,0:T(8,128)(2,1)} %param.4) | copy-start | bytes 3145732
  0.6 9.2 %collective-permute-start.2 = (bf16[32,1024]{1,0:T(8,128)(2,1)}, bf16[32,1024]{1,0:T(8,128)(2,1)S(1)}, u32[]{:S(2)}, u32[]{:S(2)}) collective-permute-start(bf16[32,1024]{1,0:T(8,128)(2,1)} %bitcast.61), channel_id=1, source_target_pairs={{0,65},{1,64},{2,67},{3,66},{4,69},{5,68},{6,71},{7,70},{8,73},{9,... | collective-permute-start | bytes 196616 | tf_op jit(solution)/shard_map/ppermute | solution.py:45
  4.3 5.5 %collective-permute-start.1 = (bf16[32,1024]{1,0:T(8,128)(2,1)}, bf16[32,1024]{1,0:T(8,128)(2,1)S(1)}, u32[]{:S(2)}, u32[]{:S(2)}) collective-permute-start(bf16[32,1024]{1,0:T(8,128)(2,1)} %bitcast.62), channel_id=1, source_target_pairs={{0,64},{1,65},{2,66},{3,67},{4,68},{5,69},{6,70},{7,71},{8,72},{9,... | collective-permute-start | bytes 196616 | tf_op jit(solution)/shard_map/ppermute | solution.py:45
  4.3 4.9 %collective-permute-start = (bf16[32,1024]{1,0:T(8,128)(2,1)}, bf16[32,1024]{1,0:T(8,128)(2,1)S(1)}, u32[]{:S(2)}, u32[]{:S(2)}) collective-permute-start(bf16[32,1024]{1,0:T(8,128)(2,1)} %bitcast.63), channel_id=1, source_target_pairs={{0,1},{1,0},{2,3},{3,2},{4,5},{5,4},{6,7},{7,6},{8,9},{9,8},{10,11... | collective-permute-start | bytes 196616 | tf_op jit(solution)/shard_map/ppermute | solution.py:45
  9.8 7.7 %collective-permute-start.3 = (bf16[128,1024]{1,0:T(8,128)(2,1)S(1)}, bf16[128,1024]{1,0:T(8,128)(2,1)S(1)}, u32[]{:S(2)}, u32[]{:S(2)}) collective-permute-start(bf16[128,1024]{1,0:T(8,128)(2,1)S(1)} %bitcast.49), channel_id=1, source_target_pairs={{0,4},{1,5},{2,6},{3,7},{4,0},{5,1},{6,2},{7,3},{8,12},{9,13},{10,... | collective-permute-start | bytes 786440 | tf_op jit(solution)/shard_map/ppermute | solution.py:45
  13.5 7.9 %collective-permute-start.5 = (bf16[128,1024]{1,0:T(8,128)(2,1)S(1)}, bf16[128,1024]{1,0:T(8,128)(2,1)S(1)}, u32[]{:S(2)}, u32[]{:S(2)}) collective-permute-start(bf16[128,1024]{1,0:T(8,128)(2,1)S(1)} %bitcast.50), channel_id=1, source_target_pairs={{0,6},{1,7},{2,0},{3,1},{4,2},{5,3},{6,4},{7,5},{8,14},{9,15},{10,... | collective-permute-start | bytes 786440 | tf_op jit(solution)/shard_map/ppermute | solution.py:45
  14.0 6.7 %collective-permute-start.4 = (bf16[128,1024]{1,0:T(8,128)(2,1)S(1)}, bf16[128,1024]{1,0:T(8,128)(2,1)S(1)}, u32[]{:S(2)}, u32[]{:S(2)}) collective-permute-start(bf16[128,1024]{1,0:T(8,128)(2,1)S(1)} %bitcast.51), channel_id=1, source_target_pairs={{0,2},{1,3},{2,4},{3,5},{4,6},{5,7},{6,0},{7,1},{8,10},{9,11},{10,... | collective-permute-start | bytes 786440 | tf_op jit(solution)/shard_map/ppermute | solution.py:45
  22.1 15.5 %collective-permute-start.6 = (bf16[512,1024]{1,0:T(8,128)(2,1)}, bf16[512,1024]{1,0:T(8,128)(2,1)}, u32[]{:S(2)}, u32[]{:S(2)}) collective-permute-start(bf16[512,1024]{1,0:T(8,128)(2,1)} %bitcast.19.refs_8_), channel_id=1, source_target_pairs={{0,8},{1,9},{2,10},{3,11},{4,12},{5,13},{6,14},{7,15},{8,16},{9,17... | collective-permute-start | bytes 3145736 | tf_op jit(solution)/shard_map/ppermute | solution.py:45
  23.2 24.9 %collective-permute-start.7 = (bf16[512,1024]{1,0:T(8,128)(2,1)}, bf16[512,1024]{1,0:T(8,128)(2,1)}, u32[]{:S(2)}, u32[]{:S(2)}) collective-permute-start(bf16[512,1024]{1,0:T(8,128)(2,1)} %bitcast.19.refs_8_), channel_id=1, source_target_pairs={{0,24},{1,25},{2,26},{3,27},{4,28},{5,29},{6,30},{7,31},{8,0},{9,1... | collective-permute-start | bytes 3145736 | tf_op jit(solution)/shard_map/ppermute | solution.py:45
  24.8 27.9 %collective-permute-start.8 = (bf16[512,1024]{1,0:T(8,128)(2,1)}, bf16[512,1024]{1,0:T(8,128)(2,1)}, u32[]{:S(2)}, u32[]{:S(2)}) collective-permute-start(bf16[512,1024]{1,0:T(8,128)(2,1)} %bitcast.19.refs_8_), channel_id=1, source_target_pairs={{0,16},{1,17},{2,18},{3,19},{4,20},{5,21},{6,22},{7,23},{8,24},{9,... | collective-permute-start | bytes 3145736 | tf_op jit(solution)/shard_map/ppermute | solution.py:45
  26.2 42.4 %collective-permute-start.9 = (bf16[512,1024]{1,0:T(8,128)(2,1)}, bf16[512,1024]{1,0:T(8,128)(2,1)}, u32[]{:S(2)}, u32[]{:S(2)}) collective-permute-start(bf16[512,1024]{1,0:T(8,128)(2,1)} %bitcast.19.refs_8_), channel_id=1, source_target_pairs={{0,32},{1,33},{2,34},{3,35},{4,36},{5,37},{6,38},{7,39},{8,40},{9,... | collective-permute-start | bytes 3145736 | tf_op jit(solution)/shard_map/ppermute | solution.py:41
  37.6 34.7 %collective-permute-start.10 = (bf16[512,1024]{1,0:T(8,128)(2,1)}, bf16[512,1024]{1,0:T(8,128)(2,1)}, u32[]{:S(2)}, u32[]{:S(2)}) collective-permute-start(bf16[512,1024]{1,0:T(8,128)(2,1)} %collective-permute-done.6.refs_9_), channel_id=1, source_target_pairs={{0,32},{1,33},{2,34},{3,35},{4,36},{5,37},{6,38},{7,39},{8,40},{9,... | collective-permute-start | bytes 3145736 | tf_op jit(solution)/shard_map/ppermute | solution.py:41
  48.1 28.0 %collective-permute-start.11 = (bf16[512,1024]{1,0:T(8,128)(2,1)}, bf16[512,1024]{1,0:T(8,128)(2,1)}, u32[]{:S(2)}, u32[]{:S(2)}) collective-permute-start(bf16[512,1024]{1,0:T(8,128)(2,1)} %collective-permute-done.7.refs_10_), channel_id=1, source_target_pairs={{0,32},{1,33},{2,34},{3,35},{4,36},{5,37},{6,38},{7,39},{8,40},{9,... | collective-permute-start | bytes 3145736 | tf_op jit(solution)/shard_map/ppermute | solution.py:41
  52.7 27.2 %collective-permute-start.12 = (bf16[512,1024]{1,0:T(8,128)(2,1)}, bf16[512,1024]{1,0:T(8,128)(2,1)}, u32[]{:S(2)}, u32[]{:S(2)}) collective-permute-start(bf16[512,1024]{1,0:T(8,128)(2,1)} %collective-permute-done.8.refs_11_), channel_id=1, source_target_pairs={{0,32},{1,33},{2,34},{3,35},{4,36},{5,37},{6,38},{7,39},{8,40},{9,... | collective-permute-start | bytes 3145736 | tf_op jit(solution)/shard_map/ppermute | solution.py:41
  54.6 10.3 %copy-start.3 = (bf16[512,1024]{1,0:T(8,128)(2,1)S(1)}, bf16[512,1024]{1,0:T(8,128)(2,1)}, u32[]{:S(2)}) copy-start(bf16[512,1024]{1,0:T(8,128)(2,1)} %param.4) | copy-start | bytes 3145732
  83.6 3.2 %collective-permute-start.15 = (f32[8,8,128]{2,1,0:T(8,128)S(1)}, f32[8,8,128]{2,1,0:T(8,128)S(1)}, u32[]{:S(2)}, u32[]{:S(2)}) collective-permute-start(f32[8,8,128]{2,1,0:T(8,128)S(1)} %get-tuple-element.71), channel_id=1, source_target_pairs={{0,65},{1,64},{2,67},{3,66},{4,69},{5,68},{6,71},{7,70},{8,73},{9,... | collective-permute-start | bytes 98312 | tf_op jit(solution)/shard_map/ppermute | solution.py:45
  84.5 4.0 %collective-permute-start.14 = (f32[8,8,128]{2,1,0:T(8,128)S(1)}, f32[8,8,128]{2,1,0:T(8,128)S(1)}, u32[]{:S(2)}, u32[]{:S(2)}) collective-permute-start(f32[8,8,128]{2,1,0:T(8,128)S(1)} %get-tuple-element.71), channel_id=1, source_target_pairs={{0,64},{1,65},{2,66},{3,67},{4,68},{5,69},{6,70},{7,71},{8,72},{9,... | collective-permute-start | bytes 98312 | tf_op jit(solution)/shard_map/ppermute | solution.py:45
  85.1 4.3 %collective-permute-start.13 = (f32[8,8,128]{2,1,0:T(8,128)S(1)}, f32[8,8,128]{2,1,0:T(8,128)S(1)}, u32[]{:S(2)}, u32[]{:S(2)}) collective-permute-start(f32[8,8,128]{2,1,0:T(8,128)S(1)} %get-tuple-element.71), channel_id=1, source_target_pairs={{0,1},{1,0},{2,3},{3,2},{4,5},{5,4},{6,7},{7,6},{8,9},{9,8},{10,11... | collective-permute-start | bytes 98312 | tf_op jit(solution)/shard_map/ppermute | solution.py:45
  89.4 3.0 %collective-permute-start.18 = (f32[8,8,128]{2,1,0:T(8,128)S(1)}, f32[8,8,128]{2,1,0:T(8,128)S(1)}, u32[]{:S(2)}, u32[]{:S(2)}) collective-permute-start(f32[8,8,128]{2,1,0:T(8,128)S(1)} %pad_maximum_fusion), channel_id=1, source_target_pairs={{0,6},{1,7},{2,0},{3,1},{4,2},{5,3},{6,4},{7,5},{8,14},{9,15},{10,... | collective-permute-start | bytes 98312 | tf_op jit(solution)/shard_map/ppermute | solution.py:45
  91.0 4.0 %collective-permute-start.17 = (f32[8,8,128]{2,1,0:T(8,128)S(1)}, f32[8,8,128]{2,1,0:T(8,128)S(1)}, u32[]{:S(2)}, u32[]{:S(2)}) collective-permute-start(f32[8,8,128]{2,1,0:T(8,128)S(1)} %pad_maximum_fusion), channel_id=1, source_target_pairs={{0,2},{1,3},{2,4},{3,5},{4,6},{5,7},{6,0},{7,1},{8,10},{9,11},{10,... | collective-permute-start | bytes 98312 | tf_op jit(solution)/shard_map/ppermute | solution.py:45
  91.0 4.3 %collective-permute-start.16 = (f32[8,8,128]{2,1,0:T(8,128)S(1)}, f32[8,8,128]{2,1,0:T(8,128)S(1)}, u32[]{:S(2)}, u32[]{:S(2)}) collective-permute-start(f32[8,8,128]{2,1,0:T(8,128)S(1)} %pad_maximum_fusion), channel_id=1, source_target_pairs={{0,4},{1,5},{2,6},{3,7},{4,0},{5,1},{6,2},{7,3},{8,12},{9,13},{10,... | collective-permute-start | bytes 98312 | tf_op jit(solution)/shard_map/ppermute | solution.py:45
  95.4 3.9 %collective-permute-start.21 = (f32[8,8,128]{2,1,0:T(8,128)S(1)}, f32[8,8,128]{2,1,0:T(8,128)S(1)}, u32[]{:S(2)}, u32[]{:S(2)}) collective-permute-start(f32[8,8,128]{2,1,0:T(8,128)S(1)} %pad_maximum_fusion.1), channel_id=1, source_target_pairs={{0,24},{1,25},{2,26},{3,27},{4,28},{5,29},{6,30},{7,31},{8,0},{9,1... | collective-permute-start | bytes 98312 | tf_op jit(solution)/shard_map/ppermute | solution.py:45
  98.1 4.0 %collective-permute-start.20 = (f32[8,8,128]{2,1,0:T(8,128)S(1)}, f32[8,8,128]{2,1,0:T(8,128)S(1)}, u32[]{:S(2)}, u32[]{:S(2)}) collective-permute-start(f32[8,8,128]{2,1,0:T(8,128)S(1)} %pad_maximum_fusion.1), channel_id=1, source_target_pairs={{0,8},{1,9},{2,10},{3,11},{4,12},{5,13},{6,14},{7,15},{8,16},{9,17... | collective-permute-start | bytes 98312 | tf_op jit(solution)/shard_map/ppermute | solution.py:45
  98.1 4.3 %collective-permute-start.19 = (f32[8,8,128]{2,1,0:T(8,128)S(1)}, f32[8,8,128]{2,1,0:T(8,128)S(1)}, u32[]{:S(2)}, u32[]{:S(2)}) collective-permute-start(f32[8,8,128]{2,1,0:T(8,128)S(1)} %pad_maximum_fusion.1), channel_id=1, source_target_pairs={{0,16},{1,17},{2,18},{3,19},{4,20},{5,21},{6,22},{7,23},{8,24},{9,... | collective-permute-start | bytes 98312 | tf_op jit(solution)/shard_map/ppermute | solution.py:45
  102.4 6.2 %collective-permute-start.22 = (f32[8,8,128]{2,1,0:T(8,128)S(1)}, f32[8,8,128]{2,1,0:T(8,128)S(1)}, u32[]{:S(2)}, u32[]{:S(2)}) collective-permute-start(f32[8,8,128]{2,1,0:T(8,128)S(1)} %pad_maximum_fusion.2.stat_a), channel_id=1, source_target_pairs={{0,32},{1,33},{2,34},{3,35},{4,36},{5,37},{6,38},{7,39},{8,40},{9,... | collective-permute-start | bytes 98312 | tf_op jit(solution)/shard_map/ppermute | solution.py:41
  108.7 1.2 copy-start
  109.9 1.2 copy-start.1

commit v2 on v1

v2 whole, which is shorter than its diff:
```python
import functools
import math

import jax
import jax.numpy as jnp
from jax import lax
from jax.experimental import pallas as pl
from jax.experimental.pallas import tpu as pltpu
from jax.sharding import PartitionSpec as P

AXES = ("blk", "shard")
SIDE = 4
LANES = 128


def place_of(device):
    blk, shard = divmod(device, 32)
    return {"x": (shard & 1) * 2 + (blk >> 1), "y": (shard >> 1) & 3, "z": shard >> 3, "c": blk & 1}


def device_at(x, y, z, c):
    return ((x & 1) * 2 + c) * 32 + z * 8 + y * 2 + (x >> 1)


def along(axis0, axis1, by):
    pairs = []
    for device in range(128):
        place = place_of(device)
        axis = axis1 if place["c"] else axis0
        place[axis] = (place[axis] + by) % SIDE
        pairs.append((device, device_at(**place)))
    return pairs


def to_core(value):
    pairs = []
    for device in range(128):
        place = place_of(device)
        place["c"] = 1 - place["c"]
        pairs.append((device, device_at(**place)))
    return lax.ppermute(value, AXES, pairs)


def shift(value, axes, by):
    return lax.ppermute(value, AXES, along(*axes, by))


COST = 4
SLOTS = 3
CALLS = ((0,), (4,), (1, 2), (5, 6), (3,), (7,))
ORDERS = (("x", "y"), ("y", "z"), ("z", "x"))


def spread(value, axes, here):
    out = jnp.zeros((SIDE,) + value.shape, value.dtype)
    out = lax.dynamic_update_index_in_dim(out, value, here, 0)
    for by in (2, 1, -1):
        got = shift(value, axes, by)
        out = lax.dynamic_update_index_in_dim(out, got, (here - by) % SIDE, 0)
    return out.reshape((SIDE * value.shape[0],) + value.shape[1:])


def in_vmem(value):
    return pltpu.with_memory_space_constraint(value, pltpu.VMEM)


def score_kernel(scale, halves, *refs):
    rows = refs[:halves]
    cent_ref, bias_ref, score_ref, stat_ref, staged, sems = refs[halves:]
    half = rows[0].shape[0]
    tiles = half // LANES
    lane = lax.broadcasted_iota(jnp.int32, (LANES, LANES), 1)
    copies = []
    for h in range(halves):
        score = (
            lax.dot_general(
                rows[h][...],
                cent_ref[...],
                (((1,), (1,)), ((), ())),
                preferred_element_type=jnp.float32,
            )
            * scale
            - bias_ref[...]
        )
        if h >= 2:
            copies[h - 2].wait()
        staged[h % 2] = score
        copy = pltpu.make_async_copy(
            staged.at[h % 2], score_ref.at[h // 2, pl.ds(h % 2 * half, half)], sems.at[h % 2]
        )
        copy.start()
        copies.append(copy)
        for t in range(tiles):
            part = score[t * LANES : (t + 1) * LANES]
            top = jnp.max(part, axis=1, keepdims=True)
            total = jnp.sum(jnp.exp(part - top), axis=1, keepdims=True)
            flat = jnp.where(lane == 0, top, total).T
            row = h % 2 * tiles + t
            stat_ref[h // 2, row : row + 1, :] = flat[0:1, :]
            stat_ref[h // 2, 2 * tiles + row : 2 * tiles + row + 1, :] = flat[1:2, :]
    for copy in copies[-2:]:
        copy.wait()


def score_blocks(pieces, centroids, bias, scale):
    rows = [h for piece in pieces for h in piece]
    half, width = rows[0].shape
    cent = centroids.shape[0]
    vmem = pl.BlockSpec(memory_space=pltpu.VMEM)
    count = half * len(rows)
    return pl.pallas_call(
        functools.partial(score_kernel, scale, len(rows)),
        out_shape=(
            jax.ShapeDtypeStruct((len(pieces), 2 * half, cent), jnp.float32),
            jax.ShapeDtypeStruct((len(pieces), 4 * half // LANES, LANES), jnp.float32),
        ),
        in_specs=[vmem] * (len(rows) + 2),
        out_specs=(pl.BlockSpec(memory_space=pl.ANY), vmem),
        scratch_shapes=[
            pltpu.VMEM((2, half, cent), jnp.float32),
            pltpu.SemaphoreType.DMA((2,)),
        ],
        compiler_params=pltpu.CompilerParams(vmem_limit_bytes=8 * 2**20),
        cost_estimate=pl.CostEstimate(
            flops=COST * 2 * count * width * cent,
            bytes_accessed=2 * width * (count + cent) + 4 * count * cent,
            transcendentals=count * cent,
        ),
        name="scores",
    )(*[in_vmem(r) for r in rows], in_vmem(centroids), in_vmem(bias))


def weight_kernel(calls, pieces, total_cent, total_rows, where_ref, stat_a, stat_b, *refs):
    score_refs = refs[: len(calls)]
    block_refs = refs[len(calls) : len(calls) + 2 * pieces]
    out_ref, sums_ref, loads_ref = refs[len(calls) + 2 * pieces : len(calls) + 2 * pieces + 3]
    scores, blocks, staged, rounded, lse, sems, score_sems, block_sems = refs[
        len(calls) + 2 * pieces + 3 :
    ]
    tiles = stat_a.shape[1] // 2
    half = block_refs[0].shape[0]
    from_call = [(c, k) for c, n in enumerate(calls) for k in range(n)]

    def score_copy(i, h):
        call, k = from_call[i]
        part = pl.ds(h * half, half)
        return pltpu.make_async_copy(
            score_refs[call].at[k, part], scores.at[i, part], score_sems.at[i, h]
        )

    def block_copy(i, h):
        return pltpu.make_async_copy(
            block_refs[2 * i + h], blocks.at[i, pl.ds(h * half, half)], block_sems.at[i, h]
        )

    for i in range(pieces):
        for h in range(2):
            score_copy(i, h).start()
        for h in range(2):
            block_copy(i, h).start()

    top = jnp.maximum(stat_a[:, :tiles, :], stat_b[:, :tiles, :])
    total = stat_a[:, tiles:, :] * jnp.exp(stat_a[:, :tiles, :] - top) + stat_b[
        :, tiles:, :
    ] * jnp.exp(stat_b[:, :tiles, :] - top)
    lse[...] = top + jnp.log(total)

    def copies(i, kind):
        slot = i % SLOTS
        here = where_ref[pieces + i]
        if kind == 0:
            return [
                pltpu.make_async_copy(
                    staged.at[slot].reshape(4, 2, 2, 2, 16, 512).at[:, :, x_lo, j],
                    out_ref.at[x_lo, 0, j, here],
                    sems.at[slot],
                )
                for x_lo in range(2)
                for j in range(2)
            ]
        return [
            pltpu.make_async_copy(
                staged.at[slot].reshape(4, 4, 2, 16, 512).at[:, :, j],
                out_ref.at[lax.rem(here, 2), 1, j, :, :, lax.div(here, 2)],
                sems.at[slot],
            )
            for j in range(2)
        ]

    def on_kind(i, act):
        for k in range(2):

            @pl.when(where_ref[i] == k)
            def _(k=k):
                for copy in copies(i, k):
                    act(copy)

    def add_sums(i):
        for h in range(2):
            block_copy(i, h).wait()
        part_sums = lax.dot_general(
            rounded[i % 2],
            blocks[i],
            (((0,), (0,)), ((), ())),
            preferred_element_type=jnp.float32,
        )
        if i == 0:
            sums_ref[...] = part_sums
        elif i + 1 < pieces:
            sums_ref[...] += part_sums
        else:
            sums_ref[...] = (sums_ref[...] + part_sums) * (1.0 / math.sqrt(total_rows))

    load = jnp.zeros((8, loads_ref.shape[1]), jnp.float32)
    for i in range(pieces):
        slot = i % SLOTS
        if i >= SLOTS:
            on_kind(i - SLOTS, lambda c: c.wait())
        for h in range(2):
            score_copy(i, h).wait()
        norm = lse[where_ref[i] * SIDE + where_ref[pieces + i]]
        for t in range(tiles):
            part = pl.ds(t * LANES, LANES)
            column = jnp.broadcast_to(norm[t : t + 1, :], (LANES, LANES)).T
            column = jnp.concatenate([column] * (scores.shape[2] // LANES), axis=1)
            weight = total_cent * jnp.exp(scores[i, part, :] - column)
            staged[slot, part, :] = weight
            load = load + jnp.sum(weight.reshape(LANES // 8, 8, weight.shape[1]), axis=0)
            rounded[i % 2, part, :] = weight.astype(jnp.bfloat16)
        if i:
            add_sums(i - 1)
        on_kind(i, lambda c: c.start())
    add_sums(pieces - 1)
    loads_ref[...] = jnp.sum(load, axis=0, keepdims=True) * (1.0 / total_rows)
    for i in range(pieces - SLOTS, pieces):
        on_kind(i, lambda c: c.wait())


def weight_all(where, stat_a, stat_b, scores, blocks, total_cent, total_rows):
    calls = [score.shape[0] for score in scores]
    pieces = sum(calls)
    _, count, cent = scores[0].shape
    width = blocks[0].shape[1]
    vmem = pl.BlockSpec(memory_space=pltpu.VMEM)
    hbm = pl.BlockSpec(memory_space=pl.ANY)
    return pl.pallas_call(
        functools.partial(weight_kernel, calls, pieces, float(total_cent), float(total_rows)),
        out_shape=(
            jax.ShapeDtypeStruct((2, 2, 2, 4, 4, 2, 16, cent), jnp.float32),
            jax.ShapeDtypeStruct((cent, width), jnp.float32),
            jax.ShapeDtypeStruct((1, cent), jnp.float32),
        ),
        in_specs=[pl.BlockSpec(memory_space=pltpu.SMEM), vmem, vmem]
        + [hbm] * (len(scores) + len(blocks)),
        out_specs=(hbm, vmem, vmem),
        scratch_shapes=[
            pltpu.VMEM((pieces, count, cent), jnp.float32),
            pltpu.VMEM((pieces, count, width), jnp.bfloat16),
            pltpu.VMEM((SLOTS, count, cent), jnp.float32),
            pltpu.VMEM((2, count, cent), jnp.bfloat16),
            pltpu.VMEM((stat_a.shape[0], stat_a.shape[1] // 2, LANES), jnp.float32),
            pltpu.SemaphoreType.DMA((SLOTS,)),
            pltpu.SemaphoreType.DMA((pieces, 2)),
            pltpu.SemaphoreType.DMA((pieces, 2)),
        ],
        compiler_params=pltpu.CompilerParams(vmem_limit_bytes=30 * 2**20),
        name="weights",
    )(
        where,
        stat_a,
        stat_b,
        *[pltpu.with_memory_space_constraint(v, pltpu.HBM) for v in (*scores, *blocks)],
    )


def merged(stats):
    half = stats[0].shape[1] // 2
    tops = [s[:, :half] for s in stats]
    top = functools.reduce(jnp.maximum, tops)
    total = sum(s[:, half:] * jnp.exp(t - top) for s, t in zip(stats, tops))
    return jnp.concatenate([top, total], axis=1)


def per_device(embeddings, centroids, prices):
    blk, shard = lax.axis_index("blk"), lax.axis_index("shard")
    core = blk % 2
    at = {"x": (shard % 2) * 2 + blk // 2, "y": (shard // 2) % 4, "z": shard // 8}
    here = [jnp.where(core == 0, at[a], at[b]) for a, b in ORDERS]
    width = embeddings.shape[2]
    cent = centroids.shape[0]
    scale = 1.0 / math.sqrt(width)
    bias = (prices.astype(jnp.float32) / 1024.0).reshape(1, cent)
    total_cent = cent * 128
    total_rows = embeddings.shape[0] * embeddings.shape[1] * 128

    block = embeddings.reshape(-1, width)
    block = spread(block, ORDERS[0], here[0])
    block = spread(block, ORDERS[1], here[1])
    half = block.shape[0] // 2
    axes = ORDERS[2]
    own_a, own_b = block[:half], block[half:]
    before_a, before_b = shift(own_a, axes, 1), shift(own_b, axes, 1)
    after_b, after_a = shift(own_b, axes, -1), shift(own_a, axes, -1)
    across_a, across_b = shift(before_a, axes, 1), shift(after_b, axes, -1)
    steps = (0, 1, -1, 2)
    mine = [(own_a, own_b), (before_a, before_b), (after_a, after_b), (across_a, across_b)]
    their_own = to_core(block)
    theirs = [(their_own[:half], their_own[half:])]
    theirs += [tuple(to_core(h) for h in piece) for piece in mine[1:]]
    blocks = mine + theirs
    other = jnp.where(core == 0, at["x"], at["z"])
    last = [(here[2] - by) % SIDE for by in steps] + [(other - by) % SIDE for by in steps]

    stats = jnp.zeros((2 * SIDE, 8, LANES), jnp.float32)
    scores, order = [], []
    for call in CALLS:
        score, stat = score_blocks([blocks[i] for i in call], centroids, bias, scale)
        scores.append(score)
        order += call
        for k, i in enumerate(call):
            kind = core if i < SIDE else 1 - core
            stats = lax.dynamic_update_index_in_dim(stats, stat[k], kind * SIDE + last[i], 0)
    for axes in ORDERS:
        stats = merged([stats] + [shift(stats, axes, by) for by in (2, 1, -1)])
    kinds = [core if i < SIDE else 1 - core for i in order]
    where = jnp.stack(kinds + [last[i] for i in order]).astype(jnp.int32)
    out, sums, loads = weight_all(
        where,
        stats,
        to_core(stats),
        scores,
        [h for i in order for h in blocks[i]],
        total_cent,
        total_rows,
    )
    return out.reshape(8, 512, cent), sums, loads.reshape(cent)


def solution(mesh):
    placed = (P("blk", "shard", None), P(AXES, None), P(AXES))
    return jax.shard_map(
        per_device,
        mesh=mesh,
        in_specs=placed,
        out_specs=(P(None, None, AXES), P(AXES, None), P(AXES)),
        check_vma=False,
    )
```

time: 125 us -> 99.1 us (0.79)
  other arithmetic: 29.2 us -> 8.09 us
  waiting for transfers between devices: 28.6 us -> 18.7 us
  Pallas kernels: 13.1 us -> 16.9 us
  local copies, waits for them, and re-layouts: 7.43 us -> 9.79 us
    pallas_call x8 -> x4, other arithmetic: 28.3 us -> 7.93 us  [score_blocks(): pl.pallas_call(functools.partial(score_kernel, scale, len(rows)), out_sha...]
    ppermute x18 -> x21, waiting for transfers between devices: 27.8 us -> 17.9 us  [shift(): return lax.ppermute(value, AXES, along(*axes, by))]
    pallas_call x1 -> x3, Pallas kernels: 13.1 us -> 16.9 us  [the longest x1 11.8 us: weight_all(): pl.pallas_call(functools.partial(weight_kernel, calls, pieces, float(tota...]
    slice x0 -> x2, local copies, waits for them, and re-layouts: none -> 3.37 us  [the longest x1 2.1 us: per_device(): own_a, own_b = (block[:half], block[half:])]
    ppermute x5 -> x8, starting transfers between devices: 20.6 us -> 17.7 us  [to_core(): return lax.ppermute(value, AXES, pairs)]
    ppermute x18 -> x21, starting transfers between devices: 24.6 us -> 26.5 us  [shift(): return lax.ppermute(value, AXES, along(*axes, by))]
  transfers between devices with their start and end apart: 23 -> 29, of which waited for: 13 -> 13; matrix products, arithmetic and copies ran while one was open for 24% -> 12% of each run, Pallas kernels for 0% -> 5%
where the time goes in v2:
time: 99.1 us; the launch traced here: 98.9 us
  starting transfers between devices  44.2 us (45%)
  waiting for transfers between devices  18.7 us (19%)
  Pallas kernels  16.9 us (17%)
  local copies, waits for them, and re-layouts  9.79 us (10%)
  other arithmetic  8.09 us (8%)
  between operations  1.23 us (1%)
    ppermute x21, starting transfers between devices, shift(): return lax.ppermute(value, AXES, along(*axes, by))  26.5 us
    ppermute x21, waiting for transfers between devices, shift(): return lax.ppermute(value, AXES, along(*axes, by))  17.9 us
    ppermute x8, starting transfers between devices, to_core(): return lax.ppermute(value, AXES, pairs)  17.7 us
    pallas_call x1, Pallas kernels, weight_all(): pl.pallas_call(functools.partial(weight_kernel, calls, pieces, float(tota...  11.8 us
    pallas_call x4, other arithmetic, score_blocks(): pl.pallas_call(functools.partial(score_kernel, scale, len(rows)), out_sha...  7.93 us
    pallas_call x2, Pallas kernels, score_blocks(): pl.pallas_call(functools.partial(score_kernel, scale, len(rows)), out_sha...  5.06 us
    dynamic_update_slice x6, local copies, waits for them, and re-layouts, spread(): out = lax.dynamic_update_index_in_dim(out, got, (here - by) % SIDE, 0)  2.19 us
    slice x1, local copies, waits for them, and re-layouts, per_device(): own_a, own_b = (block[:half], block[half:])  2.1 us
  transfers between devices with their start and end apart: 29, of which 13 were waited for; matrix products, arithmetic and copies ran while one was open for 12% of the time, Pallas kernels for 5%

profile of v2, /device:TPU:1, one launch (start us, length us, event | category | flops | bytes accessed | tf_op | source)
XLA Modules:
  0.0 98.9 jit_solution(4305376674560081035)
XLA Ops:
  0.6 3.6 %collective-permute-start.2 = (bf16[32,1024]{1,0:T(8,128)(2,1)}, bf16[32,1024]{1,0:T(8,128)(2,1)S(1)}, u32[]{:S(2)}, u32[]{:S(2)}) collective-permute-start(bf16[32,1024]{1,0:T(8,128)(2,1)} %bitcast.50), channel_id=1, source_target_pairs={{0,65},{1,64},{2,67},{3,66},{4,69},{5,68},{6,71},{7,70},{8,73},{9,... | collective-permute-start | bytes 196616 | tf_op jit(solution)/shard_map/ppermute | solution.py:45
  4.3 1.6 %collective-permute-start = (bf16[32,1024]{1,0:T(8,128)(2,1)}, bf16[32,1024]{1,0:T(8,128)(2,1)S(1)}, u32[]{:S(2)}, u32[]{:S(2)}) collective-permute-start(bf16[32,1024]{1,0:T(8,128)(2,1)} %bitcast.52), channel_id=1, source_target_pairs={{0,1},{1,0},{2,3},{3,2},{4,5},{5,4},{6,7},{7,6},{8,9},{9,8},{10,11... | collective-permute-start | bytes 196616 | tf_op jit(solution)/shard_map/ppermute | solution.py:45
  5.9 0.9 bitcast_dynamic-update-slice_fusion.7
  6.8 2.4 %collective-permute-done = bf16[32,1024]{1,0:T(8,128)(2,1)S(1)} collective-permute-done((bf16[32,1024]{1,0:T(8,128)(2,1)}, bf16[32,1024]{1,0:T(8,128)(2,1)S(1)}, u32[]{:S(2)}, u32[]{:S(2)}) %collective-permute-start) | collective-permute-done | bytes 65568 | tf_op jit(solution)/shard_map/ppermute | solution.py:45
  9.2 0.6 collective-permute-done.1
  9.8 3.7 %collective-permute-start.3 = (bf16[128,1024]{1,0:T(8,128)(2,1)S(1)}, bf16[128,1024]{1,0:T(8,128)(2,1)S(1)}, u32[]{:S(2)}, u32[]{:S(2)}) collective-permute-start(bf16[128,1024]{1,0:T(8,128)(2,1)S(1)} %bitcast.46), channel_id=1, source_target_pairs={{0,4},{1,5},{2,6},{3,7},{4,0},{5,1},{6,2},{7,3},{8,12},{9,13},{10,... | collective-permute-start | bytes 786440 | tf_op jit(solution)/shard_map/ppermute | solution.py:45
  13.5 0.4 collective-permute-start.5
  13.9 1.0 %collective-permute-start.4 = (bf16[128,1024]{1,0:T(8,128)(2,1)S(1)}, bf16[128,1024]{1,0:T(8,128)(2,1)S(1)}, u32[]{:S(2)}, u32[]{:S(2)}) collective-permute-start(bf16[128,1024]{1,0:T(8,128)(2,1)S(1)} %bitcast.48), channel_id=1, source_target_pairs={{0,2},{1,3},{2,4},{3,5},{4,6},{5,7},{6,0},{7,1},{8,10},{9,11},{10,... | collective-permute-start | bytes 786440 | tf_op jit(solution)/shard_map/ppermute | solution.py:45
  15.0 1.1 %broadcast_in_dim.45 = bf16[4,128,1024]{2,1,0:T(8,128)(2,1)} broadcast(bf16[]{:T(256)} %constant.180.clone.1), dimensions={} | broadcast | bytes 1048578 | tf_op jit(solution)/shard_map/broadcast_in_dim | solution.py:55
  16.1 0.7 bitcast_dynamic-update-slice_fusion.3
  16.8 0.8 collective-permute-done.3
  17.6 0.7 bitcast_dynamic-update-slice_fusion.2
  18.3 2.4 %collective-permute-done.4 = bf16[128,1024]{1,0:T(8,128)(2,1)S(1)} collective-permute-done((bf16[128,1024]{1,0:T(8,128)(2,1)S(1)}, bf16[128,1024]{1,0:T(8,128)(2,1)S(1)}, u32[]{:S(2)}, u32[]{:S(2)}) %collective-permute-start.4) | collective-permute-done | bytes 262176 | tf_op jit(solution)/shard_map/ppermute | solution.py:45
  20.7 0.7 bitcast_dynamic-update-slice_fusion.1
  21.4 0.7 bitcast_dynamic-update-slice_fusion
  22.1 2.1 %fusion.22 = (bf16[2,128,1024]{2,1,0:T(8,128)(2,1)S(1)}, bf16[2,128,1024]{2,1,0:T(8,128)(2,1)}) fusion(bf16[4,128,1024]{2,1,0:T(8,128)(2,1)} %bitcast_dynamic-update-slice_fusion), kind=kLoop, calls=%fused_computation.55 | loop fusion | bytes 2097152 | tf_op jit(solution)/shard_map/slice | solution.py:301
  24.2 2.2 %collective-permute-start.9 = (bf16[256,1024]{1,0:T(8,128)(2,1)}, bf16[256,1024]{1,0:T(8,128)(2,1)S(1)}, u32[]{:S(2)}, u32[]{:S(2)}) collective-permute-start(bf16[256,1024]{1,0:T(8,128)(2,1)} %bitcast.20.refs_6_), channel_id=1, source_target_pairs={{0,24},{1,25},{2,26},{3,27},{4,28},{5,29},{6,30},{7,31},{8,0},{9,1... | collective-permute-start | bytes 1572872 | tf_op jit(solution)/shard_map/ppermute | solution.py:45
  26.4 4.5 %collective-permute-start.6 = (bf16[512,1024]{1,0:T(8,128)(2,1)}, bf16[512,1024]{1,0:T(8,128)(2,1)}, u32[]{:S(2)}, u32[]{:S(2)}) collective-permute-start(bf16[512,1024]{1,0:T(8,128)(2,1)} %bitcast.23), channel_id=1, source_target_pairs={{0,32},{1,33},{2,34},{3,35},{4,36},{5,37},{6,38},{7,39},{8,40},{9,... | collective-permute-start | bytes 3145736 | tf_op jit(solution)/shard_map/ppermute | solution.py:41
  31.0 2.6 %collective-permute-start.10 = (bf16[256,1024]{1,0:T(8,128)(2,1)S(1)}, bf16[256,1024]{1,0:T(8,128)(2,1)S(1)}, u32[]{:S(2)}, u32[]{:S(2)}) collective-permute-start(bf16[256,1024]{1,0:T(8,128)(2,1)S(1)} %bitcast.42), channel_id=1, source_target_pairs={{0,24},{1,25},{2,26},{3,27},{4,28},{5,29},{6,30},{7,31},{8,0},{9,1... | collective-permute-start | bytes 1572872 | tf_op jit(solution)/shard_map/ppermute | solution.py:45
  33.6 4.3 %collective-permute-start.13 = (bf16[256,1024]{1,0:T(8,128)(2,1)S(1)}, bf16[256,1024]{1,0:T(8,128)(2,1)S(1)}, u32[]{:S(2)}, u32[]{:S(2)}) collective-permute-start(bf16[256,1024]{1,0:T(8,128)(2,1)S(1)} %collective-permute-done.9.refs_2_.refs_12_), channel_id=1, source_target_pairs={{0,32},{1,33},{2,34},{3,35},{4,36},{5,37},{6,38},{7,39},{8,40},{9,... | collective-permute-start | bytes 1572872 | tf_op jit(solution)/shard_map/ppermute | solution.py:41
  37.9 3.0 %scores.11 = (f32[8,8,128]{2,1,0:T(8,128)S(1)}, f32[1,512,512]{2,1,0:T(8,128)}) fusion(f32[8,8,128]{2,1,0:T(8,128)S(1)} %broadcast_in_dim.44, s32[]{:T(128)S(6)} %select_n.176, bf16[256,1024]{1,0:T(8,128)(2,1)} %bitcast.20.refs_6_, bf16[256,1024]{1,0:T(8,128)(2,1)S(1)} %bitcast.44, bf16[512,1024]{1,0:T(8,128)(2,1)} %refs_4_.3, f32[1,512]{1,0:T(1,128)S(1)} %bitcast.36), kind=kCustom, calls=%fused_computation.40 | custom fusion | flops 2147483648 | bytes 3151876 | tf_op jit(solution)/shard_map/scores/pallas_call | solution.py:111
  41.2 2.2 %collective-permute-start.11 = (bf16[256,1024]{1,0:T(8,128)(2,1)S(1)}, bf16[256,1024]{1,0:T(8,128)(2,1)S(1)}, u32[]{:S(2)}, u32[]{:S(2)}) collective-permute-start(bf16[256,1024]{1,0:T(8,128)(2,1)S(1)} %collective-permute-done.7.refs_0_.refs_10_), channel_id=1, source_target_pairs={{0,32},{1,33},{2,34},{3,35},{4,36},{5,37},{6,38},{7,39},{8,40},{9,... | collective-permute-start | bytes 1572872 | tf_op jit(solution)/shard_map/ppermute | solution.py:41
  43.4 2.8 %collective-permute-done.8.refs_1_.refs_11_ = bf16[256,1024]{1,0:T(8,128)(2,1)S(1)} collective-permute-done((bf16[256,1024]{1,0:T(8,128)(2,1)S(1)}, bf16[256,1024]{1,0:T(8,128)(2,1)S(1)}, u32[]{:S(2)}, u32[]{:S(2)}) %collective-permute-start.8) | collective-permute-done | bytes 524320 | tf_op jit(solution)/shard_map/ppermute | solution.py:45
  46.3 1.4 %collective-permute-start.16 = (bf16[256,1024]{1,0:T(8,128)(2,1)S(1)}, bf16[256,1024]{1,0:T(8,128)(2,1)S(1)}, u32[]{:S(2)}, u32[]{:S(2)}) collective-permute-start(bf16[256,1024]{1,0:T(8,128)(2,1)S(1)} %collective-permute-done.10.refs_3_.refs_13_), channel_id=1, source_target_pairs={{0,24},{1,25},{2,26},{3,27},{4,28},{5,29},{6,30},{7,31},{8,0},{9,1... | collective-permute-start | bytes 1572872 | tf_op jit(solution)/shard_map/ppermute | solution.py:45
  47.6 0.5 collective-permute-start.12
  48.2 2.6 %scores.6 = (f32[2,512,512]{2,1,0:T(8,128)S(1)}, f32[2,8,128]{2,1,0:T(8,128)S(1)}) custom-call(bf16[256,1024]{1,0:T(8,128)(2,1)S(1)} %collective-permute-done.7.refs_0_.refs_10_, bf16[256,1024]{1,0:T(8,128)(2,1)S(1)} %collective-permute-done.8.refs_1_.refs_11_, bf16[256,1024]{1,0:T(8,128)(2,1)S(1)} %collective-permute-done.9.refs_2_.refs_12_, ...), custom_call_target="tpu_custom_call" | custom-call | flops 4294967296 | bytes 5242880 | tf_op jit(solution)/shard_map/scores/pallas_call | solution.py:111
  50.8 1.3 %copy-done = f32[2,512,512]{2,1,0:T(8,128)} copy-done((f32[2,512,512]{2,1,0:T(8,128)}, f32[2,512,512]{2,1,0:T(8,128)S(1)}, u32[]{:S(2)}) %copy-start) | copy-done | bytes 2097176
  52.1 1.3 %fusion.21 = (bf16[256,1024]{1,0:T(8,128)(2,1)S(1)}, bf16[256,1024]{1,0:T(8,128)(2,1)S(1)}) fusion(bf16[512,1024]{1,0:T(8,128)(2,1)} %collective-permute-done.6), kind=kLoop, calls=%fused_computation.54 | loop fusion | bytes 2097152 | tf_op jit(solution)/shard_map/slice | solution.py:308
  53.4 1.6 %scores.10 = (f32[8,8,128]{2,1,0:T(8,128)S(1)}, f32[1,512,512]{2,1,0:T(8,128)}) fusion(f32[8,8,128]{2,1,0:T(8,128)S(1)} %get-tuple-element.43, s32[]{:T(128)S(6)} %select_n.177, bf16[256,1024]{1,0:T(8,128)(2,1)S(1)} %get-tuple-element.56.refs_8_, bf16[256,1024]{1,0:T(8,128)(2,1)S(1)} %get-tuple-element.55.refs_9_, bf16[512,1024]{1,0:T(8,128)(2,1)S(1)} %copy-done.10, ...), kind=kCustom, calls=%fused_computation.39 | custom fusion | flops 2147483648 | bytes 3151876 | tf_op jit(solution)/shard_map/scores/pallas_call | solution.py:111
  55.2 1.1 %collective-permute-start.18 = (bf16[256,1024]{1,0:T(8,128)(2,1)S(1)}, bf16[256,1024]{1,0:T(8,128)(2,1)S(1)}, u32[]{:S(2)}, u32[]{:S(2)}) collective-permute-start(bf16[256,1024]{1,0:T(8,128)(2,1)S(1)} %collective-permute-done.16.refs_19_), channel_id=1, source_target_pairs={{0,32},{1,33},{2,34},{3,35},{4,36},{5,37},{6,38},{7,39},{8,40},{9,... | collective-permute-start | bytes 1572872 | tf_op jit(solution)/shard_map/ppermute | solution.py:41
  56.4 2.5 %scores.7 = (f32[2,512,512]{2,1,0:T(8,128)S(1)}, f32[2,8,128]{2,1,0:T(8,128)S(1)}) custom-call(bf16[256,1024]{1,0:T(8,128)(2,1)S(1)} %collective-permute-done.11.refs_0_.refs_14_, bf16[256,1024]{1,0:T(8,128)(2,1)S(1)} %collective-permute-done.12.refs_1_.refs_15_, bf16[256,1024]{1,0:T(8,128)(2,1)S(1)} %collective-permute-done.13.refs_2_.refs_16_, ...), custom_call_target="tpu_custom_call" | custom-call | flops 4294967296 | bytes 5242880 | tf_op jit(solution)/shard_map/scores/pallas_call | solution.py:111
  59.0 1.6 %scores.9 = (f32[8,8,128]{2,1,0:T(8,128)S(1)}, f32[1,512,512]{2,1,0:T(8,128)}) fusion(f32[8,8,128]{2,1,0:T(8,128)S(1)} %slice_dynamic-update-slice_fusion, s32[]{:T(128)S(6)} %select_n.182, bf16[256,1024]{1,0:T(8,128)(2,1)S(1)} %collective-permute-done.15.refs_18_, bf16[256,1024]{1,0:T(8,128)(2,1)S(1)} %collective-permute-done.16.refs_19_, ...), kind=kCustom, calls=%fused_computation.38 | custom fusion | flops 2147483648 | bytes 3151876 | tf_op jit(solution)/shard_map/scores/pallas_call | solution.py:111
  60.6 1.7 %scores.8 = (f32[8,8,128]{2,1,0:T(8,128)S(1)}, f32[1,512,512]{2,1,0:T(8,128)}) fusion(f32[8,8,128]{2,1,0:T(8,128)S(1)} %get-tuple-element.39, s32[]{:T(128)S(6)} %select_n.183, bf16[256,1024]{1,0:T(8,128)(2,1)S(1)} %collective-permute-done.17.refs_20_, bf16[256,1024]{1,0:T(8,128)(2,1)S(1)} %collective-permute-done.18.refs_21_, ...), kind=kCustom, calls=%fused_computation.37 | custom fusion | flops 2147483648 | bytes 3151876 | tf_op jit(solution)/shard_map/scores/pallas_call | solution.py:111
  62.3 0.9 collective-permute-start.21
  63.3 0.6 collective-permute-start.20
  63.9 1.8 %collective-permute-start.19 = (f32[8,8,128]{2,1,0:T(8,128)S(1)}, f32[8,8,128]{2,1,0:T(8,128)S(1)}, u32[]{:S(2)}, u32[]{:S(2)}) collective-permute-start(f32[8,8,128]{2,1,0:T(8,128)S(1)} %get-tuple-element.35), channel_id=1, source_target_pairs={{0,1},{1,0},{2,3},{3,2},{4,5},{5,4},{6,7},{7,6},{8,9},{9,8},{10,11... | collective-permute-start | bytes 98312 | tf_op jit(solution)/shard_map/ppermute | solution.py:45
  65.6 1.6 %collective-permute-done.20 = f32[8,8,128]{2,1,0:T(8,128)S(1)} collective-permute-done((f32[8,8,128]{2,1,0:T(8,128)S(1)}, f32[8,8,128]{2,1,0:T(8,128)S(1)}, u32[]{:S(2)}, u32[]{:S(2)}) %collective-permute-start.20) | collective-permute-done | bytes 32800 | tf_op jit(solution)/shard_map/ppermute | solution.py:45
  67.2 0.9 collective-permute-done.19
  68.2 1.2 %collective-permute-start.24 = (f32[8,8,128]{2,1,0:T(8,128)S(1)}, f32[8,8,128]{2,1,0:T(8,128)S(1)}, u32[]{:S(2)}, u32[]{:S(2)}) collective-permute-start(f32[8,8,128]{2,1,0:T(8,128)S(1)} %pad_maximum_fusion), channel_id=1, source_target_pairs={{0,6},{1,7},{2,0},{3,1},{4,2},{5,3},{6,4},{7,5},{8,14},{9,15},{10,... | collective-permute-start | bytes 98312 | tf_op jit(solution)/shard_map/ppermute | solution.py:45
  69.7 1.0 collective-permute-start.22
  71.0 2.4 %collective-permute-done.23 = f32[8,8,128]{2,1,0:T(8,128)S(1)} collective-permute-done((f32[8,8,128]{2,1,0:T(8,128)S(1)}, f32[8,8,128]{2,1,0:T(8,128)S(1)}, u32[]{:S(2)}, u32[]{:S(2)}) %collective-permute-start.23) | collective-permute-done | bytes 32800 | tf_op jit(solution)/shard_map/ppermute | solution.py:45
  73.4 0.6 collective-permute-done.22
  74.1 2.6 %collective-permute-start.27 = (f32[8,8,128]{2,1,0:T(8,128)S(1)}, f32[8,8,128]{2,1,0:T(8,128)S(1)}, u32[]{:S(2)}, u32[]{:S(2)}) collective-permute-start(f32[8,8,128]{2,1,0:T(8,128)S(1)} %pad_maximum_fusion.1), channel_id=1, source_target_pairs={{0,24},{1,25},{2,26},{3,27},{4,28},{5,29},{6,30},{7,31},{8,0},{9,1... | collective-permute-start | bytes 98312 | tf_op jit(solution)/shard_map/ppermute | solution.py:45
  76.7 1.3 %collective-permute-start.25 = (f32[8,8,128]{2,1,0:T(8,128)S(1)}, f32[8,8,128]{2,1,0:T(8,128)S(1)}, u32[]{:S(2)}, u32[]{:S(2)}) collective-permute-start(f32[8,8,128]{2,1,0:T(8,128)S(1)} %pad_maximum_fusion.1), channel_id=1, source_target_pairs={{0,16},{1,17},{2,18},{3,19},{4,20},{5,21},{6,22},{7,23},{8,24},{9,... | collective-permute-start | bytes 98312 | tf_op jit(solution)/shard_map/ppermute | solution.py:45
  78.0 2.7 %collective-permute-done.26 = f32[8,8,128]{2,1,0:T(8,128)S(1)} collective-permute-done((f32[8,8,128]{2,1,0:T(8,128)S(1)}, f32[8,8,128]{2,1,0:T(8,128)S(1)}, u32[]{:S(2)}, u32[]{:S(2)}) %collective-permute-start.26) | collective-permute-done | bytes 32800 | tf_op jit(solution)/shard_map/ppermute | solution.py:45
  81.1 4.9 %collective-permute-start.28 = (f32[8,8,128]{2,1,0:T(8,128)S(1)}, f32[8,8,128]{2,1,0:T(8,128)S(1)}, u32[]{:S(2)}, u32[]{:S(2)}) collective-permute-start(f32[8,8,128]{2,1,0:T(8,128)S(1)} %pad_maximum_fusion.2.stat_a), channel_id=1, source_target_pairs={{0,32},{1,33},{2,34},{3,35},{4,36},{5,37},{6,38},{7,39},{8,40},{9,... | collective-permute-start | bytes 98312 | tf_op jit(solution)/shard_map/ppermute | solution.py:41
  86.1 0.8 collective-permute-done.28.stat_b
  86.9 11.8 %weights.1 = (f32[2,2,2,4,4,2,16,512]{7,6,5,4,3,2,1,0:T(8,128)}, f32[512,1024]{1,0:T(8,128)}, f32[1,512]{1,0:T(1,128)}) custom-call(s32[16]{0:T(128)S(1)} %stack.49.where_ref, f32[8,8,128]{2,1,0:T(8,128)S(1)} %pad_maximum_fusion.2.stat_a, f32[8,8,128]{2,1,0:T(8,128)S(1)} %collective-permute-done.28.stat_b, f32[1,512,512]{2,1,0:T(8,128)} %get-tuple-element.44.refs_0_, ...), custom_call_target="tpu_custom_call" | custom-call | tf_op jit(solution)/shard_map/weights/pallas_call | solution.py:246
  (80 shorter events, 1.9 us)
Async XLA Ops:
  0.6 9.2 %collective-permute-start.2 = (bf16[32,1024]{1,0:T(8,128)(2,1)}, bf16[32,1024]{1,0:T(8,128)(2,1)S(1)}, u32[]{:S(2)}, u32[]{:S(2)}) collective-permute-start(bf16[32,1024]{1,0:T(8,128)(2,1)} %bitcast.50), channel_id=1, source_target_pairs={{0,65},{1,64},{2,67},{3,66},{4,69},{5,68},{6,71},{7,70},{8,73},{9,... | collective-permute-start | bytes 196616 | tf_op jit(solution)/shard_map/ppermute | solution.py:45
  4.3 5.5 %collective-permute-start.1 = (bf16[32,1024]{1,0:T(8,128)(2,1)}, bf16[32,1024]{1,0:T(8,128)(2,1)S(1)}, u32[]{:S(2)}, u32[]{:S(2)}) collective-permute-start(bf16[32,1024]{1,0:T(8,128)(2,1)} %bitcast.51), channel_id=1, source_target_pairs={{0,64},{1,65},{2,66},{3,67},{4,68},{5,69},{6,70},{7,71},{8,72},{9,... | collective-permute-start | bytes 196616 | tf_op jit(solution)/shard_map/ppermute | solution.py:45
  4.3 4.9 %collective-permute-start = (bf16[32,1024]{1,0:T(8,128)(2,1)}, bf16[32,1024]{1,0:T(8,128)(2,1)S(1)}, u32[]{:S(2)}, u32[]{:S(2)}) collective-permute-start(bf16[32,1024]{1,0:T(8,128)(2,1)} %bitcast.52), channel_id=1, source_target_pairs={{0,1},{1,0},{2,3},{3,2},{4,5},{5,4},{6,7},{7,6},{8,9},{9,8},{10,11... | collective-permute-start | bytes 196616 | tf_op jit(solution)/shard_map/ppermute | solution.py:45
  9.8 7.7 %collective-permute-start.3 = (bf16[128,1024]{1,0:T(8,128)(2,1)S(1)}, bf16[128,1024]{1,0:T(8,128)(2,1)S(1)}, u32[]{:S(2)}, u32[]{:S(2)}) collective-permute-start(bf16[128,1024]{1,0:T(8,128)(2,1)S(1)} %bitcast.46), channel_id=1, source_target_pairs={{0,4},{1,5},{2,6},{3,7},{4,0},{5,1},{6,2},{7,3},{8,12},{9,13},{10,... | collective-permute-start | bytes 786440 | tf_op jit(solution)/shard_map/ppermute | solution.py:45
  13.5 7.9 %collective-permute-start.5 = (bf16[128,1024]{1,0:T(8,128)(2,1)S(1)}, bf16[128,1024]{1,0:T(8,128)(2,1)S(1)}, u32[]{:S(2)}, u32[]{:S(2)}) collective-permute-start(bf16[128,1024]{1,0:T(8,128)(2,1)S(1)} %bitcast.47), channel_id=1, source_target_pairs={{0,6},{1,7},{2,0},{3,1},{4,2},{5,3},{6,4},{7,5},{8,14},{9,15},{10,... | collective-permute-start | bytes 786440 | tf_op jit(solution)/shard_map/ppermute | solution.py:45
  13.9 6.7 %collective-permute-start.4 = (bf16[128,1024]{1,0:T(8,128)(2,1)S(1)}, bf16[128,1024]{1,0:T(8,128)(2,1)S(1)}, u32[]{:S(2)}, u32[]{:S(2)}) collective-permute-start(bf16[128,1024]{1,0:T(8,128)(2,1)S(1)} %bitcast.48), channel_id=1, source_target_pairs={{0,2},{1,3},{2,4},{3,5},{4,6},{5,7},{6,0},{7,1},{8,10},{9,11},{10,... | collective-permute-start | bytes 786440 | tf_op jit(solution)/shard_map/ppermute | solution.py:45
  16.8 21.1 %copy-start.18 = (s32[512]{0:T(512)S(1)}, s32[512]{0:T(512)}, u32[]{:S(2)}) copy-start(s32[512]{0:T(512)} %param.5) | copy-start | bytes 6148
  24.2 16.8 %copy-start.11 = (bf16[2,128,1024]{2,1,0:T(8,128)(2,1)}, bf16[2,128,1024]{2,1,0:T(8,128)(2,1)S(1)}, u32[]{:S(2)}) copy-start(bf16[2,128,1024]{2,1,0:T(8,128)(2,1)S(1)} %get-tuple-element.57) | copy-start | bytes 1572868
  24.2 9.3 %collective-permute-start.9 = (bf16[256,1024]{1,0:T(8,128)(2,1)}, bf16[256,1024]{1,0:T(8,128)(2,1)S(1)}, u32[]{:S(2)}, u32[]{:S(2)}) collective-permute-start(bf16[256,1024]{1,0:T(8,128)(2,1)} %bitcast.20.refs_6_), channel_id=1, source_target_pairs={{0,24},{1,25},{2,26},{3,27},{4,28},{5,29},{6,30},{7,31},{8,0},{9,1... | collective-permute-start | bytes 1572872 | tf_op jit(solution)/shard_map/ppermute | solution.py:45
  26.4 21.2 %collective-permute-start.6 = (bf16[512,1024]{1,0:T(8,128)(2,1)}, bf16[512,1024]{1,0:T(8,128)(2,1)}, u32[]{:S(2)}, u32[]{:S(2)}) collective-permute-start(bf16[512,1024]{1,0:T(8,128)(2,1)} %bitcast.23), channel_id=1, source_target_pairs={{0,32},{1,33},{2,34},{3,35},{4,36},{5,37},{6,38},{7,39},{8,40},{9,... | collective-permute-start | bytes 3145736 | tf_op jit(solution)/shard_map/ppermute | solution.py:41
  30.9 10.1 %collective-permute-start.7 = (bf16[256,1024]{1,0:T(8,128)(2,1)}, bf16[256,1024]{1,0:T(8,128)(2,1)S(1)}, u32[]{:S(2)}, u32[]{:S(2)}) collective-permute-start(bf16[256,1024]{1,0:T(8,128)(2,1)} %bitcast.20.refs_6_), channel_id=1, source_target_pairs={{0,8},{1,9},{2,10},{3,11},{4,12},{5,13},{6,14},{7,15},{8,16},{9,17... | collective-permute-start | bytes 1572872 | tf_op jit(solution)/shard_map/ppermute | solution.py:45
  31.0 10.2 %collective-permute-start.10 = (bf16[256,1024]{1,0:T(8,128)(2,1)S(1)}, bf16[256,1024]{1,0:T(8,128)(2,1)S(1)}, u32[]{:S(2)}, u32[]{:S(2)}) collective-permute-start(bf16[256,1024]{1,0:T(8,128)(2,1)S(1)} %bitcast.42), channel_id=1, source_target_pairs={{0,24},{1,25},{2,26},{3,27},{4,28},{5,29},{6,30},{7,31},{8,0},{9,1... | collective-permute-start | bytes 1572872 | tf_op jit(solution)/shard_map/ppermute | solution.py:45
  33.6 12.7 %collective-permute-start.8 = (bf16[256,1024]{1,0:T(8,128)(2,1)S(1)}, bf16[256,1024]{1,0:T(8,128)(2,1)S(1)}, u32[]{:S(2)}, u32[]{:S(2)}) collective-permute-start(bf16[256,1024]{1,0:T(8,128)(2,1)S(1)} %bitcast.43), channel_id=1, source_target_pairs={{0,8},{1,9},{2,10},{3,11},{4,12},{5,13},{6,14},{7,15},{8,16},{9,17... | collective-permute-start | bytes 1572872 | tf_op jit(solution)/shard_map/ppermute | solution.py:45
  33.6 14.6 %copy-start.2 = (bf16[256,1024]{1,0:T(8,128)(2,1)}, bf16[256,1024]{1,0:T(8,128)(2,1)S(1)}, u32[]{:S(2)}) copy-start(bf16[256,1024]{1,0:T(8,128)(2,1)S(1)} %collective-permute-done.9.refs_2_.refs_12_) | copy-start | bytes 1572868
  33.6 14.1 %collective-permute-start.13 = (bf16[256,1024]{1,0:T(8,128)(2,1)S(1)}, bf16[256,1024]{1,0:T(8,128)(2,1)S(1)}, u32[]{:S(2)}, u32[]{:S(2)}) collective-permute-start(bf16[256,1024]{1,0:T(8,128)(2,1)S(1)} %collective-permute-done.9.refs_2_.refs_12_), channel_id=1, source_target_pairs={{0,32},{1,33},{2,34},{3,35},{4,36},{5,37},{6,38},{7,39},{8,40},{9,... | collective-permute-start | bytes 1572872 | tf_op jit(solution)/shard_map/ppermute | solution.py:41
  37.9 10.2 %copy-start.10 = (bf16[512,1024]{1,0:T(8,128)(2,1)S(1)}, bf16[512,1024]{1,0:T(8,128)(2,1)}, u32[]{:S(2)}) copy-start(bf16[512,1024]{1,0:T(8,128)(2,1)} %refs_4_.3) | copy-start | bytes 3145732
  41.0 9.7 %copy-start.3 = (bf16[256,1024]{1,0:T(8,128)(2,1)}, bf16[256,1024]{1,0:T(8,128)(2,1)S(1)}, u32[]{:S(2)}) copy-start(bf16[256,1024]{1,0:T(8,128)(2,1)S(1)} %collective-permute-done.7.refs_0_.refs_10_) | copy-start | bytes 1572868
  41.0 14.0 %collective-permute-start.15 = (bf16[256,1024]{1,0:T(8,128)(2,1)S(1)}, bf16[256,1024]{1,0:T(8,128)(2,1)S(1)}, u32[]{:S(2)}, u32[]{:S(2)}) collective-permute-start(bf16[256,1024]{1,0:T(8,128)(2,1)S(1)} %collective-permute-done.7.refs_0_.refs_10_), channel_id=1, source_target_pairs={{0,8},{1,9},{2,10},{3,11},{4,12},{5,13},{6,14},{7,15},{8,16},{9,17... | collective-permute-start | bytes 1572872 | tf_op jit(solution)/shard_map/ppermute | solution.py:45
  41.2 9.5 %copy-start.4 = (bf16[256,1024]{1,0:T(8,128)(2,1)}, bf16[256,1024]{1,0:T(8,128)(2,1)S(1)}, u32[]{:S(2)}) copy-start(bf16[256,1024]{1,0:T(8,128)(2,1)S(1)} %collective-permute-done.10.refs_3_.refs_13_) | copy-start | bytes 1572868
  41.2 15.1 %collective-permute-start.11 = (bf16[256,1024]{1,0:T(8,128)(2,1)S(1)}, bf16[256,1024]{1,0:T(8,128)(2,1)S(1)}, u32[]{:S(2)}, u32[]{:S(2)}) collective-permute-start(bf16[256,1024]{1,0:T(8,128)(2,1)S(1)} %collective-permute-done.7.refs_0_.refs_10_), channel_id=1, source_target_pairs={{0,32},{1,33},{2,34},{3,35},{4,36},{5,37},{6,38},{7,39},{8,40},{9,... | collective-permute-start | bytes 1572872 | tf_op jit(solution)/shard_map/ppermute | solution.py:41
  46.3 4.5 %copy-start.5 = (bf16[256,1024]{1,0:T(8,128)(2,1)}, bf16[256,1024]{1,0:T(8,128)(2,1)S(1)}, u32[]{:S(2)}) copy-start(bf16[256,1024]{1,0:T(8,128)(2,1)S(1)} %collective-permute-done.8.refs_1_.refs_11_) | copy-start | bytes 1572868
  46.3 9.0 %collective-permute-start.16 = (bf16[256,1024]{1,0:T(8,128)(2,1)S(1)}, bf16[256,1024]{1,0:T(8,128)(2,1)S(1)}, u32[]{:S(2)}, u32[]{:S(2)}) collective-permute-start(bf16[256,1024]{1,0:T(8,128)(2,1)S(1)} %collective-permute-done.10.refs_3_.refs_13_), channel_id=1, source_target_pairs={{0,24},{1,25},{2,26},{3,27},{4,28},{5,29},{6,30},{7,31},{8,0},{9,1... | collective-permute-start | bytes 1572872 | tf_op jit(solution)/shard_map/ppermute | solution.py:45
  47.6 8.7 %copy-start.6 = (bf16[256,1024]{1,0:T(8,128)(2,1)}, bf16[256,1024]{1,0:T(8,128)(2,1)S(1)}, u32[]{:S(2)}) copy-start(bf16[256,1024]{1,0:T(8,128)(2,1)S(1)} %collective-permute-done.13.refs_2_.refs_16_) | copy-start | bytes 1572868
  47.6 8.7 %collective-permute-start.14 = (bf16[256,1024]{1,0:T(8,128)(2,1)S(1)}, bf16[256,1024]{1,0:T(8,128)(2,1)S(1)}, u32[]{:S(2)}, u32[]{:S(2)}) collective-permute-start(bf16[256,1024]{1,0:T(8,128)(2,1)S(1)} %collective-permute-done.10.refs_3_.refs_13_), channel_id=1, source_target_pairs={{0,32},{1,33},{2,34},{3,35},{4,36},{5,37},{6,38},{7,39},{8,40},{9,... | collective-permute-start | bytes 1572872 | tf_op jit(solution)/shard_map/ppermute | solution.py:41
  47.6 8.7 %collective-permute-start.12 = (bf16[256,1024]{1,0:T(8,128)(2,1)S(1)}, bf16[256,1024]{1,0:T(8,128)(2,1)S(1)}, u32[]{:S(2)}, u32[]{:S(2)}) collective-permute-start(bf16[256,1024]{1,0:T(8,128)(2,1)S(1)} %collective-permute-done.8.refs_1_.refs_11_), channel_id=1, source_target_pairs={{0,32},{1,33},{2,34},{3,35},{4,36},{5,37},{6,38},{7,39},{8,40},{9,... | collective-permute-start | bytes 1572872 | tf_op jit(solution)/shard_map/ppermute | solution.py:41
  50.7 1.4 %copy-start = (f32[2,512,512]{2,1,0:T(8,128)}, f32[2,512,512]{2,1,0:T(8,128)S(1)}, u32[]{:S(2)}) copy-start(f32[2,512,512]{2,1,0:T(8,128)S(1)} %get-tuple-element.26.refs_2_) | copy-start | bytes 6291460
  53.4 1.6 %copy-start.12 = (bf16[256,1024]{1,0:T(8,128)(2,1)}, bf16[256,1024]{1,0:T(8,128)(2,1)S(1)}, u32[]{:S(2)}) copy-start(bf16[256,1024]{1,0:T(8,128)(2,1)S(1)} %get-tuple-element.55.refs_9_) | copy-start | bytes 1572868
  53.4 1.6 %copy-start.13 = (bf16[256,1024]{1,0:T(8,128)(2,1)}, bf16[256,1024]{1,0:T(8,128)(2,1)S(1)}, u32[]{:S(2)}) copy-start(bf16[256,1024]{1,0:T(8,128)(2,1)S(1)} %get-tuple-element.56.refs_8_) | copy-start | bytes 1572868
  55.1 3.9 %copy-start.14 = (bf16[256,1024]{1,0:T(8,128)(2,1)}, bf16[256,1024]{1,0:T(8,128)(2,1)S(1)}, u32[]{:S(2)}) copy-start(bf16[256,1024]{1,0:T(8,128)(2,1)S(1)} %collective-permute-done.15.refs_18_) | copy-start | bytes 1572868
  55.1 5.5 %collective-permute-start.17 = (bf16[256,1024]{1,0:T(8,128)(2,1)S(1)}, bf16[256,1024]{1,0:T(8,128)(2,1)S(1)}, u32[]{:S(2)}, u32[]{:S(2)}) collective-permute-start(bf16[256,1024]{1,0:T(8,128)(2,1)S(1)} %collective-permute-done.15.refs_18_), channel_id=1, source_target_pairs={{0,32},{1,33},{2,34},{3,35},{4,36},{5,37},{6,38},{7,39},{8,40},{9,... | collective-permute-start | bytes 1572872 | tf_op jit(solution)/shard_map/ppermute | solution.py:41
  55.2 3.7 %copy-start.15 = (bf16[256,1024]{1,0:T(8,128)(2,1)}, bf16[256,1024]{1,0:T(8,128)(2,1)S(1)}, u32[]{:S(2)}) copy-start(bf16[256,1024]{1,0:T(8,128)(2,1)S(1)} %collective-permute-done.16.refs_19_) | copy-start | bytes 1572868
  55.2 5.4 %collective-permute-start.18 = (bf16[256,1024]{1,0:T(8,128)(2,1)S(1)}, bf16[256,1024]{1,0:T(8,128)(2,1)S(1)}, u32[]{:S(2)}, u32[]{:S(2)}) collective-permute-start(bf16[256,1024]{1,0:T(8,128)(2,1)S(1)} %collective-permute-done.16.refs_19_), channel_id=1, source_target_pairs={{0,32},{1,33},{2,34},{3,35},{4,36},{5,37},{6,38},{7,39},{8,40},{9,... | collective-permute-start | bytes 1572872 | tf_op jit(solution)/shard_map/ppermute | solution.py:41
  56.3 2.6 %copy-start.7 = (bf16[256,1024]{1,0:T(8,128)(2,1)}, bf16[256,1024]{1,0:T(8,128)(2,1)S(1)}, u32[]{:S(2)}) copy-start(bf16[256,1024]{1,0:T(8,128)(2,1)S(1)} %collective-permute-done.11.refs_0_.refs_14_) | copy-start | bytes 1572868
  56.3 2.6 %copy-start.8 = (bf16[256,1024]{1,0:T(8,128)(2,1)}, bf16[256,1024]{1,0:T(8,128)(2,1)S(1)}, u32[]{:S(2)}) copy-start(bf16[256,1024]{1,0:T(8,128)(2,1)S(1)} %collective-permute-done.14.refs_3_.refs_17_) | copy-start | bytes 1572868
  56.3 2.5 %copy-start.9 = (bf16[256,1024]{1,0:T(8,128)(2,1)}, bf16[256,1024]{1,0:T(8,128)(2,1)S(1)}, u32[]{:S(2)}) copy-start(bf16[256,1024]{1,0:T(8,128)(2,1)S(1)} %collective-permute-done.12.refs_1_.refs_15_) | copy-start | bytes 1572868
  58.9 1.7 %copy-start.1 = (f32[2,512,512]{2,1,0:T(8,128)}, f32[2,512,512]{2,1,0:T(8,128)S(1)}, u32[]{:S(2)}) copy-start(f32[2,512,512]{2,1,0:T(8,128)S(1)} %get-tuple-element.27.refs_3_) | copy-start | bytes 6291460
  60.6 1.7 %copy-start.16 = (bf16[256,1024]{1,0:T(8,128)(2,1)}, bf16[256,1024]{1,0:T(8,128)(2,1)S(1)}, u32[]{:S(2)}) copy-start(bf16[256,1024]{1,0:T(8,128)(2,1)S(1)} %collective-permute-done.17.refs_20_) | copy-start | bytes 1572868
  60.6 1.7 %copy-start.17 = (bf16[256,1024]{1,0:T(8,128)(2,1)}, bf16[256,1024]{1,0:T(8,128)(2,1)S(1)}, u32[]{:S(2)}) copy-start(bf16[256,1024]{1,0:T(8,128)(2,1)S(1)} %collective-permute-done.18.refs_21_) | copy-start | bytes 1572868
  62.3 3.3 %collective-permute-start.21 = (f32[8,8,128]{2,1,0:T(8,128)S(1)}, f32[8,8,128]{2,1,0:T(8,128)S(1)}, u32[]{:S(2)}, u32[]{:S(2)}) collective-permute-start(f32[8,8,128]{2,1,0:T(8,128)S(1)} %get-tuple-element.35), channel_id=1, source_target_pairs={{0,65},{1,64},{2,67},{3,66},{4,69},{5,68},{6,71},{7,70},{8,73},{9,... | collective-permute-start | bytes 98312 | tf_op jit(solution)/shard_map/ppermute | solution.py:45
  63.3 4.0 %collective-permute-start.20 = (f32[8,8,128]{2,1,0:T(8,128)S(1)}, f32[8,8,128]{2,1,0:T(8,128)S(1)}, u32[]{:S(2)}, u32[]{:S(2)}) collective-permute-start(f32[8,8,128]{2,1,0:T(8,128)S(1)} %get-tuple-element.35), channel_id=1, source_target_pairs={{0,64},{1,65},{2,66},{3,67},{4,68},{5,69},{6,70},{7,71},{8,72},{9,... | collective-permute-start | bytes 98312 | tf_op jit(solution)/shard_map/ppermute | solution.py:45
  63.9 4.3 %collective-permute-start.19 = (f32[8,8,128]{2,1,0:T(8,128)S(1)}, f32[8,8,128]{2,1,0:T(8,128)S(1)}, u32[]{:S(2)}, u32[]{:S(2)}) collective-permute-start(f32[8,8,128]{2,1,0:T(8,128)S(1)} %get-tuple-element.35), channel_id=1, source_target_pairs={{0,1},{1,0},{2,3},{3,2},{4,5},{5,4},{6,7},{7,6},{8,9},{9,8},{10,11... | collective-permute-start | bytes 98312 | tf_op jit(solution)/shard_map/ppermute | solution.py:45
  68.2 2.8 %collective-permute-start.24 = (f32[8,8,128]{2,1,0:T(8,128)S(1)}, f32[8,8,128]{2,1,0:T(8,128)S(1)}, u32[]{:S(2)}, u32[]{:S(2)}) collective-permute-start(f32[8,8,128]{2,1,0:T(8,128)S(1)} %pad_maximum_fusion), channel_id=1, source_target_pairs={{0,6},{1,7},{2,0},{3,1},{4,2},{5,3},{6,4},{7,5},{8,14},{9,15},{10,... | collective-permute-start | bytes 98312 | tf_op jit(solution)/shard_map/ppermute | solution.py:45
  69.4 4.0 %collective-permute-start.23 = (f32[8,8,128]{2,1,0:T(8,128)S(1)}, f32[8,8,128]{2,1,0:T(8,128)S(1)}, u32[]{:S(2)}, u32[]{:S(2)}) collective-permute-start(f32[8,8,128]{2,1,0:T(8,128)S(1)} %pad_maximum_fusion), channel_id=1, source_target_pairs={{0,2},{1,3},{2,4},{3,5},{4,6},{5,7},{6,0},{7,1},{8,10},{9,11},{10,... | collective-permute-start | bytes 98312 | tf_op jit(solution)/shard_map/ppermute | solution.py:45
  69.7 4.3 %collective-permute-start.22 = (f32[8,8,128]{2,1,0:T(8,128)S(1)}, f32[8,8,128]{2,1,0:T(8,128)S(1)}, u32[]{:S(2)}, u32[]{:S(2)}) collective-permute-start(f32[8,8,128]{2,1,0:T(8,128)S(1)} %pad_maximum_fusion), channel_id=1, source_target_pairs={{0,4},{1,5},{2,6},{3,7},{4,0},{5,1},{6,2},{7,3},{8,12},{9,13},{10,... | collective-permute-start | bytes 98312 | tf_op jit(solution)/shard_map/ppermute | solution.py:45
  74.1 3.9 %collective-permute-start.27 = (f32[8,8,128]{2,1,0:T(8,128)S(1)}, f32[8,8,128]{2,1,0:T(8,128)S(1)}, u32[]{:S(2)}, u32[]{:S(2)}) collective-permute-start(f32[8,8,128]{2,1,0:T(8,128)S(1)} %pad_maximum_fusion.1), channel_id=1, source_target_pairs={{0,24},{1,25},{2,26},{3,27},{4,28},{5,29},{6,30},{7,31},{8,0},{9,1... | collective-permute-start | bytes 98312 | tf_op jit(solution)/shard_map/ppermute | solution.py:45
  76.7 4.0 %collective-permute-start.26 = (f32[8,8,128]{2,1,0:T(8,128)S(1)}, f32[8,8,128]{2,1,0:T(8,128)S(1)}, u32[]{:S(2)}, u32[]{:S(2)}) collective-permute-start(f32[8,8,128]{2,1,0:T(8,128)S(1)} %pad_maximum_fusion.1), channel_id=1, source_target_pairs={{0,8},{1,9},{2,10},{3,11},{4,12},{5,13},{6,14},{7,15},{8,16},{9,17... | collective-permute-start | bytes 98312 | tf_op jit(solution)/shard_map/ppermute | solution.py:45
  76.7 4.3 %collective-permute-start.25 = (f32[8,8,128]{2,1,0:T(8,128)S(1)}, f32[8,8,128]{2,1,0:T(8,128)S(1)}, u32[]{:S(2)}, u32[]{:S(2)}) collective-permute-start(f32[8,8,128]{2,1,0:T(8,128)S(1)} %pad_maximum_fusion.1), channel_id=1, source_target_pairs={{0,16},{1,17},{2,18},{3,19},{4,20},{5,21},{6,22},{7,23},{8,24},{9,... | collective-permute-start | bytes 98312 | tf_op jit(solution)/shard_map/ppermute | solution.py:45
  81.1 5.8 %collective-permute-start.28 = (f32[8,8,128]{2,1,0:T(8,128)S(1)}, f32[8,8,128]{2,1,0:T(8,128)S(1)}, u32[]{:S(2)}, u32[]{:S(2)}) collective-permute-start(f32[8,8,128]{2,1,0:T(8,128)S(1)} %pad_maximum_fusion.2.stat_a), channel_id=1, source_target_pairs={{0,32},{1,33},{2,34},{3,35},{4,36},{5,37},{6,38},{7,39},{8,40},{9,... | collective-permute-start | bytes 98312 | tf_op jit(solution)/shard_map/ppermute | solution.py:41

commit v3 on v0

v3 whole, which is shorter than its diff:
```python
import functools
import math

import jax
import jax.numpy as jnp
from jax import lax
from jax.experimental import pallas as pl
from jax.experimental.pallas import tpu as pltpu
from jax.sharding import PartitionSpec as P

AXES = ("blk", "shard")
SIDE = 4
LANES = 128
CHUNK = 256


def place_of(device):
    blk, shard = divmod(device, 32)
    return {"x": (shard & 1) * 2 + (blk >> 1), "y": (shard >> 1) & 3, "z": shard >> 3, "c": blk & 1}


def device_at(x, y, z, c):
    return ((x & 1) * 2 + c) * 32 + z * 8 + y * 2 + (x >> 1)


def along(axis0, axis1, by):
    pairs = []
    for device in range(128):
        place = place_of(device)
        axis = axis1 if place["c"] else axis0
        place[axis] = (place[axis] + by) % SIDE
        pairs.append((device, device_at(**place)))
    return pairs


def to_core(value):
    pairs = []
    for device in range(128):
        place = place_of(device)
        place["c"] = 1 - place["c"]
        pairs.append((device, device_at(**place)))
    return lax.ppermute(value, AXES, pairs)


def shift(value, axes, by):
    return lax.ppermute(value, AXES, along(*axes, by))


COST = 1
SWAPS = ((), (0, 1), (2,))
SLOTS = 3
STEPS = (0, 1, -1, 2)
TURN = (0, 1, 3, 2)
ORDERS = (("x", "z"), ("y", "x"), ("z", "y"))


def spread(value, axes, here):
    out = jnp.zeros((SIDE,) + value.shape, value.dtype)
    out = lax.dynamic_update_index_in_dim(out, value, here, 0)
    for by in (2, 1, -1):
        got = shift(value, axes, by)
        out = lax.dynamic_update_index_in_dim(out, got, (here - by) % SIDE, 0)
    return out.reshape((SIDE * value.shape[0],) + value.shape[1:])


def places():
    blk, shard = lax.axis_index("blk"), lax.axis_index("shard")
    at = {"x": (shard & 1) * 2 + (blk >> 1), "y": (shard >> 1) & 3, "z": shard >> 3}
    return blk & 1, [[at[axes[kind]] for axes in ORDERS] for kind in range(2)]


def sources(place):
    return [(place[2] - by) & 3 for by in STEPS], [(place[1] + by) & 3 for by in TURN]


def in_vmem(value):
    return pltpu.with_memory_space_constraint(value, pltpu.VMEM)


def in_hbm(value):
    return pltpu.with_memory_space_constraint(value, pltpu.HBM)


def score_kernel(scale, sizes, *refs):
    count = sum(len(parts) for parts in sizes)
    rows = refs[:count]
    cents, biases = refs[count : count + 2], refs[count + 2 : count + 4]
    outs, refs = refs[count + 4 : count + 6], refs[count + 6 :]
    stat_ref, staged, part_sems, kept_sems = refs
    cent, width = cents[0].shape
    core, place = places()
    mids = [sources(p)[1] for p in place]
    mid = [jnp.where(core == 0, a, b) for a, b in zip(*mids)]
    lane = lax.broadcasted_iota(jnp.int32, (LANES, LANES), 1)
    copies = []
    ref = iter(rows)
    for k, parts in enumerate(sizes):
        done = 0
        for n, size in enumerate(parts):
            rows_ref = next(ref)
            copy = pltpu.make_async_copy(
                rows_ref, outs[1].at[k, pl.ds(done, size), pl.ds(cent, width)], kept_sems.at[k, n]
            )
            copy.start()
            copies.append(copy)
            done += size
    ref = iter(rows)
    for k, parts in enumerate(sizes):
        done = 0
        for size in parts:
            rows_ref = next(ref)
            for start in range(0, size, CHUNK):
                scores = [
                    lax.dot_general(
                        rows_ref[start : start + CHUNK, :],
                        cent_ref[...],
                        (((1,), (1,)), ((), ())),
                        preferred_element_type=jnp.float32,
                    )
                    * scale
                    - bias_ref[...]
                    for cent_ref, bias_ref in zip(cents, biases)
                ]
                for t in range(CHUNK // LANES):
                    cut = slice(t * LANES, (t + 1) * LANES)
                    top = jnp.max(jnp.maximum(scores[0][cut], scores[1][cut]), axis=1, keepdims=True)
                    powers = [jnp.exp(score[cut] - top) for score in scores]
                    for c, power in enumerate(powers):
                        staged[c, k, done : done + LANES, :] = power.astype(jnp.bfloat16)
                    total = jnp.sum(powers[0] + powers[1], axis=1, keepdims=True)
                    flat = jnp.where(lane == 0, top, total).T
                    row = mid[done // LANES]
                    stat_ref[k, pl.ds(row, 1), :] = flat[0:1, :]
                    stat_ref[k, pl.ds(SIDE + row, 1), :] = flat[1:2, :]
                    done += LANES
                half = done - CHUNK
                for c in range(2):
                    copy = pltpu.make_async_copy(
                        staged.at[c, k, pl.ds(half, CHUNK)],
                        outs[c].at[k, pl.ds(half, CHUNK), pl.ds(0, cent)],
                        part_sems.at[c, k, half // CHUNK],
                    )
                    copy.start()
                    copies.append(copy)
    for copy in copies:
        copy.wait()


def score_blocks(pieces, cents, biases, scale):
    sizes = [[rows.shape[0] for rows in piece] for piece in pieces]
    rows = [r for piece in pieces for r in piece]
    width = rows[0].shape[1]
    cent = cents[0].shape[0]
    height = sum(sizes[0])
    n = len(pieces)
    count = height * n
    hbm = pl.BlockSpec(memory_space=pl.ANY)
    vmem = pl.BlockSpec(memory_space=pltpu.VMEM)
    return pl.pallas_call(
        functools.partial(score_kernel, scale, sizes),
        out_shape=(
            pltpu.HBM((n, height, cent), jnp.bfloat16),
            pltpu.HBM((n, height, cent + width), jnp.bfloat16),
            jax.ShapeDtypeStruct((n, 2 * height // LANES, LANES), jnp.float32),
        ),
        in_specs=[vmem] * (len(rows) + 4),
        out_specs=(hbm, hbm, vmem),
        scratch_shapes=[
            pltpu.VMEM((2, n, height, cent), jnp.bfloat16),
            pltpu.SemaphoreType.DMA((2, n, height // CHUNK)),
            pltpu.SemaphoreType.DMA((n, 2)),
        ],
        compiler_params=pltpu.CompilerParams(vmem_limit_bytes=14 * 2**20),
        cost_estimate=pl.CostEstimate(
            flops=int(COST * 4 * count * width * cent),
            bytes_accessed=int(COST * (2 * width * (count + 2 * cent) + 4 * count * cent)),
            transcendentals=int(COST * 2 * count * cent),
        ),
        name="scores",
    )(*[in_vmem(v) for v in (*rows, *cents, *biases)])


def weight_kernel(spots, total_rows, *refs):
    pieces = 2 * SIDE
    calls = 1 + max(call for call, _ in spots)
    factors, refs = refs[:2], refs[2:]
    ours, sent, got, refs = refs[:calls], refs[calls : 2 * calls], refs[2 * calls : 3 * calls], refs[3 * calls :]
    out_ref, sums_ref, loads_ref, parts, blocks, staged, rounded, sems, part_sems, block_sems = refs
    tiles = SIDE
    cent = sums_ref.shape[0]

    def fetches(i):
        if i >= SIDE:
            return ()
        call, k = spots[i]
        return (
            pltpu.make_async_copy(ours[call].at[k], parts.at[i], part_sems.at[i]),
            pltpu.make_async_copy(
                sent[call].at[k, :, pl.ds(cent, blocks.shape[2])], blocks.at[i], block_sems.at[i]
            ),
        )

    def part_of(i, part):
        if i < SIDE:
            return parts[i, part, :]
        call, k = spots[i - SIDE]
        return got[call][k, part, :cent]

    def block_of(i):
        if i < SIDE:
            return blocks[i]
        call, k = spots[i - SIDE]
        return got[call][k, :, cent:]

    for i in range(SIDE):
        for copy in fetches(i):
            copy.start()

    here, place = places()
    found = [sources(p) for p in place]

    def body(core):
        def sends(i):
            slot = i % SLOTS
            kind = core if i < SIDE else 1 - core
            last = found[kind][0][i % SIDE]
            for x_lo in range(2):
                for j in range(2):
                    if kind == 0:
                        there = out_ref.at[x_lo, 0, j, last]
                    else:
                        there = out_ref.at[x_lo, 1, j, :, last]
                    yield pltpu.make_async_copy(staged.at[slot, x_lo, j], there, sems.at[slot])

        def add_sums(i):
            for copy in fetches(i)[1:]:
                copy.wait()
            part_sums = lax.dot_general(
                rounded[i % 2],
                block_of(i),
                (((0,), (0,)), ((), ())),
                preferred_element_type=jnp.float32,
            )
            if i == 0:
                sums_ref[...] = part_sums
            elif i + 1 < pieces:
                sums_ref[...] += part_sums
            else:
                sums_ref[...] = (sums_ref[...] + part_sums) * (1.0 / math.sqrt(total_rows))

        load = jnp.zeros((8, cent), jnp.float32)
        for i in range(pieces):
            slot = i % SLOTS
            if i >= SLOTS:
                for copy in sends(i - SLOTS):
                    copy.wait()
            kind = core if i < SIDE else 1 - core
            for copy in fetches(i)[:1]:
                copy.wait()
            for t in range(tiles):
                mid = found[kind][1][t]
                part = slice(t * LANES, (t + 1) * LANES)
                row = factors[i // SIDE][found[kind][0][i % SIDE], pl.ds(mid, 1), :]
                column = jnp.broadcast_to(row, (LANES, LANES)).T
                column = jnp.concatenate([column] * (cent // LANES), axis=1)
                weight = part_of(i, part).astype(jnp.float32) * column
                for p in range(SIDE):
                    for j in range(2):
                        chunk = weight[(p * 2 + j) * 16 : (p * 2 + j) * 16 + 16]
                        if kind == 0:
                            staged[slot, p % 2, j, mid, p // 2] = chunk
                        else:
                            staged[slot, mid & 1, j, p, mid >> 1] = chunk
                load = load + jnp.sum(weight.reshape(LANES // 8, 8, cent), axis=0)
                rounded[i % 2, part, :] = weight.astype(jnp.bfloat16)
            if i:
                add_sums(i - 1)
            for copy in sends(i):
                copy.start()
        add_sums(pieces - 1)
        loads_ref[...] = jnp.sum(load, axis=0, keepdims=True) * (1.0 / total_rows)
        for i in range(pieces - SLOTS, pieces):
            for copy in sends(i):
                copy.wait()

    for core in range(2):

        @pl.when(here == core)
        def _(core=core):
            body(core)


def weight_all(factors, ours, sent, got, spots, total_rows):
    _, height, cent = ours[0].shape
    width = sent[0].shape[2] - cent
    vmem = pl.BlockSpec(memory_space=pltpu.VMEM)
    hbm = pl.BlockSpec(memory_space=pl.ANY)
    return pl.pallas_call(
        functools.partial(weight_kernel, spots, float(total_rows)),
        out_shape=(
            jax.ShapeDtypeStruct((2, 2, 2, 4, 4, 2, 16, cent), jnp.float32),
            jax.ShapeDtypeStruct((cent, width), jnp.float32),
            jax.ShapeDtypeStruct((1, cent), jnp.float32),
        ),
        in_specs=[vmem] * 2
        + [hbm] * (len(ours) + len(sent))
        + [vmem] * len(got),
        out_specs=(hbm, vmem, vmem),
        scratch_shapes=[
            pltpu.VMEM((SIDE, height, cent), jnp.bfloat16),
            pltpu.VMEM((SIDE, height, width), jnp.bfloat16),
            pltpu.VMEM((SLOTS, 2, 2, 4, 2, 16, cent), jnp.float32),
            pltpu.VMEM((2, height, cent), jnp.bfloat16),
            pltpu.SemaphoreType.DMA((SLOTS,)),
            pltpu.SemaphoreType.DMA((SIDE,)),
            pltpu.SemaphoreType.DMA((SIDE,)),
        ],
        compiler_params=pltpu.CompilerParams(vmem_limit_bytes=20 * 2**20),
        name="weights",
    )(*factors, *[in_hbm(v) for v in (*ours, *sent)], *[in_vmem(v) for v in got])


def merged(stats):
    half = stats[0].shape[1] // 2
    tops = [s[:, :half] for s in stats]
    top = functools.reduce(jnp.maximum, tops)
    total = sum(s[:, half:] * jnp.exp(t - top) for s, t in zip(stats, tops))
    return jnp.concatenate([top, total], axis=1)


def per_device(embeddings, centroids, prices):
    core, place = places()
    first_place = jnp.where(core == 0, place[0][0], place[1][0])
    lasts = [sources(p)[0] for p in place]
    width = embeddings.shape[2]
    cent = centroids.shape[0]
    scale = 1.0 / math.sqrt(width)
    bias = (prices.astype(jnp.float32) / 1024.0).reshape(1, cent)
    with jax.named_scope("core"):
        cents, biases = (centroids, to_core(centroids)), (bias, to_core(bias))
    total_cent = cent * 128
    total_rows = embeddings.shape[0] * embeddings.shape[1] * 128

    first = spread(embeddings.reshape(-1, width), ORDERS[0], first_place)
    with jax.named_scope("mid"):
        mids = [first] + [shift(first, ORDERS[1], -by if by < 3 else 1) for by in TURN[1:]]
    own = jnp.concatenate(mids)
    half = own.shape[0] // 2
    axes = ORDERS[2]
    lasts = [jnp.where(core == 0, a, b) for a, b in zip(*lasts)]
    local = jnp.zeros((SIDE, 8, LANES), jnp.float32)
    ours, theirs, got, spots = [], [], [], []

    def score(call, pieces, local):
        our, their, stat = score_blocks(pieces, cents, biases, scale)
        for k, i in enumerate(call):
            spots.append((len(ours), k))
            local = lax.dynamic_update_index_in_dim(local, stat[k], lasts[i], 0)
        ours.append(our)
        theirs.append(their)
        return local

    with jax.named_scope("last"):
        before, after = shift(own, axes, 1), shift(own, axes, -1)
    local = score((0,), [(own,)], local)
    before, after, local = lax.optimization_barrier((before, after, local))
    with jax.named_scope("across"):
        across = shift(before[:half], axes, 1), shift(after[half:], axes, -1)
    local = score((1, 2), [(before,), (after,)], local)
    *across, local = lax.optimization_barrier((*across, local))
    local = score((3,), [across], local)
    stats = local
    for axes, calls in zip(ORDERS, SWAPS):
        with jax.named_scope("core"):
            new = [to_core(theirs[c]) for c in calls]
        stats = merged([stats] + [shift(stats, axes, by) for by in (2, 1, -1)])
        stats, theirs, new = lax.optimization_barrier((stats, theirs, new))
        got += new
    factor = total_cent * jnp.exp(local[:, :SIDE] - (stats[:, :SIDE] + jnp.log(stats[:, SIDE:])))
    with jax.named_scope("core"):
        factors = factor, to_core(factor)
    out, sums, loads = weight_all(factors, ours, theirs, got, spots, total_rows)
    return out.reshape(8, 512, cent), sums, loads.reshape(cent)


def solution(mesh):
    placed = (P("blk", "shard", None), P(AXES, None), P(AXES))
    return jax.shard_map(
        per_device,
        mesh=mesh,
        in_specs=placed,
        out_specs=(P(None, None, AXES), P(AXES, None), P(AXES)),
        check_vma=False,
    )
```

time: 480 us -> 92.6 us (0.19)
  waiting for transfers between devices: 270 us -> 25.9 us
  blocking collectives: 128 us -> 0 us
  starting transfers between devices: 7.47 us -> 40.6 us
  local copies, waits for them, and re-layouts: 30.1 us -> 2.25 us
  Pallas kernels: 0 us -> 22.3 us
  matrix products: 18.1 us -> 0 us
  between operations: 14 us -> 1 us
  other arithmetic: 11.7 us -> 0.19 us
    all_gather x4 -> x0, waiting for transfers between devices: 264 us -> none  [per_device(): block = lax.all_gather(moving, 'shard', axis=1, tiled=True)]
    pmax x1 -> x0, blocking collectives: 65 us -> none  [merge_stats(): global_top = lax.pmax(top, ('blk', 'shard'))]
    psum x1 -> x0, blocking collectives: 62.9 us -> none  [merge_stats(): return (global_top, lax.psum(scaled, ('blk', 'shard')))]
    ppermute x3 -> x25, starting transfers between devices: 7.31 us -> 40.6 us  [the longest x19 27.1 us: shift(): return lax.ppermute(value, AXES, along(*axes, by))]
    pallas_call x0 -> x4, Pallas kernels: none -> 22.3 us  [the longest x3 12.9 us: score_blocks(): pl.pallas_call(functools.partial(score_kernel, scale, sizes), out_shape=(...]
    ppermute x3 -> x25, waiting for transfers between devices: 4.94 us -> 25.9 us  [the longest x19 23.8 us: shift(): return lax.ppermute(value, AXES, along(*axes, by))]
    dot_general x8 -> x0, matrix products: 18.1 us -> none  [the longest x4 11.6 us: per_device(): jnp.einsum('mrd,kd->mrk', block, centroids, preferred_element_type=jnp.fl...]
    unnamed x38 -> x10, local copies, waits for them, and re-layouts: 16.3 us -> 1.24 us
  transfers between devices with their start and end apart: 7 -> 25, of which waited for: 7 -> 18; matrix products, arithmetic and copies ran while one was open for 2% -> 1% of each run, Pallas kernels for 0% -> 10%
where the time goes in v3:
time: 92.6 us; the launch traced here: 92.3 us
  starting transfers between devices  40.6 us (44%)
  waiting for transfers between devices  25.9 us (28%)
  Pallas kernels  22.3 us (24%)
  local copies, waits for them, and re-layouts  2.25 us (2%)
  between operations  1 us (1%)
    ppermute x19, starting transfers between devices, shift(): return lax.ppermute(value, AXES, along(*axes, by))  27.1 us
    ppermute x19, waiting for transfers between devices, shift(): return lax.ppermute(value, AXES, along(*axes, by))  23.8 us
    ppermute x6, starting transfers between devices, to_core(): return lax.ppermute(value, AXES, pairs)  13.5 us
    pallas_call x3, Pallas kernels, score_blocks(): pl.pallas_call(functools.partial(score_kernel, scale, sizes), out_shape=(...  12.9 us
    pallas_call x1, Pallas kernels, weight_all(): pl.pallas_call(functools.partial(weight_kernel, spots, float(total_rows))...  9.43 us
    ppermute x6, waiting for transfers between devices, to_core(): return lax.ppermute(value, AXES, pairs)  2.04 us
  transfers between devices with their start and end apart: 25, of which 18 were waited for; matrix products, arithmetic and copies ran while one was open for 1% of the time, Pallas kernels for 10%

profile of v3, /device:TPU:1, one launch (start us, length us, event | category | flops | bytes accessed | tf_op | source)
XLA Modules:
  0.0 92.3 jit_solution(1324506585159330236)
XLA Ops:
  0.6 4.7 %collective-permute-start.2 = (bf16[32,1024]{1,0:T(8,128)(2,1)}, bf16[32,1024]{1,0:T(8,128)(2,1)S(1)}, u32[]{:S(2)}, u32[]{:S(2)}) collective-permute-start(bf16[32,1024]{1,0:T(8,128)(2,1)} %bitcast.22), channel_id=1, source_target_pairs={{0,65},{1,64},{2,67},{3,66},{4,69},{5,68},{6,71},{7,70},{8,73},{9,... | collective-permute-start | bytes 196616 | tf_op jit(solution)/shard_map/ppermute | solution.py:46
  5.3 1.3 %collective-permute-start = (bf16[32,1024]{1,0:T(8,128)(2,1)}, bf16[32,1024]{1,0:T(8,128)(2,1)S(1)}, u32[]{:S(2)}, u32[]{:S(2)}) collective-permute-start(bf16[32,1024]{1,0:T(8,128)(2,1)} %bitcast.24), channel_id=1, source_target_pairs={{0,1},{1,0},{2,3},{3,2},{4,5},{5,4},{6,7},{7,6},{8,9},{9,8},{10,11... | collective-permute-start | bytes 196616 | tf_op jit(solution)/shard_map/ppermute | solution.py:46
  6.6 0.9 bitcast_dynamic-update-slice_fusion.3
  7.5 2.9 %collective-permute-done = bf16[32,1024]{1,0:T(8,128)(2,1)S(1)} collective-permute-done((bf16[32,1024]{1,0:T(8,128)(2,1)}, bf16[32,1024]{1,0:T(8,128)(2,1)S(1)}, u32[]{:S(2)}, u32[]{:S(2)}) %collective-permute-start) | collective-permute-done | bytes 65568 | tf_op jit(solution)/shard_map/ppermute | solution.py:46
  10.4 0.4 collective-permute-done.1
  10.8 0.0 collective-permute-done.2
  10.9 2.5 %collective-permute-start.5 = (bf16[128,1024]{1,0:T(8,128)(2,1)S(1)}, bf16[128,1024]{1,0:T(8,128)(2,1)S(1)}, u32[]{:S(2)}, u32[]{:S(2)}) collective-permute-start(bf16[128,1024]{1,0:T(8,128)(2,1)S(1)} %bitcast.18), channel_id=1, source_target_pairs={{0,4},{1,5},{2,6},{3,7},{4,0},{5,1},{6,2},{7,3},{8,12},{9,13},{10,... | collective-permute-start | bytes 786440 | tf_op jit(solution)/shard_map/mid/ppermute | solution.py:46
  13.4 0.6 collective-permute-start.4
  14.0 2.1 %collective-permute-start.3 = (bf16[128,1024]{1,0:T(8,128)(2,1)S(1)}, bf16[128,1024]{1,0:T(8,128)(2,1)S(1)}, u32[]{:S(2)}, u32[]{:S(2)}) collective-permute-start(bf16[128,1024]{1,0:T(8,128)(2,1)S(1)} %bitcast.20), channel_id=1, source_target_pairs={{0,6},{1,7},{2,0},{3,1},{4,2},{5,3},{6,4},{7,5},{8,14},{9,15},{10,... | collective-permute-start | bytes 786440 | tf_op jit(solution)/shard_map/mid/ppermute | solution.py:46
  16.1 1.8 %collective-permute-start.8 = (bf16[512,1024]{1,0:T(8,128)(2,1)}, bf16[512,1024]{1,0:T(8,128)(2,1)}, u32[]{:S(2)}, u32[]{:S(2)}) collective-permute-start(bf16[512,1024]{1,0:T(8,128)(2,1)} %refs_2_.3), channel_id=1, source_target_pairs={{0,32},{1,33},{2,34},{3,35},{4,36},{5,37},{6,38},{7,39},{8,40},{9,... | collective-permute-start | bytes 3145736 | tf_op jit(solution)/shard_map/core/ppermute | solution.py:42
  17.9 0.1 collective-permute-done.5
  18.0 2.8 %collective-permute-done.4 = bf16[128,1024]{1,0:T(8,128)(2,1)S(1)} collective-permute-done((bf16[128,1024]{1,0:T(8,128)(2,1)S(1)}, bf16[128,1024]{1,0:T(8,128)(2,1)S(1)}, u32[]{:S(2)}, u32[]{:S(2)}) %collective-permute-start.4) | collective-permute-done | bytes 262176 | tf_op jit(solution)/shard_map/mid/ppermute | solution.py:46
  20.8 0.1 collective-permute-done.3
  20.9 0.1 pad_maximum_fusion.refs_0_
  20.9 2.8 %collective-permute-start.7 = (bf16[512,1024]{1,0:T(8,128)(2,1)S(1)}, bf16[512,1024]{1,0:T(8,128)(2,1)S(1)}, u32[]{:S(2)}, u32[]{:S(2)}) collective-permute-start(bf16[512,1024]{1,0:T(8,128)(2,1)S(1)} %pad_maximum_fusion.refs_0_), channel_id=1, source_target_pairs={{0,24},{1,25},{2,26},{3,27},{4,28},{5,29},{6,30},{7,31},{8,0},{9,1... | collective-permute-start | bytes 3145736 | tf_op jit(solution)/shard_map/last/ppermute | solution.py:46
  23.7 0.0 collective-permute-start.6
  23.8 3.1 %collective-permute-start.9 = (f32[1,512]{1,0:T(1,128)S(1)}, f32[1,512]{1,0:T(1,128)S(1)}, u32[]{:S(2)}, u32[]{:S(2)}) collective-permute-start(f32[1,512]{1,0:T(1,128)S(1)} %bitcast.14), channel_id=1, source_target_pairs={{0,32},{1,33},{2,34},{3,35},{4,36},{5,37},{6,38},{7,39},{8,40},{9,... | collective-permute-start | bytes 6152 | tf_op jit(solution)/shard_map/core/ppermute | solution.py:42
  26.9 0.8 collective-permute-done.9.refs_4_.refs_5_
  27.7 1.2 %copy-done = bf16[512,1024]{1,0:T(8,128)(2,1)S(1)} copy-done((bf16[512,1024]{1,0:T(8,128)(2,1)S(1)}, bf16[512,1024]{1,0:T(8,128)(2,1)}, u32[]{:S(2)}) %copy-start) | copy-done | bytes 1048600
  28.9 3.8 %scores.3 = (bf16[1,512,512]{2,1,0:T(8,128)(2,1)}, bf16[1,512,1536]{2,1,0:T(8,128)(2,1)}, f32[1,8,128]{2,1,0:T(8,128)S(1)}) custom-call(bf16[512,1024]{1,0:T(8,128)(2,1)S(1)} %pad_maximum_fusion.refs_0_, bf16[512,1024]{1,0:T(8,128)(2,1)S(1)} %copy-done, bf16[512,1024]{1,0:T(8,128)(2,1)} %collective-permute-done.8.refs_2_.refs_3_, f32[1,512]{1,0:T(1,128)S(1)} %bitcast.15, ...), custom_call_target="tpu_custom_call" | custom-call | flops 1073741824 | bytes 4194304 | tf_op jit(solution)/shard_map/scores/pallas_call | solution.py:159
  32.8 2.7 %collective-permute-done.7.refs_1_ = bf16[512,1024]{1,0:T(8,128)(2,1)S(1)} collective-permute-done((bf16[512,1024]{1,0:T(8,128)(2,1)S(1)}, bf16[512,1024]{1,0:T(8,128)(2,1)S(1)}, u32[]{:S(2)}, u32[]{:S(2)}) %collective-permute-start.7) | collective-permute-done | bytes 1048608 | tf_op jit(solution)/shard_map/last/ppermute | solution.py:46
  35.5 3.4 %collective-permute-done.6.refs_0_ = bf16[512,1024]{1,0:T(8,128)(2,1)S(1)} collective-permute-done((bf16[512,1024]{1,0:T(8,128)(2,1)S(1)}, bf16[512,1024]{1,0:T(8,128)(2,1)S(1)}, u32[]{:S(2)}, u32[]{:S(2)}) %collective-permute-start.6) | collective-permute-done | bytes 1048608 | tf_op jit(solution)/shard_map/last/ppermute | solution.py:46
  39.0 0.1 collective-permute-start.11
  39.1 1.5 %collective-permute-start.10 = (bf16[256,1024]{1,0:T(8,128)(2,1)S(1)}, bf16[256,1024]{1,0:T(8,128)(2,1)S(1)}, u32[]{:S(2)}, u32[]{:S(2)}) collective-permute-start(bf16[256,1024]{1,0:T(8,128)(2,1)S(1)} %slice.91), channel_id=1, source_target_pairs={{0,8},{1,9},{2,10},{3,11},{4,12},{5,13},{6,14},{7,15},{8,16},{9,17... | collective-permute-start | bytes 1572872 | tf_op jit(solution)/shard_map/across/ppermute | solution.py:46
  40.5 5.3 %scores.4 = (bf16[2,512,512]{2,1,0:T(8,128)(2,1)}, bf16[2,512,1536]{2,1,0:T(8,128)(2,1)}, f32[2,8,128]{2,1,0:T(8,128)S(1)}) custom-call(bf16[512,1024]{1,0:T(8,128)(2,1)S(1)} %collective-permute-done.6.refs_0_, bf16[512,1024]{1,0:T(8,128)(2,1)S(1)} %collective-permute-done.7.refs_1_, bf16[512,1024]{1,0:T(8,128)(2,1)S(1)} %copy-done.1, ...), custom_call_target="tpu_custom_call" | custom-call | flops 2147483648 | bytes 6291456 | tf_op jit(solution)/shard_map/scores/pallas_call | solution.py:159
  45.9 1.5 %collective-permute-done.11.refs_1_ = bf16[256,1024]{1,0:T(8,128)(2,1)S(1)} collective-permute-done((bf16[256,1024]{1,0:T(8,128)(2,1)S(1)}, bf16[256,1024]{1,0:T(8,128)(2,1)S(1)}, u32[]{:S(2)}, u32[]{:S(2)}) %collective-permute-start.11) | collective-permute-done | bytes 524320 | tf_op jit(solution)/shard_map/across/ppermute | solution.py:46
  47.4 1.3 %collective-permute-done.10.refs_0_ = bf16[256,1024]{1,0:T(8,128)(2,1)S(1)} collective-permute-done((bf16[256,1024]{1,0:T(8,128)(2,1)S(1)}, bf16[256,1024]{1,0:T(8,128)(2,1)S(1)}, u32[]{:S(2)}, u32[]{:S(2)}) %collective-permute-start.10) | collective-permute-done | bytes 524320 | tf_op jit(solution)/shard_map/across/ppermute | solution.py:46
  48.7 3.8 %scores.5 = (bf16[1,512,512]{2,1,0:T(8,128)(2,1)}, bf16[1,512,1536]{2,1,0:T(8,128)(2,1)}, f32[1,8,128]{2,1,0:T(8,128)S(1)}) custom-call(bf16[256,1024]{1,0:T(8,128)(2,1)S(1)} %collective-permute-done.10.refs_0_, bf16[256,1024]{1,0:T(8,128)(2,1)S(1)} %collective-permute-done.11.refs_1_, bf16[512,1024]{1,0:T(8,128)(2,1)S(1)} %copy-done.1, ...), custom_call_target="tpu_custom_call" | custom-call | flops 1073741824 | bytes 4194304 | tf_op jit(solution)/shard_map/scores/pallas_call | solution.py:159
  52.5 2.1 %collective-permute-start.14 = (f32[4,8,128]{2,1,0:T(8,128)S(1)}, f32[4,8,128]{2,1,0:T(8,128)S(1)}, u32[]{:S(2)}, u32[]{:S(2)}) collective-permute-start(f32[4,8,128]{2,1,0:T(8,128)S(1)} %constant_dynamic-update-slice_fusion), channel_id=1, source_target_pairs={{0,65},{1,64},{2,67},{3,66},{4,69},{5,68},{6,71},{7,70},{8,73},{9,... | collective-permute-start | bytes 49160 | tf_op jit(solution)/shard_map/ppermute | solution.py:46
  54.5 1.3 %collective-permute-start.12 = (f32[4,8,128]{2,1,0:T(8,128)S(1)}, f32[4,8,128]{2,1,0:T(8,128)S(1)}, u32[]{:S(2)}, u32[]{:S(2)}) collective-permute-start(f32[4,8,128]{2,1,0:T(8,128)S(1)} %constant_dynamic-update-slice_fusion), channel_id=1, source_target_pairs={{0,1},{1,0},{2,3},{3,2},{4,5},{5,4},{6,7},{7,6},{8,9},{9,8},{10,11... | collective-permute-start | bytes 49160 | tf_op jit(solution)/shard_map/ppermute | solution.py:46
  55.8 0.0 collective-permute-done.14
  55.8 2.5 %collective-permute-done.13 = f32[4,8,128]{2,1,0:T(8,128)S(1)} collective-permute-done((f32[4,8,128]{2,1,0:T(8,128)S(1)}, f32[4,8,128]{2,1,0:T(8,128)S(1)}, u32[]{:S(2)}, u32[]{:S(2)}) %collective-permute-start.13) | collective-permute-done | bytes 16416 | tf_op jit(solution)/shard_map/ppermute | solution.py:46
  58.3 0.3 collective-permute-done.12
  58.7 7.1 %collective-permute-start.19 = (bf16[2,512,1536]{2,1,0:T(8,128)(2,1)S(1)}, bf16[2,512,1536]{2,1,0:T(8,128)(2,1)S(1)}, u32[]{:S(2)}, u32[]{:S(2)}) collective-permute-start(bf16[2,512,1536]{2,1,0:T(8,128)(2,1)S(1)} %copy-done.2), channel_id=1, source_target_pairs={{0,32},{1,33},{2,34},{3,35},{4,36},{5,37},{6,38},{7,39},{8,40},{9,... | collective-permute-start | bytes 9437192 | tf_op jit(solution)/shard_map/core/ppermute | solution.py:42
  65.8 0.1 collective-permute-start.18
  65.9 3.0 %collective-permute-start.17 = (f32[4,8,128]{2,1,0:T(8,128)S(1)}, f32[4,8,128]{2,1,0:T(8,128)S(1)}, u32[]{:S(2)}, u32[]{:S(2)}) collective-permute-start(f32[4,8,128]{2,1,0:T(8,128)S(1)} %pad_maximum_fusion.1), channel_id=1, source_target_pairs={{0,6},{1,7},{2,0},{3,1},{4,2},{5,3},{6,4},{7,5},{8,14},{9,15},{10,... | collective-permute-start | bytes 49160 | tf_op jit(solution)/shard_map/ppermute | solution.py:46
  68.8 1.2 %collective-permute-start.15 = (f32[4,8,128]{2,1,0:T(8,128)S(1)}, f32[4,8,128]{2,1,0:T(8,128)S(1)}, u32[]{:S(2)}, u32[]{:S(2)}) collective-permute-start(f32[4,8,128]{2,1,0:T(8,128)S(1)} %pad_maximum_fusion.1), channel_id=1, source_target_pairs={{0,4},{1,5},{2,6},{3,7},{4,0},{5,1},{6,2},{7,3},{8,12},{9,13},{10,... | collective-permute-start | bytes 49160 | tf_op jit(solution)/shard_map/ppermute | solution.py:46
  70.0 2.6 %collective-permute-done.16 = f32[4,8,128]{2,1,0:T(8,128)S(1)} collective-permute-done((f32[4,8,128]{2,1,0:T(8,128)S(1)}, f32[4,8,128]{2,1,0:T(8,128)S(1)}, u32[]{:S(2)}, u32[]{:S(2)}) %collective-permute-start.16) | collective-permute-done | bytes 16416 | tf_op jit(solution)/shard_map/ppermute | solution.py:46
  72.6 0.3 collective-permute-done.15
  73.0 0.3 collective-permute-done.18.refs_8_
  73.3 1.0 %collective-permute-start.23 = (bf16[1,512,1536]{2,1,0:T(8,128)(2,1)}, bf16[1,512,1536]{2,1,0:T(8,128)(2,1)S(1)}, u32[]{:S(2)}, u32[]{:S(2)}) collective-permute-start(bf16[1,512,1536]{2,1,0:T(8,128)(2,1)} %get-tuple-element.62.refs_7_), channel_id=1, source_target_pairs={{0,32},{1,33},{2,34},{3,35},{4,36},{5,37},{6,38},{7,39},{8,40},{9,... | collective-permute-start | bytes 4718600 | tf_op jit(solution)/shard_map/core/ppermute | solution.py:42
  74.3 3.0 %collective-permute-start.22 = (f32[4,8,128]{2,1,0:T(8,128)S(1)}, f32[4,8,128]{2,1,0:T(8,128)S(1)}, u32[]{:S(2)}, u32[]{:S(2)}) collective-permute-start(f32[4,8,128]{2,1,0:T(8,128)S(1)} %pad_maximum_fusion.2), channel_id=1, source_target_pairs={{0,24},{1,25},{2,26},{3,27},{4,28},{5,29},{6,30},{7,31},{8,0},{9,1... | collective-permute-start | bytes 49160 | tf_op jit(solution)/shard_map/ppermute | solution.py:46
  77.3 1.2 %collective-permute-start.20 = (f32[4,8,128]{2,1,0:T(8,128)S(1)}, f32[4,8,128]{2,1,0:T(8,128)S(1)}, u32[]{:S(2)}, u32[]{:S(2)}) collective-permute-start(f32[4,8,128]{2,1,0:T(8,128)S(1)} %pad_maximum_fusion.2), channel_id=1, source_target_pairs={{0,16},{1,17},{2,18},{3,19},{4,20},{5,21},{6,22},{7,23},{8,24},{9,... | collective-permute-start | bytes 49160 | tf_op jit(solution)/shard_map/ppermute | solution.py:46
  78.4 2.8 %collective-permute-done.21 = f32[4,8,128]{2,1,0:T(8,128)S(1)} collective-permute-done((f32[4,8,128]{2,1,0:T(8,128)S(1)}, f32[4,8,128]{2,1,0:T(8,128)S(1)}, u32[]{:S(2)}, u32[]{:S(2)}) %collective-permute-start.21) | collective-permute-done | bytes 16416 | tf_op jit(solution)/shard_map/ppermute | solution.py:46
  81.3 0.1 collective-permute-done.20
  81.4 0.4 collective-permute-start.24
  81.8 0.9 collective-permute-done.24.refs_1_
  82.7 9.4 %weights.1 = (f32[2,2,2,4,4,2,16,512]{7,6,5,4,3,2,1,0:T(8,128)}, f32[512,1024]{1,0:T(8,128)}, f32[1,512]{1,0:T(1,128)}) custom-call(f32[4,4,128]{2,1,0:T(4,128)S(1)} %exponential_multiply_fusion.refs_0_, f32[4,4,128]{2,1,0:T(4,128)S(1)} %collective-permute-done.24.refs_1_, bf16[1,512,512]{2,1,0:T(8,128)(2,1)} %get-tuple-element.57.refs_2_, ...), custom_call_target="tpu_custom_call" | custom-call | tf_op jit(solution)/shard_map/weights/pallas_call | solution.py:298
  (37 shorter events, 0.3 us)
Async XLA Ops:
  0.6 23.1 %copy-start.4 = (s32[512]{0:T(512)S(1)}, s32[512]{0:T(512)}, u32[]{:S(2)}) copy-start(s32[512]{0:T(512)} %param.5) | copy-start | bytes 6148
  0.6 10.2 %collective-permute-start.2 = (bf16[32,1024]{1,0:T(8,128)(2,1)}, bf16[32,1024]{1,0:T(8,128)(2,1)S(1)}, u32[]{:S(2)}, u32[]{:S(2)}) collective-permute-start(bf16[32,1024]{1,0:T(8,128)(2,1)} %bitcast.22), channel_id=1, source_target_pairs={{0,65},{1,64},{2,67},{3,66},{4,69},{5,68},{6,71},{7,70},{8,73},{9,... | collective-permute-start | bytes 196616 | tf_op jit(solution)/shard_map/ppermute | solution.py:46
  5.3 5.5 %collective-permute-start.1 = (bf16[32,1024]{1,0:T(8,128)(2,1)}, bf16[32,1024]{1,0:T(8,128)(2,1)S(1)}, u32[]{:S(2)}, u32[]{:S(2)}) collective-permute-start(bf16[32,1024]{1,0:T(8,128)(2,1)} %bitcast.23), channel_id=1, source_target_pairs={{0,64},{1,65},{2,66},{3,67},{4,68},{5,69},{6,70},{7,71},{8,72},{9,... | collective-permute-start | bytes 196616 | tf_op jit(solution)/shard_map/ppermute | solution.py:46
  5.3 5.1 %collective-permute-start = (bf16[32,1024]{1,0:T(8,128)(2,1)}, bf16[32,1024]{1,0:T(8,128)(2,1)S(1)}, u32[]{:S(2)}, u32[]{:S(2)}) collective-permute-start(bf16[32,1024]{1,0:T(8,128)(2,1)} %bitcast.24), channel_id=1, source_target_pairs={{0,1},{1,0},{2,3},{3,2},{4,5},{5,4},{6,7},{7,6},{8,9},{9,8},{10,11... | collective-permute-start | bytes 196616 | tf_op jit(solution)/shard_map/ppermute | solution.py:46
  10.9 7.1 %collective-permute-start.5 = (bf16[128,1024]{1,0:T(8,128)(2,1)S(1)}, bf16[128,1024]{1,0:T(8,128)(2,1)S(1)}, u32[]{:S(2)}, u32[]{:S(2)}) collective-permute-start(bf16[128,1024]{1,0:T(8,128)(2,1)S(1)} %bitcast.18), channel_id=1, source_target_pairs={{0,4},{1,5},{2,6},{3,7},{4,0},{5,1},{6,2},{7,3},{8,12},{9,13},{10,... | collective-permute-start | bytes 786440 | tf_op jit(solution)/shard_map/mid/ppermute | solution.py:46
  13.4 7.4 %collective-permute-start.4 = (bf16[128,1024]{1,0:T(8,128)(2,1)S(1)}, bf16[128,1024]{1,0:T(8,128)(2,1)S(1)}, u32[]{:S(2)}, u32[]{:S(2)}) collective-permute-start(bf16[128,1024]{1,0:T(8,128)(2,1)S(1)} %bitcast.19), channel_id=1, source_target_pairs={{0,2},{1,3},{2,4},{3,5},{4,6},{5,7},{6,0},{7,1},{8,10},{9,11},{10,... | collective-permute-start | bytes 786440 | tf_op jit(solution)/shard_map/mid/ppermute | solution.py:46
  14.0 6.9 %collective-permute-start.3 = (bf16[128,1024]{1,0:T(8,128)(2,1)S(1)}, bf16[128,1024]{1,0:T(8,128)(2,1)S(1)}, u32[]{:S(2)}, u32[]{:S(2)}) collective-permute-start(bf16[128,1024]{1,0:T(8,128)(2,1)S(1)} %bitcast.20), channel_id=1, source_target_pairs={{0,6},{1,7},{2,0},{3,1},{4,2},{5,3},{6,4},{7,5},{8,14},{9,15},{10,... | collective-permute-start | bytes 786440 | tf_op jit(solution)/shard_map/mid/ppermute | solution.py:46
  16.1 11.6 %collective-permute-start.8 = (bf16[512,1024]{1,0:T(8,128)(2,1)}, bf16[512,1024]{1,0:T(8,128)(2,1)}, u32[]{:S(2)}, u32[]{:S(2)}) collective-permute-start(bf16[512,1024]{1,0:T(8,128)(2,1)} %refs_2_.3), channel_id=1, source_target_pairs={{0,32},{1,33},{2,34},{3,35},{4,36},{5,37},{6,38},{7,39},{8,40},{9,... | collective-permute-start | bytes 3145736 | tf_op jit(solution)/shard_map/core/ppermute | solution.py:42
  20.9 14.5 %collective-permute-start.7 = (bf16[512,1024]{1,0:T(8,128)(2,1)S(1)}, bf16[512,1024]{1,0:T(8,128)(2,1)S(1)}, u32[]{:S(2)}, u32[]{:S(2)}) collective-permute-start(bf16[512,1024]{1,0:T(8,128)(2,1)S(1)} %pad_maximum_fusion.refs_0_), channel_id=1, source_target_pairs={{0,24},{1,25},{2,26},{3,27},{4,28},{5,29},{6,30},{7,31},{8,0},{9,1... | collective-permute-start | bytes 3145736 | tf_op jit(solution)/shard_map/last/ppermute | solution.py:46
  23.7 15.2 %collective-permute-start.6 = (bf16[512,1024]{1,0:T(8,128)(2,1)S(1)}, bf16[512,1024]{1,0:T(8,128)(2,1)S(1)}, u32[]{:S(2)}, u32[]{:S(2)}) collective-permute-start(bf16[512,1024]{1,0:T(8,128)(2,1)S(1)} %pad_maximum_fusion.refs_0_), channel_id=1, source_target_pairs={{0,8},{1,9},{2,10},{3,11},{4,12},{5,13},{6,14},{7,15},{8,16},{9,17... | collective-permute-start | bytes 3145736 | tf_op jit(solution)/shard_map/last/ppermute | solution.py:46
  23.8 3.9 %collective-permute-start.9 = (f32[1,512]{1,0:T(1,128)S(1)}, f32[1,512]{1,0:T(1,128)S(1)}, u32[]{:S(2)}, u32[]{:S(2)}) collective-permute-start(f32[1,512]{1,0:T(1,128)S(1)} %bitcast.14), channel_id=1, source_target_pairs={{0,32},{1,33},{2,34},{3,35},{4,36},{5,37},{6,38},{7,39},{8,40},{9,... | collective-permute-start | bytes 6152 | tf_op jit(solution)/shard_map/core/ppermute | solution.py:42
  27.7 1.2 %copy-start = (bf16[512,1024]{1,0:T(8,128)(2,1)S(1)}, bf16[512,1024]{1,0:T(8,128)(2,1)}, u32[]{:S(2)}) copy-start(bf16[512,1024]{1,0:T(8,128)(2,1)} %refs_2_.3) | copy-start | bytes 3145732
  28.9 11.6 %copy-start.1 = (bf16[512,1024]{1,0:T(8,128)(2,1)S(1)}, bf16[512,1024]{1,0:T(8,128)(2,1)}, u32[]{:S(2)}) copy-start(bf16[512,1024]{1,0:T(8,128)(2,1)} %refs_2_.3) | copy-start | bytes 3145732
  39.0 8.4 %collective-permute-start.11 = (bf16[256,1024]{1,0:T(8,128)(2,1)S(1)}, bf16[256,1024]{1,0:T(8,128)(2,1)S(1)}, u32[]{:S(2)}, u32[]{:S(2)}) collective-permute-start(bf16[256,1024]{1,0:T(8,128)(2,1)S(1)} %slice.92), channel_id=1, source_target_pairs={{0,24},{1,25},{2,26},{3,27},{4,28},{5,29},{6,30},{7,31},{8,0},{9,1... | collective-permute-start | bytes 1572872 | tf_op jit(solution)/shard_map/across/ppermute | solution.py:46
  39.1 9.6 %collective-permute-start.10 = (bf16[256,1024]{1,0:T(8,128)(2,1)S(1)}, bf16[256,1024]{1,0:T(8,128)(2,1)S(1)}, u32[]{:S(2)}, u32[]{:S(2)}) collective-permute-start(bf16[256,1024]{1,0:T(8,128)(2,1)S(1)} %slice.91), channel_id=1, source_target_pairs={{0,8},{1,9},{2,10},{3,11},{4,12},{5,13},{6,14},{7,15},{8,16},{9,17... | collective-permute-start | bytes 1572872 | tf_op jit(solution)/shard_map/across/ppermute | solution.py:46
  40.5 25.3 %copy-start.3 = (bf16[1,512,1536]{2,1,0:T(8,128)(2,1)S(1)}, bf16[1,512,1536]{2,1,0:T(8,128)(2,1)}, u32[]{:S(2)}) copy-start(bf16[1,512,1536]{2,1,0:T(8,128)(2,1)} %get-tuple-element.60.refs_5_) | copy-start | bytes 4718596
  45.9 12.8 %copy-start.2 = (bf16[2,512,1536]{2,1,0:T(8,128)(2,1)S(1)}, bf16[2,512,1536]{2,1,0:T(8,128)(2,1)}, u32[]{:S(2)}) copy-start(bf16[2,512,1536]{2,1,0:T(8,128)(2,1)} %get-tuple-element.61.refs_6_) | copy-start | bytes 9437188
  52.5 3.3 %collective-permute-start.14 = (f32[4,8,128]{2,1,0:T(8,128)S(1)}, f32[4,8,128]{2,1,0:T(8,128)S(1)}, u32[]{:S(2)}, u32[]{:S(2)}) collective-permute-start(f32[4,8,128]{2,1,0:T(8,128)S(1)} %constant_dynamic-update-slice_fusion), channel_id=1, source_target_pairs={{0,65},{1,64},{2,67},{3,66},{4,69},{5,68},{6,71},{7,70},{8,73},{9,... | collective-permute-start | bytes 49160 | tf_op jit(solution)/shard_map/ppermute | solution.py:46
  54.5 3.8 %collective-permute-start.13 = (f32[4,8,128]{2,1,0:T(8,128)S(1)}, f32[4,8,128]{2,1,0:T(8,128)S(1)}, u32[]{:S(2)}, u32[]{:S(2)}) collective-permute-start(f32[4,8,128]{2,1,0:T(8,128)S(1)} %constant_dynamic-update-slice_fusion), channel_id=1, source_target_pairs={{0,64},{1,65},{2,66},{3,67},{4,68},{5,69},{6,70},{7,71},{8,72},{9,... | collective-permute-start | bytes 49160 | tf_op jit(solution)/shard_map/ppermute | solution.py:46
  54.5 4.1 %collective-permute-start.12 = (f32[4,8,128]{2,1,0:T(8,128)S(1)}, f32[4,8,128]{2,1,0:T(8,128)S(1)}, u32[]{:S(2)}, u32[]{:S(2)}) collective-permute-start(f32[4,8,128]{2,1,0:T(8,128)S(1)} %constant_dynamic-update-slice_fusion), channel_id=1, source_target_pairs={{0,1},{1,0},{2,3},{3,2},{4,5},{5,4},{6,7},{7,6},{8,9},{9,8},{10,11... | collective-permute-start | bytes 49160 | tf_op jit(solution)/shard_map/ppermute | solution.py:46
  58.7 14.6 %collective-permute-start.19 = (bf16[2,512,1536]{2,1,0:T(8,128)(2,1)S(1)}, bf16[2,512,1536]{2,1,0:T(8,128)(2,1)S(1)}, u32[]{:S(2)}, u32[]{:S(2)}) collective-permute-start(bf16[2,512,1536]{2,1,0:T(8,128)(2,1)S(1)} %copy-done.2), channel_id=1, source_target_pairs={{0,32},{1,33},{2,34},{3,35},{4,36},{5,37},{6,38},{7,39},{8,40},{9,... | collective-permute-start | bytes 9437192 | tf_op jit(solution)/shard_map/core/ppermute | solution.py:42
  65.8 7.5 %collective-permute-start.18 = (bf16[1,512,1536]{2,1,0:T(8,128)(2,1)S(1)}, bf16[1,512,1536]{2,1,0:T(8,128)(2,1)S(1)}, u32[]{:S(2)}, u32[]{:S(2)}) collective-permute-start(bf16[1,512,1536]{2,1,0:T(8,128)(2,1)S(1)} %copy-done.3), channel_id=1, source_target_pairs={{0,32},{1,33},{2,34},{3,35},{4,36},{5,37},{6,38},{7,39},{8,40},{9,... | collective-permute-start | bytes 4718600 | tf_op jit(solution)/shard_map/core/ppermute | solution.py:42
  65.9 4.1 %collective-permute-start.17 = (f32[4,8,128]{2,1,0:T(8,128)S(1)}, f32[4,8,128]{2,1,0:T(8,128)S(1)}, u32[]{:S(2)}, u32[]{:S(2)}) collective-permute-start(f32[4,8,128]{2,1,0:T(8,128)S(1)} %pad_maximum_fusion.1), channel_id=1, source_target_pairs={{0,6},{1,7},{2,0},{3,1},{4,2},{5,3},{6,4},{7,5},{8,14},{9,15},{10,... | collective-permute-start | bytes 49160 | tf_op jit(solution)/shard_map/ppermute | solution.py:46
  68.8 3.8 %collective-permute-start.16 = (f32[4,8,128]{2,1,0:T(8,128)S(1)}, f32[4,8,128]{2,1,0:T(8,128)S(1)}, u32[]{:S(2)}, u32[]{:S(2)}) collective-permute-start(f32[4,8,128]{2,1,0:T(8,128)S(1)} %pad_maximum_fusion.1), channel_id=1, source_target_pairs={{0,2},{1,3},{2,4},{3,5},{4,6},{5,7},{6,0},{7,1},{8,10},{9,11},{10,... | collective-permute-start | bytes 49160 | tf_op jit(solution)/shard_map/ppermute | solution.py:46
  68.8 4.1 %collective-permute-start.15 = (f32[4,8,128]{2,1,0:T(8,128)S(1)}, f32[4,8,128]{2,1,0:T(8,128)S(1)}, u32[]{:S(2)}, u32[]{:S(2)}) collective-permute-start(f32[4,8,128]{2,1,0:T(8,128)S(1)} %pad_maximum_fusion.1), channel_id=1, source_target_pairs={{0,4},{1,5},{2,6},{3,7},{4,0},{5,1},{6,2},{7,3},{8,12},{9,13},{10,... | collective-permute-start | bytes 49160 | tf_op jit(solution)/shard_map/ppermute | solution.py:46
  73.3 8.1 %collective-permute-start.23 = (bf16[1,512,1536]{2,1,0:T(8,128)(2,1)}, bf16[1,512,1536]{2,1,0:T(8,128)(2,1)S(1)}, u32[]{:S(2)}, u32[]{:S(2)}) collective-permute-start(bf16[1,512,1536]{2,1,0:T(8,128)(2,1)} %get-tuple-element.62.refs_7_), channel_id=1, source_target_pairs={{0,32},{1,33},{2,34},{3,35},{4,36},{5,37},{6,38},{7,39},{8,40},{9,... | collective-permute-start | bytes 4718600 | tf_op jit(solution)/shard_map/core/ppermute | solution.py:42
  74.3 4.1 %collective-permute-start.22 = (f32[4,8,128]{2,1,0:T(8,128)S(1)}, f32[4,8,128]{2,1,0:T(8,128)S(1)}, u32[]{:S(2)}, u32[]{:S(2)}) collective-permute-start(f32[4,8,128]{2,1,0:T(8,128)S(1)} %pad_maximum_fusion.2), channel_id=1, source_target_pairs={{0,24},{1,25},{2,26},{3,27},{4,28},{5,29},{6,30},{7,31},{8,0},{9,1... | collective-permute-start | bytes 49160 | tf_op jit(solution)/shard_map/ppermute | solution.py:46
  77.3 4.0 %collective-permute-start.21 = (f32[4,8,128]{2,1,0:T(8,128)S(1)}, f32[4,8,128]{2,1,0:T(8,128)S(1)}, u32[]{:S(2)}, u32[]{:S(2)}) collective-permute-start(f32[4,8,128]{2,1,0:T(8,128)S(1)} %pad_maximum_fusion.2), channel_id=1, source_target_pairs={{0,8},{1,9},{2,10},{3,11},{4,12},{5,13},{6,14},{7,15},{8,16},{9,17... | collective-permute-start | bytes 49160 | tf_op jit(solution)/shard_map/ppermute | solution.py:46
  77.3 4.1 %collective-permute-start.20 = (f32[4,8,128]{2,1,0:T(8,128)S(1)}, f32[4,8,128]{2,1,0:T(8,128)S(1)}, u32[]{:S(2)}, u32[]{:S(2)}) collective-permute-start(f32[4,8,128]{2,1,0:T(8,128)S(1)} %pad_maximum_fusion.2), channel_id=1, source_target_pairs={{0,16},{1,17},{2,18},{3,19},{4,20},{5,21},{6,22},{7,23},{8,24},{9,... | collective-permute-start | bytes 49160 | tf_op jit(solution)/shard_map/ppermute | solution.py:46
  81.4 1.3 %collective-permute-start.24 = (f32[4,4,128]{2,1,0:T(4,128)S(1)}, f32[4,4,128]{2,1,0:T(4,128)S(1)}, u32[]{:S(2)}, u32[]{:S(2)}) collective-permute-start(f32[4,4,128]{2,1,0:T(4,128)S(1)} %exponential_multiply_fusion.refs_0_), channel_id=1, source_target_pairs={{0,32},{1,33},{2,34},{3,35},{4,36},{5,37},{6,38},{7,39},{8,40},{9,... | collective-permute-start | bytes 24584 | tf_op jit(solution)/shard_map/core/ppermute | solution.py:42

commit v4 on v3

v4 whole, which is shorter than its diff:
```python
import functools
import math

import jax
import jax.numpy as jnp
from jax import lax
from jax.experimental import pallas as pl
from jax.experimental.pallas import tpu as pltpu
from jax.sharding import PartitionSpec as P

AXES = ("blk", "shard")
SIDE = 4
LANES = 128


def place_of(device):
    blk, shard = divmod(device, 32)
    return {"x": (shard & 1) * 2 + (blk >> 1), "y": (shard >> 1) & 3, "z": shard >> 3, "c": blk & 1}


def device_at(x, y, z, c):
    return ((x & 1) * 2 + c) * 32 + z * 8 + y * 2 + (x >> 1)


def along(axis0, axis1, by):
    pairs = []
    for device in range(128):
        place = place_of(device)
        axis = axis1 if place["c"] else axis0
        place[axis] = (place[axis] + by) % SIDE
        pairs.append((device, device_at(**place)))
    return pairs


def to_core(value):
    pairs = []
    for device in range(128):
        place = place_of(device)
        place["c"] = 1 - place["c"]
        pairs.append((device, device_at(**place)))
    return lax.ppermute(value, AXES, pairs)


def shift(value, axes, by):
    return lax.ppermute(value, AXES, along(*axes, by))


COST = 1
SWAPS = ((), (0, 1), (2, 3))
SLOTS = 3
SPLIT = 2
STEPS = (0, 1, -1, 2)
TURN = (0, 1, 3, 2)
ORDERS = (("x", "z"), ("y", "x"), ("z", "y"))


def spread(value, axes, here):
    out = jnp.zeros((SIDE,) + value.shape, value.dtype)
    out = lax.dynamic_update_index_in_dim(out, value, here, 0)
    for by in (2, 1, -1):
        got = shift(value, axes, by)
        out = lax.dynamic_update_index_in_dim(out, got, (here - by) % SIDE, 0)
    return out.reshape((SIDE * value.shape[0],) + value.shape[1:])


def places():
    blk, shard = lax.axis_index("blk"), lax.axis_index("shard")
    at = {"x": (shard & 1) * 2 + (blk >> 1), "y": (shard >> 1) & 3, "z": shard >> 3}
    return blk & 1, [[at[axes[kind]] for axes in ORDERS] for kind in range(2)]


def sources(place):
    return [(place[2] - by) & 3 for by in STEPS], [(place[1] + by) & 3 for by in TURN]


def in_vmem(value):
    return pltpu.with_memory_space_constraint(value, pltpu.VMEM)


def in_hbm(value):
    return pltpu.with_memory_space_constraint(value, pltpu.HBM)


def score_kernel(scale, units, rows_a, rows_b, cent_a, cent_b, bias_a, bias_b, before_ref, *refs):
    ours_ref, sent_ref, stat_ref, staged, part_sems, row_sems = refs
    cent, width = cent_a.shape
    size = rows_a.shape[0]
    core, place = places()
    lasts, mids = zip(*[sources(p) for p in place])
    lane = lax.broadcasted_iota(jnp.int32, (LANES, LANES), 1)
    copies = []
    for u, rows_ref in enumerate((rows_a, rows_b)):
        copy = pltpu.make_async_copy(
            rows_ref, sent_ref.at[u, :, pl.ds(cent, width)], row_sems.at[u]
        )
        copy.start()
        copies.append(copy)
    stat_ref[...] = before_ref[...]
    for u, rows_ref in enumerate((rows_a, rows_b)):
        piece, half = units[u]
        last = jnp.where(core == 0, lasts[0][piece], lasts[1][piece])
        scores = [
            lax.dot_general(
                rows_ref[...],
                cent_ref[...],
                (((1,), (1,)), ((), ())),
                preferred_element_type=jnp.float32,
            )
            * scale
            - bias_ref[...]
            for cent_ref, bias_ref in ((cent_a, bias_a), (cent_b, bias_b))
        ]
        for t in range(size // LANES):
            cut = slice(t * LANES, (t + 1) * LANES)
            top = jnp.max(jnp.maximum(scores[0][cut], scores[1][cut]), axis=1, keepdims=True)
            powers = [jnp.exp(score[cut] - top) for score in scores]
            for c, power in enumerate(powers):
                staged[c, u, cut, :] = power.astype(jnp.bfloat16)
            total = jnp.sum(powers[0] + powers[1], axis=1, keepdims=True)
            flat = jnp.where(lane == 0, top, total).T
            turn = half * (size // LANES) + t
            row = jnp.where(core == 0, mids[0][turn], mids[1][turn])
            stat_ref[last, pl.ds(row, 1), :] = flat[0:1, :]
            stat_ref[last, pl.ds(SIDE + row, 1), :] = flat[1:2, :]
        for c, there in enumerate((ours_ref.at[u], sent_ref.at[u, :, pl.ds(0, cent)])):
            copy = pltpu.make_async_copy(staged.at[c, u], there, part_sems.at[c, u])
            copy.start()
            copies.append(copy)
    for copy in copies:
        copy.wait()


def score_rows(units, rows, cents, biases, local, scale):
    size, width = rows[0].shape
    cent = cents[0].shape[0]
    hbm = pl.BlockSpec(memory_space=pl.ANY)
    vmem = pl.BlockSpec(memory_space=pltpu.VMEM)
    return pl.pallas_call(
        functools.partial(score_kernel, scale, units),
        out_shape=(
            pltpu.HBM((2, size, cent), jnp.bfloat16),
            pltpu.HBM((2, size, cent + width), jnp.bfloat16),
            jax.ShapeDtypeStruct(local.shape, jnp.float32),
        ),
        in_specs=[vmem] * 7,
        out_specs=(hbm, hbm, vmem),
        scratch_shapes=[
            pltpu.VMEM((2, 2, size, cent), jnp.bfloat16),
            pltpu.SemaphoreType.DMA((2, 2)),
            pltpu.SemaphoreType.DMA((2,)),
        ],
        compiler_params=pltpu.CompilerParams(vmem_limit_bytes=14 * 2**20),
        cost_estimate=pl.CostEstimate(
            flops=int(COST * 8 * size * width * cent),
            bytes_accessed=int(COST * (4 * width * (size + cent) + 8 * size * cent)),
            transcendentals=int(COST * 4 * size * cent),
        ),
        name="scores",
    )(*[in_vmem(v) for v in (*rows, *cents, *biases)], local)


def weight_kernel(spots, total_rows, *refs):
    pieces = 2 * SIDE
    calls = len(spots) // 2
    factors, refs = refs[:2], refs[2:]
    ours, sent, got, refs = refs[:calls], refs[calls : 2 * calls], refs[2 * calls : 3 * calls], refs[3 * calls :]
    out_ref, sums_ref, loads_ref, parts, blocks, staged, rounded, sems, part_sems, block_sems = refs
    tiles = SIDE
    cent = sums_ref.shape[0]
    half = parts.shape[1] // 2

    def fetches(i):
        if i >= SIDE:
            return ()
        moves = []
        for h in range(2):
            call, u = spots[2 * i + h]
            there = pl.ds(h * half, half)
            moves += [
                pltpu.make_async_copy(ours[call].at[u], parts.at[i, there], part_sems.at[i, h]),
                pltpu.make_async_copy(
                    sent[call].at[u, :, pl.ds(cent, blocks.shape[2])],
                    blocks.at[i, there],
                    block_sems.at[i, h],
                ),
            ]
        return moves

    def part_of(i, t):
        if i < SIDE:
            return parts[i, t * LANES : (t + 1) * LANES, :]
        call, u = spots[2 * (i - SIDE) + t * LANES // half]
        start = t * LANES % half
        return got[call][u, start : start + LANES, :cent]

    def block_of(i, cols):
        if i < SIDE:
            return blocks[i, :, cols]
        halves = [spots[2 * (i - SIDE) + h] for h in range(2)]
        there = slice(cent + cols.start, cent + cols.stop)
        return jnp.concatenate([got[call][u, :, there] for call, u in halves])

    for i in range(SIDE):
        for copy in fetches(i):
            copy.start()

    here, place = places()
    found = [sources(p) for p in place]

    def body(core):
        def sends(i):
            slot = i % SLOTS
            kind = core if i < SIDE else 1 - core
            last = found[kind][0][i % SIDE]
            for x_lo in range(2):
                for j in range(2):
                    if kind == 0:
                        there = out_ref.at[x_lo, 0, j, last]
                    else:
                        there = out_ref.at[x_lo, 1, j, :, last]
                    yield pltpu.make_async_copy(staged.at[slot, x_lo, j], there, sems.at[slot])

        def add_sums(i, part):
            width = blocks.shape[2] // SPLIT
            cols = slice(part * width, (part + 1) * width)
            part_sums = lax.dot_general(
                rounded[i % 2],
                block_of(i, cols),
                (((0,), (0,)), ((), ())),
                preferred_element_type=jnp.float32,
            )
            if i == 0:
                sums_ref[:, cols] = part_sums
            elif i + 1 < pieces:
                sums_ref[:, cols] += part_sums
            else:
                sums_ref[:, cols] = (sums_ref[:, cols] + part_sums) * (1.0 / math.sqrt(total_rows))

        def weigh(i, t):
            slot = i % SLOTS
            kind = core if i < SIDE else 1 - core
            mid = found[kind][1][t]
            part = slice(t * LANES, (t + 1) * LANES)
            row = factors[i // SIDE][found[kind][0][i % SIDE], pl.ds(mid, 1), :]
            column = jnp.broadcast_to(row, (LANES, LANES)).T
            column = jnp.concatenate([column] * (cent // LANES), axis=1)
            weight = part_of(i, t).astype(jnp.float32) * column
            for p in range(SIDE):
                for j in range(2):
                    chunk = weight[(p * 2 + j) * 16 : (p * 2 + j) * 16 + 16]
                    if kind == 0:
                        staged[slot, p % 2, j, mid, p // 2] = chunk
                    else:
                        staged[slot, mid & 1, j, p, mid >> 1] = chunk
            rounded[i % 2, part, :] = weight.astype(jnp.bfloat16)
            return jnp.sum(weight.reshape(LANES // 8, 8, cent), axis=0)

        load = jnp.zeros((8, cent), jnp.float32)
        for i in range(pieces):
            if i >= SLOTS:
                for copy in sends(i - SLOTS):
                    copy.wait()
            for copy in fetches(i):
                copy.wait()
            for t in range(tiles):
                load = load + weigh(i, t)
                if i and (t + 1) % (tiles // SPLIT) == 0:
                    add_sums(i - 1, t // (tiles // SPLIT))
            for copy in sends(i):
                copy.start()
        for part in range(SPLIT):
            add_sums(pieces - 1, part)
        loads_ref[...] = jnp.sum(load, axis=0, keepdims=True) * (1.0 / total_rows)
        for i in range(pieces - SLOTS, pieces):
            for copy in sends(i):
                copy.wait()

    for core in range(2):

        @pl.when(here == core)
        def _(core=core):
            body(core)


def weight_all(factors, ours, sent, got, spots, total_rows):
    _, size, cent = ours[0].shape
    height = 2 * size
    width = sent[0].shape[2] - cent
    vmem = pl.BlockSpec(memory_space=pltpu.VMEM)
    hbm = pl.BlockSpec(memory_space=pl.ANY)
    return pl.pallas_call(
        functools.partial(weight_kernel, spots, float(total_rows)),
        out_shape=(
            jax.ShapeDtypeStruct((2, 2, 2, 4, 4, 2, 16, cent), jnp.float32),
            jax.ShapeDtypeStruct((cent, width), jnp.float32),
            jax.ShapeDtypeStruct((1, cent), jnp.float32),
        ),
        in_specs=[vmem] * 2
        + [hbm] * (len(ours) + len(sent))
        + [vmem] * len(got),
        out_specs=(hbm, vmem, vmem),
        scratch_shapes=[
            pltpu.VMEM((SIDE, height, cent), jnp.bfloat16),
            pltpu.VMEM((SIDE, height, width), jnp.bfloat16),
            pltpu.VMEM((SLOTS, 2, 2, 4, 2, 16, cent), jnp.float32),
            pltpu.VMEM((2, height, cent), jnp.bfloat16),
            pltpu.SemaphoreType.DMA((SLOTS,)),
            pltpu.SemaphoreType.DMA((SIDE, 2)),
            pltpu.SemaphoreType.DMA((SIDE, 2)),
        ],
        compiler_params=pltpu.CompilerParams(vmem_limit_bytes=20 * 2**20),
        name="weights",
    )(*factors, *[in_hbm(v) for v in (*ours, *sent)], *[in_vmem(v) for v in got])


def merged(stats):
    half = stats[0].shape[1] // 2
    tops = [s[:, :half] for s in stats]
    top = functools.reduce(jnp.maximum, tops)
    total = sum(s[:, half:] * jnp.exp(t - top) for s, t in zip(stats, tops))
    return jnp.concatenate([top, total], axis=1)


def per_device(embeddings, centroids, prices):
    core, place = places()
    first_place = jnp.where(core == 0, place[0][0], place[1][0])
    width = embeddings.shape[2]
    cent = centroids.shape[0]
    scale = 1.0 / math.sqrt(width)
    bias = (prices.astype(jnp.float32) / 1024.0).reshape(1, cent)
    with jax.named_scope("core"):
        cents, biases = (centroids, to_core(centroids)), (bias, to_core(bias))
    total_cent = cent * 128
    total_rows = embeddings.shape[0] * embeddings.shape[1] * 128

    first = spread(embeddings.reshape(-1, width), ORDERS[0], first_place)
    first, cents, biases = lax.optimization_barrier((first, cents, biases))
    with jax.named_scope("mid"):
        mids = [first] + [shift(first, ORDERS[1], -by if by < 3 else 1) for by in TURN[1:]]
    own_a, own_b = jnp.concatenate(mids[:2]), jnp.concatenate(mids[2:])
    axes = ORDERS[2]
    local = jnp.zeros((SIDE, 2 * SIDE, LANES), jnp.float32)
    ours, theirs, got, spots = [], [], [], {}

    def score(units, rows, local):
        our, their, local = score_rows(units, rows, cents, biases, local, scale)
        for u, unit in enumerate(units):
            spots[unit] = len(ours), u
        ours.append(our)
        theirs.append(their)
        return local

    with jax.named_scope("last"):
        before_a, after_b = shift(own_a, axes, 1), shift(own_b, axes, -1)
        before_b, after_a = shift(own_b, axes, 1), shift(own_a, axes, -1)
    with jax.named_scope("across"):
        across_a, across_b = shift(before_a, axes, 1), shift(after_b, axes, -1)
    local = score(((0, 0), (0, 1)), (own_a, own_b), local)
    local = score(((1, 0), (2, 1)), (before_a, after_b), local)
    before_b, after_a, local = lax.optimization_barrier((before_b, after_a, local))
    local = score(((1, 1), (2, 0)), (before_b, after_a), local)
    across_a, across_b, local = lax.optimization_barrier((across_a, across_b, local))
    local = score(((3, 0), (3, 1)), (across_a, across_b), local)
    spots = [spots[i, h] for i in range(SIDE) for h in range(2)]
    stats = local
    for axes, calls in zip(ORDERS, SWAPS):
        with jax.named_scope("core"):
            new = [to_core(theirs[c]) for c in calls]
        stats = merged([stats] + [shift(stats, axes, by) for by in (2, 1, -1)])
        stats, theirs, new = lax.optimization_barrier((stats, theirs, new))
        got += new
    factor = total_cent * jnp.exp(local[:, :SIDE] - (stats[:, :SIDE] + jnp.log(stats[:, SIDE:])))
    with jax.named_scope("core"):
        factors = factor, to_core(factor)
    out, sums, loads = weight_all(factors, ours, theirs, got, spots, total_rows)
    return out.reshape(8, 512, cent), sums, loads.reshape(cent)


def solution(mesh):
    placed = (P("blk", "shard", None), P(AXES, None), P(AXES))
    return jax.shard_map(
        per_device,
        mesh=mesh,
        in_specs=placed,
        out_specs=(P(None, None, AXES), P(AXES, None), P(AXES)),
        check_vma=False,
    )
```

time: 92.6 us -> 87.4 us (0.944)
  waiting for transfers between devices: 25.9 us -> 22.8 us
  Pallas kernels: 22.3 us -> 20.4 us
  local copies, waits for them, and re-layouts: 2.25 us -> 0.99 us
    ppermute x19 -> x21, starting transfers between devices: 27.1 us -> 29.1 us  [shift(): return lax.ppermute(value, AXES, along(*axes, by))]
    ppermute x19 -> x21, waiting for transfers between devices: 23.8 us -> 22 us  [shift(): return lax.ppermute(value, AXES, along(*axes, by))]
    pallas_call x3 -> x4, Pallas kernels: 12.9 us -> 11.1 us  [score_rows(): pl.pallas_call(functools.partial(score_kernel, scale, units), out_shape=(...]
    ppermute x6 -> x7, starting transfers between devices: 13.5 us -> 12 us  [to_core(): return lax.ppermute(value, AXES, pairs)]
    ppermute x6 -> x7, waiting for transfers between devices: 2.04 us -> 0.84 us  [to_core(): return lax.ppermute(value, AXES, pairs)]
    unnamed x10 -> x8, local copies, waits for them, and re-layouts: 1.24 us -> 0.05 us
  transfers between devices with their start and end apart: 25 -> 28, of which waited for: 18 -> 13; matrix products, arithmetic and copies ran while one was open for 1% -> 2% of each run, Pallas kernels for 10% -> 10%
where the time goes in v4:
time: 87.4 us; the launch traced here: 87.2 us
  starting transfers between devices  41.1 us (47%)
  waiting for transfers between devices  22.8 us (26%)
  Pallas kernels  20.4 us (23%)
  between operations  1.07 us (1%)
  local copies, waits for them, and re-layouts  0.99 us (1%)
    ppermute x21, starting transfers between devices, shift(): return lax.ppermute(value, AXES, along(*axes, by))  29.1 us
    ppermute x21, waiting for transfers between devices, shift(): return lax.ppermute(value, AXES, along(*axes, by))  22 us
    ppermute x7, starting transfers between devices, to_core(): return lax.ppermute(value, AXES, pairs)  12 us
    pallas_call x4, Pallas kernels, score_rows(): pl.pallas_call(functools.partial(score_kernel, scale, units), out_shape=(...  11.1 us
    pallas_call x1, Pallas kernels, weight_all(): pl.pallas_call(functools.partial(weight_kernel, spots, float(total_rows))...  9.3 us
  transfers between devices with their start and end apart: 28, of which 13 were waited for; matrix products, arithmetic and copies ran while one was open for 2% of the time, Pallas kernels for 10%

profile of v4, /device:TPU:1, one launch (start us, length us, event | category | flops | bytes accessed | tf_op | source)
XLA Modules:
  0.0 87.2 jit_solution(2128598969319297347)
XLA Ops:
  0.6 1.5 %collective-permute-start.3 = (bf16[512,1024]{1,0:T(8,128)(2,1)}, bf16[512,1024]{1,0:T(8,128)(2,1)S(1)}, u32[]{:S(2)}, u32[]{:S(2)}) collective-permute-start(bf16[512,1024]{1,0:T(8,128)(2,1)} %cent_a.3), channel_id=1, source_target_pairs={{0,32},{1,33},{2,34},{3,35},{4,36},{5,37},{6,38},{7,39},{8,40},{9,... | collective-permute-start | bytes 3145736 | tf_op jit(solution)/shard_map/core/ppermute | solution.py:41
  2.1 3.8 %collective-permute-start.2 = (bf16[32,1024]{1,0:T(8,128)(2,1)}, bf16[32,1024]{1,0:T(8,128)(2,1)S(1)}, u32[]{:S(2)}, u32[]{:S(2)}) collective-permute-start(bf16[32,1024]{1,0:T(8,128)(2,1)} %bitcast.23), channel_id=1, source_target_pairs={{0,65},{1,64},{2,67},{3,66},{4,69},{5,68},{6,71},{7,70},{8,73},{9,... | collective-permute-start | bytes 196616 | tf_op jit(solution)/shard_map/ppermute | solution.py:45
  6.0 1.3 %collective-permute-start = (bf16[32,1024]{1,0:T(8,128)(2,1)}, bf16[32,1024]{1,0:T(8,128)(2,1)S(1)}, u32[]{:S(2)}, u32[]{:S(2)}) collective-permute-start(bf16[32,1024]{1,0:T(8,128)(2,1)} %bitcast.25), channel_id=1, source_target_pairs={{0,1},{1,0},{2,3},{3,2},{4,5},{5,4},{6,7},{7,6},{8,9},{9,8},{10,11... | collective-permute-start | bytes 196616 | tf_op jit(solution)/shard_map/ppermute | solution.py:45
  7.3 0.7 convert_multiply_fusion
  8.0 0.1 collective-permute-start.4
  8.1 0.9 bitcast_dynamic-update-slice_fusion.3
  8.9 2.0 %collective-permute-done = bf16[32,1024]{1,0:T(8,128)(2,1)S(1)} collective-permute-done((bf16[32,1024]{1,0:T(8,128)(2,1)}, bf16[32,1024]{1,0:T(8,128)(2,1)S(1)}, u32[]{:S(2)}, u32[]{:S(2)}) %collective-permute-start) | collective-permute-done | bytes 65568 | tf_op jit(solution)/shard_map/ppermute | solution.py:45
  10.9 0.3 collective-permute-done.1
  11.3 2.5 %collective-permute-start.5 = (bf16[128,1024]{1,0:T(8,128)(2,1)S(1)}, bf16[128,1024]{1,0:T(8,128)(2,1)S(1)}, u32[]{:S(2)}, u32[]{:S(2)}) collective-permute-start(bf16[128,1024]{1,0:T(8,128)(2,1)S(1)} %bitcast.19), channel_id=1, source_target_pairs={{0,6},{1,7},{2,0},{3,1},{4,2},{5,3},{6,4},{7,5},{8,14},{9,15},{10,... | collective-permute-start | bytes 786440 | tf_op jit(solution)/shard_map/mid/ppermute | solution.py:45
  13.8 1.7 %collective-permute-start.9 = (bf16[128,1024]{1,0:T(8,128)(2,1)S(1)}, bf16[128,1024]{1,0:T(8,128)(2,1)S(1)}, u32[]{:S(2)}, u32[]{:S(2)}) collective-permute-start(bf16[128,1024]{1,0:T(8,128)(2,1)S(1)} %bitcast.21), channel_id=1, source_target_pairs={{0,4},{1,5},{2,6},{3,7},{4,0},{5,1},{6,2},{7,3},{8,12},{9,13},{10,... | collective-permute-start | bytes 786440 | tf_op jit(solution)/shard_map/mid/ppermute | solution.py:45
  15.6 1.6 %collective-permute-done.5 = bf16[128,1024]{1,0:T(8,128)(2,1)S(1)} collective-permute-done((bf16[128,1024]{1,0:T(8,128)(2,1)S(1)}, bf16[128,1024]{1,0:T(8,128)(2,1)S(1)}, u32[]{:S(2)}, u32[]{:S(2)}) %collective-permute-start.5) | collective-permute-done | bytes 262176 | tf_op jit(solution)/shard_map/mid/ppermute | solution.py:45
  17.2 1.4 %collective-permute-start.6 = (bf16[256,1024]{1,0:T(8,128)(2,1)S(1)}, bf16[256,1024]{1,0:T(8,128)(2,1)S(1)}, u32[]{:S(2)}, u32[]{:S(2)}) collective-permute-start(bf16[256,1024]{1,0:T(8,128)(2,1)S(1)} %constant_dynamic-update-slice_fusion.rows_a), channel_id=1, source_target_pairs={{0,8},{1,9},{2,10},{3,11},{4,12},{5,13},{6,14},{7,15},{8,16},{9,17... | collective-permute-start | bytes 1572872 | tf_op jit(solution)/shard_map/last/ppermute | solution.py:45
  18.5 4.8 %collective-permute-done.8 = bf16[128,1024]{1,0:T(8,128)(2,1)S(1)} collective-permute-done((bf16[128,1024]{1,0:T(8,128)(2,1)S(1)}, bf16[128,1024]{1,0:T(8,128)(2,1)S(1)}, u32[]{:S(2)}, u32[]{:S(2)}) %collective-permute-start.8) | collective-permute-done | bytes 262176 | tf_op jit(solution)/shard_map/mid/ppermute | solution.py:45
  23.4 0.0 collective-permute-done.9
  23.4 2.5 %collective-permute-start.10 = (bf16[256,1024]{1,0:T(8,128)(2,1)S(1)}, bf16[256,1024]{1,0:T(8,128)(2,1)S(1)}, u32[]{:S(2)}, u32[]{:S(2)}) collective-permute-start(bf16[256,1024]{1,0:T(8,128)(2,1)S(1)} %constant_dynamic-update-slice_fusion.2.rows_b), channel_id=1, source_target_pairs={{0,24},{1,25},{2,26},{3,27},{4,28},{5,29},{6,30},{7,31},{8,0},{9,1... | collective-permute-start | bytes 1572872 | tf_op jit(solution)/shard_map/last/ppermute | solution.py:45
  25.9 0.8 collective-permute-start.13
  26.7 0.7 collective-permute-start.12
  27.4 2.5 %collective-permute-done.6.rows_a = bf16[256,1024]{1,0:T(8,128)(2,1)S(1)} collective-permute-done((bf16[256,1024]{1,0:T(8,128)(2,1)S(1)}, bf16[256,1024]{1,0:T(8,128)(2,1)S(1)}, u32[]{:S(2)}, u32[]{:S(2)}) %collective-permute-start.6) | collective-permute-done | bytes 524320 | tf_op jit(solution)/shard_map/last/ppermute | solution.py:45
  29.9 0.0 collective-permute-start.7
  29.9 2.1 %collective-permute-done.10.rows_b = bf16[256,1024]{1,0:T(8,128)(2,1)S(1)} collective-permute-done((bf16[256,1024]{1,0:T(8,128)(2,1)S(1)}, bf16[256,1024]{1,0:T(8,128)(2,1)S(1)}, u32[]{:S(2)}, u32[]{:S(2)}) %collective-permute-start.10) | collective-permute-done | bytes 524320 | tf_op jit(solution)/shard_map/last/ppermute | solution.py:45
  32.1 3.4 %collective-permute-start.11 = (bf16[256,1024]{1,0:T(8,128)(2,1)S(1)}, bf16[256,1024]{1,0:T(8,128)(2,1)S(1)}, u32[]{:S(2)}, u32[]{:S(2)}) collective-permute-start(bf16[256,1024]{1,0:T(8,128)(2,1)S(1)} %collective-permute-done.10.rows_b), channel_id=1, source_target_pairs={{0,24},{1,25},{2,26},{3,27},{4,28},{5,29},{6,30},{7,31},{8,0},{9,1... | collective-permute-start | bytes 1572872 | tf_op jit(solution)/shard_map/across/ppermute | solution.py:45
  35.5 2.7 %scores.4 = (bf16[2,256,512]{2,1,0:T(8,128)(2,1)}, bf16[2,256,1536]{2,1,0:T(8,128)(2,1)}, f32[4,8,128]{2,1,0:T(8,128)S(1)}) custom-call(bf16[256,1024]{1,0:T(8,128)(2,1)S(1)} %constant_dynamic-update-slice_fusion.rows_a, bf16[256,1024]{1,0:T(8,128)(2,1)S(1)} %constant_dynamic-update-slice_fusion.2.rows_b, bf16[512,1024]{1,0:T(8,128)(2,1)S(1)} %copy-done, ...), custom_call_target="tpu_custom_call" | custom-call | flops 1073741824 | bytes 4194304 | tf_op jit(solution)/shard_map/scores/pallas_call | solution.py:138
  38.2 2.7 %scores.5 = (bf16[2,256,512]{2,1,0:T(8,128)(2,1)}, bf16[2,256,1536]{2,1,0:T(8,128)(2,1)}, f32[4,8,128]{2,1,0:T(8,128)S(1)}) custom-call(bf16[256,1024]{1,0:T(8,128)(2,1)S(1)} %collective-permute-done.6.rows_a, bf16[256,1024]{1,0:T(8,128)(2,1)S(1)} %collective-permute-done.10.rows_b, bf16[512,1024]{1,0:T(8,128)(2,1)S(1)} %copy-done, ...), custom_call_target="tpu_custom_call" | custom-call | flops 1073741824 | bytes 4194304 | tf_op jit(solution)/shard_map/scores/pallas_call | solution.py:138
  41.0 0.0 collective-permute-done.13.rows_b
  41.0 2.9 %scores.6 = (bf16[2,256,512]{2,1,0:T(8,128)(2,1)}, bf16[2,256,1536]{2,1,0:T(8,128)(2,1)}, f32[4,8,128]{2,1,0:T(8,128)S(1)}) custom-call(bf16[256,1024]{1,0:T(8,128)(2,1)S(1)} %collective-permute-done.12.rows_a, bf16[256,1024]{1,0:T(8,128)(2,1)S(1)} %collective-permute-done.13.rows_b, bf16[512,1024]{1,0:T(8,128)(2,1)S(1)} %copy-done, ...), custom_call_target="tpu_custom_call" | custom-call | flops 1073741824 | bytes 4194304 | tf_op jit(solution)/shard_map/scores/pallas_call | solution.py:138
  43.9 0.0 collective-permute-done.11.rows_b
  43.9 2.8 %scores.7 = (bf16[2,256,512]{2,1,0:T(8,128)(2,1)}, bf16[2,256,1536]{2,1,0:T(8,128)(2,1)}, f32[4,8,128]{2,1,0:T(8,128)S(1)}) custom-call(bf16[256,1024]{1,0:T(8,128)(2,1)S(1)} %collective-permute-done.7.rows_a, bf16[256,1024]{1,0:T(8,128)(2,1)S(1)} %collective-permute-done.11.rows_b, bf16[512,1024]{1,0:T(8,128)(2,1)S(1)} %copy-done, ...), custom_call_target="tpu_custom_call" | custom-call | flops 1073741824 | bytes 4194304 | tf_op jit(solution)/shard_map/scores/pallas_call | solution.py:138
  46.7 2.7 %collective-permute-start.16 = (f32[4,8,128]{2,1,0:T(8,128)S(1)}, f32[4,8,128]{2,1,0:T(8,128)S(1)}, u32[]{:S(2)}, u32[]{:S(2)}) collective-permute-start(f32[4,8,128]{2,1,0:T(8,128)S(1)} %get-tuple-element.62), channel_id=1, source_target_pairs={{0,65},{1,64},{2,67},{3,66},{4,69},{5,68},{6,71},{7,70},{8,73},{9,... | collective-permute-start | bytes 49160 | tf_op jit(solution)/shard_map/ppermute | solution.py:45
  49.3 0.0 collective-permute-start.15
  49.3 1.3 %collective-permute-start.14 = (f32[4,8,128]{2,1,0:T(8,128)S(1)}, f32[4,8,128]{2,1,0:T(8,128)S(1)}, u32[]{:S(2)}, u32[]{:S(2)}) collective-permute-start(f32[4,8,128]{2,1,0:T(8,128)S(1)} %get-tuple-element.62), channel_id=1, source_target_pairs={{0,1},{1,0},{2,3},{3,2},{4,5},{5,4},{6,7},{7,6},{8,9},{9,8},{10,11... | collective-permute-start | bytes 49160 | tf_op jit(solution)/shard_map/ppermute | solution.py:45
  50.6 2.5 %collective-permute-done.15 = f32[4,8,128]{2,1,0:T(8,128)S(1)} collective-permute-done((f32[4,8,128]{2,1,0:T(8,128)S(1)}, f32[4,8,128]{2,1,0:T(8,128)S(1)}, u32[]{:S(2)}, u32[]{:S(2)}) %collective-permute-start.15) | collective-permute-done | bytes 16416 | tf_op jit(solution)/shard_map/ppermute | solution.py:45
  53.1 0.3 collective-permute-done.14
  53.5 6.8 %collective-permute-start.20 = (bf16[2,256,1536]{2,1,0:T(8,128)(2,1)S(1)}, bf16[2,256,1536]{2,1,0:T(8,128)(2,1)S(1)}, u32[]{:S(2)}, u32[]{:S(2)}) collective-permute-start(bf16[2,256,1536]{2,1,0:T(8,128)(2,1)S(1)} %copy-done.1), channel_id=1, source_target_pairs={{0,32},{1,33},{2,34},{3,35},{4,36},{5,37},{6,38},{7,39},{8,40},{9,... | collective-permute-start | bytes 4718600 | tf_op jit(solution)/shard_map/core/ppermute | solution.py:41
  60.3 0.1 collective-permute-start.21
  60.4 2.9 %collective-permute-start.19 = (f32[4,8,128]{2,1,0:T(8,128)S(1)}, f32[4,8,128]{2,1,0:T(8,128)S(1)}, u32[]{:S(2)}, u32[]{:S(2)}) collective-permute-start(f32[4,8,128]{2,1,0:T(8,128)S(1)} %pad_maximum_fusion), channel_id=1, source_target_pairs={{0,6},{1,7},{2,0},{3,1},{4,2},{5,3},{6,4},{7,5},{8,14},{9,15},{10,... | collective-permute-start | bytes 49160 | tf_op jit(solution)/shard_map/ppermute | solution.py:45
  63.2 1.2 %collective-permute-start.17 = (f32[4,8,128]{2,1,0:T(8,128)S(1)}, f32[4,8,128]{2,1,0:T(8,128)S(1)}, u32[]{:S(2)}, u32[]{:S(2)}) collective-permute-start(f32[4,8,128]{2,1,0:T(8,128)S(1)} %pad_maximum_fusion), channel_id=1, source_target_pairs={{0,4},{1,5},{2,6},{3,7},{4,0},{5,1},{6,2},{7,3},{8,12},{9,13},{10,... | collective-permute-start | bytes 49160 | tf_op jit(solution)/shard_map/ppermute | solution.py:45
  64.4 2.9 %collective-permute-done.18 = f32[4,8,128]{2,1,0:T(8,128)S(1)} collective-permute-done((f32[4,8,128]{2,1,0:T(8,128)S(1)}, f32[4,8,128]{2,1,0:T(8,128)S(1)}, u32[]{:S(2)}, u32[]{:S(2)}) %collective-permute-start.18) | collective-permute-done | bytes 16416 | tf_op jit(solution)/shard_map/ppermute | solution.py:45
  67.3 0.3 collective-permute-done.17
  67.7 0.5 collective-permute-start.25
  68.2 0.1 collective-permute-start.26
  68.3 1.0 %collective-permute-start.24 = (f32[4,8,128]{2,1,0:T(8,128)S(1)}, f32[4,8,128]{2,1,0:T(8,128)S(1)}, u32[]{:S(2)}, u32[]{:S(2)}) collective-permute-start(f32[4,8,128]{2,1,0:T(8,128)S(1)} %pad_maximum_fusion.1), channel_id=1, source_target_pairs={{0,24},{1,25},{2,26},{3,27},{4,28},{5,29},{6,30},{7,31},{8,0},{9,1... | collective-permute-start | bytes 49160 | tf_op jit(solution)/shard_map/ppermute | solution.py:45
  69.3 0.5 collective-permute-start.23
  69.8 1.5 %collective-permute-start.22 = (f32[4,8,128]{2,1,0:T(8,128)S(1)}, f32[4,8,128]{2,1,0:T(8,128)S(1)}, u32[]{:S(2)}, u32[]{:S(2)}) collective-permute-start(f32[4,8,128]{2,1,0:T(8,128)S(1)} %pad_maximum_fusion.1), channel_id=1, source_target_pairs={{0,16},{1,17},{2,18},{3,19},{4,20},{5,21},{6,22},{7,23},{8,24},{9,... | collective-permute-start | bytes 49160 | tf_op jit(solution)/shard_map/ppermute | solution.py:45
  71.3 1.8 %collective-permute-done.23 = f32[4,8,128]{2,1,0:T(8,128)S(1)} collective-permute-done((f32[4,8,128]{2,1,0:T(8,128)S(1)}, f32[4,8,128]{2,1,0:T(8,128)S(1)}, u32[]{:S(2)}, u32[]{:S(2)}) %collective-permute-start.23) | collective-permute-done | bytes 16416 | tf_op jit(solution)/shard_map/ppermute | solution.py:45
  73.1 0.8 collective-permute-done.22
  73.9 3.0 %collective-permute-start.27 = (f32[4,4,128]{2,1,0:T(4,128)S(1)}, f32[4,4,128]{2,1,0:T(4,128)S(1)}, u32[]{:S(2)}, u32[]{:S(2)}) collective-permute-start(f32[4,4,128]{2,1,0:T(4,128)S(1)} %exponential_multiply_fusion.refs_0_), channel_id=1, source_target_pairs={{0,32},{1,33},{2,34},{3,35},{4,36},{5,37},{6,38},{7,39},{8,40},{9,... | collective-permute-start | bytes 24584 | tf_op jit(solution)/shard_map/core/ppermute | solution.py:41
  76.9 0.8 collective-permute-done.27.refs_1_
  77.8 9.3 %weights.1 = (f32[2,2,2,4,4,2,16,512]{7,6,5,4,3,2,1,0:T(8,128)}, f32[512,1024]{1,0:T(8,128)}, f32[1,512]{1,0:T(1,128)}) custom-call(f32[4,4,128]{2,1,0:T(4,128)S(1)} %exponential_multiply_fusion.refs_0_, f32[4,4,128]{2,1,0:T(4,128)S(1)} %collective-permute-done.27.refs_1_, bf16[2,256,512]{2,1,0:T(8,128)(2,1)} %get-tuple-element.78.refs_2_, ...), custom_call_target="tpu_custom_call" | custom-call | tf_op jit(solution)/shard_map/weights/pallas_call | solution.py:291
  (37 shorter events, 0.3 us)
Async XLA Ops:
  0.6 34.9 %copy-start = (bf16[512,1024]{1,0:T(8,128)(2,1)S(1)}, bf16[512,1024]{1,0:T(8,128)(2,1)}, u32[]{:S(2)}) copy-start(bf16[512,1024]{1,0:T(8,128)(2,1)} %cent_a.3) | copy-start | bytes 3145732
  0.6 10.6 %collective-permute-start.3 = (bf16[512,1024]{1,0:T(8,128)(2,1)}, bf16[512,1024]{1,0:T(8,128)(2,1)S(1)}, u32[]{:S(2)}, u32[]{:S(2)}) collective-permute-start(bf16[512,1024]{1,0:T(8,128)(2,1)} %cent_a.3), channel_id=1, source_target_pairs={{0,32},{1,33},{2,34},{3,35},{4,36},{5,37},{6,38},{7,39},{8,40},{9,... | collective-permute-start | bytes 3145736 | tf_op jit(solution)/shard_map/core/ppermute | solution.py:41
  2.1 9.1 %collective-permute-start.2 = (bf16[32,1024]{1,0:T(8,128)(2,1)}, bf16[32,1024]{1,0:T(8,128)(2,1)S(1)}, u32[]{:S(2)}, u32[]{:S(2)}) collective-permute-start(bf16[32,1024]{1,0:T(8,128)(2,1)} %bitcast.23), channel_id=1, source_target_pairs={{0,65},{1,64},{2,67},{3,66},{4,69},{5,68},{6,71},{7,70},{8,73},{9,... | collective-permute-start | bytes 196616 | tf_op jit(solution)/shard_map/ppermute | solution.py:45
  6.0 5.2 %collective-permute-start.1 = (bf16[32,1024]{1,0:T(8,128)(2,1)}, bf16[32,1024]{1,0:T(8,128)(2,1)S(1)}, u32[]{:S(2)}, u32[]{:S(2)}) collective-permute-start(bf16[32,1024]{1,0:T(8,128)(2,1)} %bitcast.24), channel_id=1, source_target_pairs={{0,64},{1,65},{2,66},{3,67},{4,68},{5,69},{6,70},{7,71},{8,72},{9,... | collective-permute-start | bytes 196616 | tf_op jit(solution)/shard_map/ppermute | solution.py:45
  6.0 4.9 %collective-permute-start = (bf16[32,1024]{1,0:T(8,128)(2,1)}, bf16[32,1024]{1,0:T(8,128)(2,1)S(1)}, u32[]{:S(2)}, u32[]{:S(2)}) collective-permute-start(bf16[32,1024]{1,0:T(8,128)(2,1)} %bitcast.25), channel_id=1, source_target_pairs={{0,1},{1,0},{2,3},{3,2},{4,5},{5,4},{6,7},{7,6},{8,9},{9,8},{10,11... | collective-permute-start | bytes 196616 | tf_op jit(solution)/shard_map/ppermute | solution.py:45
  8.0 3.3 %collective-permute-start.4 = (f32[1,512]{1,0:T(1,128)S(1)}, f32[1,512]{1,0:T(1,128)S(1)}, u32[]{:S(2)}, u32[]{:S(2)}) collective-permute-start(f32[1,512]{1,0:T(1,128)S(1)} %bitcast.14), channel_id=1, source_target_pairs={{0,32},{1,33},{2,34},{3,35},{4,36},{5,37},{6,38},{7,39},{8,40},{9,... | collective-permute-start | bytes 6152 | tf_op jit(solution)/shard_map/core/ppermute | solution.py:41
  11.3 5.9 %collective-permute-start.5 = (bf16[128,1024]{1,0:T(8,128)(2,1)S(1)}, bf16[128,1024]{1,0:T(8,128)(2,1)S(1)}, u32[]{:S(2)}, u32[]{:S(2)}) collective-permute-start(bf16[128,1024]{1,0:T(8,128)(2,1)S(1)} %bitcast.19), channel_id=1, source_target_pairs={{0,6},{1,7},{2,0},{3,1},{4,2},{5,3},{6,4},{7,5},{8,14},{9,15},{10,... | collective-permute-start | bytes 786440 | tf_op jit(solution)/shard_map/mid/ppermute | solution.py:45
  13.8 9.5 %collective-permute-start.8 = (bf16[128,1024]{1,0:T(8,128)(2,1)S(1)}, bf16[128,1024]{1,0:T(8,128)(2,1)S(1)}, u32[]{:S(2)}, u32[]{:S(2)}) collective-permute-start(bf16[128,1024]{1,0:T(8,128)(2,1)S(1)} %bitcast.20), channel_id=1, source_target_pairs={{0,2},{1,3},{2,4},{3,5},{4,6},{5,7},{6,0},{7,1},{8,10},{9,11},{10,... | collective-permute-start | bytes 786440 | tf_op jit(solution)/shard_map/mid/ppermute | solution.py:45
  13.8 9.6 %collective-permute-start.9 = (bf16[128,1024]{1,0:T(8,128)(2,1)S(1)}, bf16[128,1024]{1,0:T(8,128)(2,1)S(1)}, u32[]{:S(2)}, u32[]{:S(2)}) collective-permute-start(bf16[128,1024]{1,0:T(8,128)(2,1)S(1)} %bitcast.21), channel_id=1, source_target_pairs={{0,4},{1,5},{2,6},{3,7},{4,0},{5,1},{6,2},{7,3},{8,12},{9,13},{10,... | collective-permute-start | bytes 786440 | tf_op jit(solution)/shard_map/mid/ppermute | solution.py:45
  17.2 12.7 %collective-permute-start.6 = (bf16[256,1024]{1,0:T(8,128)(2,1)S(1)}, bf16[256,1024]{1,0:T(8,128)(2,1)S(1)}, u32[]{:S(2)}, u32[]{:S(2)}) collective-permute-start(bf16[256,1024]{1,0:T(8,128)(2,1)S(1)} %constant_dynamic-update-slice_fusion.rows_a), channel_id=1, source_target_pairs={{0,8},{1,9},{2,10},{3,11},{4,12},{5,13},{6,14},{7,15},{8,16},{9,17... | collective-permute-start | bytes 1572872 | tf_op jit(solution)/shard_map/last/ppermute | solution.py:45
  23.4 8.6 %collective-permute-start.10 = (bf16[256,1024]{1,0:T(8,128)(2,1)S(1)}, bf16[256,1024]{1,0:T(8,128)(2,1)S(1)}, u32[]{:S(2)}, u32[]{:S(2)}) collective-permute-start(bf16[256,1024]{1,0:T(8,128)(2,1)S(1)} %constant_dynamic-update-slice_fusion.2.rows_b), channel_id=1, source_target_pairs={{0,24},{1,25},{2,26},{3,27},{4,28},{5,29},{6,30},{7,31},{8,0},{9,1... | collective-permute-start | bytes 1572872 | tf_op jit(solution)/shard_map/last/ppermute | solution.py:45
  25.9 15.0 %collective-permute-start.13 = (bf16[256,1024]{1,0:T(8,128)(2,1)S(1)}, bf16[256,1024]{1,0:T(8,128)(2,1)S(1)}, u32[]{:S(2)}, u32[]{:S(2)}) collective-permute-start(bf16[256,1024]{1,0:T(8,128)(2,1)S(1)} %constant_dynamic-update-slice_fusion.rows_a), channel_id=1, source_target_pairs={{0,24},{1,25},{2,26},{3,27},{4,28},{5,29},{6,30},{7,31},{8,0},{9,1... | collective-permute-start | bytes 1572872 | tf_op jit(solution)/shard_map/last/ppermute | solution.py:45
  26.7 14.3 %collective-permute-start.12 = (bf16[256,1024]{1,0:T(8,128)(2,1)S(1)}, bf16[256,1024]{1,0:T(8,128)(2,1)S(1)}, u32[]{:S(2)}, u32[]{:S(2)}) collective-permute-start(bf16[256,1024]{1,0:T(8,128)(2,1)S(1)} %constant_dynamic-update-slice_fusion.2.rows_b), channel_id=1, source_target_pairs={{0,8},{1,9},{2,10},{3,11},{4,12},{5,13},{6,14},{7,15},{8,16},{9,17... | collective-permute-start | bytes 1572872 | tf_op jit(solution)/shard_map/last/ppermute | solution.py:45
  29.9 13.9 %collective-permute-start.7 = (bf16[256,1024]{1,0:T(8,128)(2,1)S(1)}, bf16[256,1024]{1,0:T(8,128)(2,1)S(1)}, u32[]{:S(2)}, u32[]{:S(2)}) collective-permute-start(bf16[256,1024]{1,0:T(8,128)(2,1)S(1)} %collective-permute-done.6.rows_a), channel_id=1, source_target_pairs={{0,8},{1,9},{2,10},{3,11},{4,12},{5,13},{6,14},{7,15},{8,16},{9,17... | collective-permute-start | bytes 1572872 | tf_op jit(solution)/shard_map/across/ppermute | solution.py:45
  32.1 11.8 %collective-permute-start.11 = (bf16[256,1024]{1,0:T(8,128)(2,1)S(1)}, bf16[256,1024]{1,0:T(8,128)(2,1)S(1)}, u32[]{:S(2)}, u32[]{:S(2)}) collective-permute-start(bf16[256,1024]{1,0:T(8,128)(2,1)S(1)} %collective-permute-done.10.rows_b), channel_id=1, source_target_pairs={{0,24},{1,25},{2,26},{3,27},{4,28},{5,29},{6,30},{7,31},{8,0},{9,1... | collective-permute-start | bytes 1572872 | tf_op jit(solution)/shard_map/across/ppermute | solution.py:45
  43.9 9.6 %copy-start.1 = (bf16[2,256,1536]{2,1,0:T(8,128)(2,1)S(1)}, bf16[2,256,1536]{2,1,0:T(8,128)(2,1)}, u32[]{:S(2)}) copy-start(bf16[2,256,1536]{2,1,0:T(8,128)(2,1)} %get-tuple-element.82.refs_6_) | copy-start | bytes 4718596
  43.9 16.4 %copy-start.2 = (bf16[2,256,1536]{2,1,0:T(8,128)(2,1)S(1)}, bf16[2,256,1536]{2,1,0:T(8,128)(2,1)}, u32[]{:S(2)}) copy-start(bf16[2,256,1536]{2,1,0:T(8,128)(2,1)} %get-tuple-element.83.refs_7_) | copy-start | bytes 4718596
  46.7 3.9 %collective-permute-start.16 = (f32[4,8,128]{2,1,0:T(8,128)S(1)}, f32[4,8,128]{2,1,0:T(8,128)S(1)}, u32[]{:S(2)}, u32[]{:S(2)}) collective-permute-start(f32[4,8,128]{2,1,0:T(8,128)S(1)} %get-tuple-element.62), channel_id=1, source_target_pairs={{0,65},{1,64},{2,67},{3,66},{4,69},{5,68},{6,71},{7,70},{8,73},{9,... | collective-permute-start | bytes 49160 | tf_op jit(solution)/shard_map/ppermute | solution.py:45
  49.3 3.8 %collective-permute-start.15 = (f32[4,8,128]{2,1,0:T(8,128)S(1)}, f32[4,8,128]{2,1,0:T(8,128)S(1)}, u32[]{:S(2)}, u32[]{:S(2)}) collective-permute-start(f32[4,8,128]{2,1,0:T(8,128)S(1)} %get-tuple-element.62), channel_id=1, source_target_pairs={{0,64},{1,65},{2,66},{3,67},{4,68},{5,69},{6,70},{7,71},{8,72},{9,... | collective-permute-start | bytes 49160 | tf_op jit(solution)/shard_map/ppermute | solution.py:45
  49.3 4.1 %collective-permute-start.14 = (f32[4,8,128]{2,1,0:T(8,128)S(1)}, f32[4,8,128]{2,1,0:T(8,128)S(1)}, u32[]{:S(2)}, u32[]{:S(2)}) collective-permute-start(f32[4,8,128]{2,1,0:T(8,128)S(1)} %get-tuple-element.62), channel_id=1, source_target_pairs={{0,1},{1,0},{2,3},{3,2},{4,5},{5,4},{6,7},{7,6},{8,9},{9,8},{10,11... | collective-permute-start | bytes 49160 | tf_op jit(solution)/shard_map/ppermute | solution.py:45
  53.5 14.2 %collective-permute-start.20 = (bf16[2,256,1536]{2,1,0:T(8,128)(2,1)S(1)}, bf16[2,256,1536]{2,1,0:T(8,128)(2,1)S(1)}, u32[]{:S(2)}, u32[]{:S(2)}) collective-permute-start(bf16[2,256,1536]{2,1,0:T(8,128)(2,1)S(1)} %copy-done.1), channel_id=1, source_target_pairs={{0,32},{1,33},{2,34},{3,35},{4,36},{5,37},{6,38},{7,39},{8,40},{9,... | collective-permute-start | bytes 4718600 | tf_op jit(solution)/shard_map/core/ppermute | solution.py:41
  60.3 7.4 %collective-permute-start.21 = (bf16[2,256,1536]{2,1,0:T(8,128)(2,1)S(1)}, bf16[2,256,1536]{2,1,0:T(8,128)(2,1)S(1)}, u32[]{:S(2)}, u32[]{:S(2)}) collective-permute-start(bf16[2,256,1536]{2,1,0:T(8,128)(2,1)S(1)} %copy-done.2), channel_id=1, source_target_pairs={{0,32},{1,33},{2,34},{3,35},{4,36},{5,37},{6,38},{7,39},{8,40},{9,... | collective-permute-start | bytes 4718600 | tf_op jit(solution)/shard_map/core/ppermute | solution.py:41
  60.4 4.1 %collective-permute-start.19 = (f32[4,8,128]{2,1,0:T(8,128)S(1)}, f32[4,8,128]{2,1,0:T(8,128)S(1)}, u32[]{:S(2)}, u32[]{:S(2)}) collective-permute-start(f32[4,8,128]{2,1,0:T(8,128)S(1)} %pad_maximum_fusion), channel_id=1, source_target_pairs={{0,6},{1,7},{2,0},{3,1},{4,2},{5,3},{6,4},{7,5},{8,14},{9,15},{10,... | collective-permute-start | bytes 49160 | tf_op jit(solution)/shard_map/ppermute | solution.py:45
  63.2 4.1 %collective-permute-start.18 = (f32[4,8,128]{2,1,0:T(8,128)S(1)}, f32[4,8,128]{2,1,0:T(8,128)S(1)}, u32[]{:S(2)}, u32[]{:S(2)}) collective-permute-start(f32[4,8,128]{2,1,0:T(8,128)S(1)} %pad_maximum_fusion), channel_id=1, source_target_pairs={{0,2},{1,3},{2,4},{3,5},{4,6},{5,7},{6,0},{7,1},{8,10},{9,11},{10,... | collective-permute-start | bytes 49160 | tf_op jit(solution)/shard_map/ppermute | solution.py:45
  63.2 4.4 %collective-permute-start.17 = (f32[4,8,128]{2,1,0:T(8,128)S(1)}, f32[4,8,128]{2,1,0:T(8,128)S(1)}, u32[]{:S(2)}, u32[]{:S(2)}) collective-permute-start(f32[4,8,128]{2,1,0:T(8,128)S(1)} %pad_maximum_fusion), channel_id=1, source_target_pairs={{0,4},{1,5},{2,6},{3,7},{4,0},{5,1},{6,2},{7,3},{8,12},{9,13},{10,... | collective-permute-start | bytes 49160 | tf_op jit(solution)/shard_map/ppermute | solution.py:45
  67.7 6.2 %collective-permute-start.25 = (bf16[2,256,1536]{2,1,0:T(8,128)(2,1)}, bf16[2,256,1536]{2,1,0:T(8,128)(2,1)S(1)}, u32[]{:S(2)}, u32[]{:S(2)}) collective-permute-start(bf16[2,256,1536]{2,1,0:T(8,128)(2,1)} %get-tuple-element.84.refs_8_), channel_id=1, source_target_pairs={{0,32},{1,33},{2,34},{3,35},{4,36},{5,37},{6,38},{7,39},{8,40},{9,... | collective-permute-start | bytes 4718600 | tf_op jit(solution)/shard_map/core/ppermute | solution.py:41
  68.2 5.7 %collective-permute-start.26 = (bf16[2,256,1536]{2,1,0:T(8,128)(2,1)}, bf16[2,256,1536]{2,1,0:T(8,128)(2,1)S(1)}, u32[]{:S(2)}, u32[]{:S(2)}) collective-permute-start(bf16[2,256,1536]{2,1,0:T(8,128)(2,1)} %get-tuple-element.85.refs_9_), channel_id=1, source_target_pairs={{0,32},{1,33},{2,34},{3,35},{4,36},{5,37},{6,38},{7,39},{8,40},{9,... | collective-permute-start | bytes 4718600 | tf_op jit(solution)/shard_map/core/ppermute | solution.py:41
  68.3 3.0 %collective-permute-start.24 = (f32[4,8,128]{2,1,0:T(8,128)S(1)}, f32[4,8,128]{2,1,0:T(8,128)S(1)}, u32[]{:S(2)}, u32[]{:S(2)}) collective-permute-start(f32[4,8,128]{2,1,0:T(8,128)S(1)} %pad_maximum_fusion.1), channel_id=1, source_target_pairs={{0,24},{1,25},{2,26},{3,27},{4,28},{5,29},{6,30},{7,31},{8,0},{9,1... | collective-permute-start | bytes 49160 | tf_op jit(solution)/shard_map/ppermute | solution.py:45
  69.3 3.8 %collective-permute-start.23 = (f32[4,8,128]{2,1,0:T(8,128)S(1)}, f32[4,8,128]{2,1,0:T(8,128)S(1)}, u32[]{:S(2)}, u32[]{:S(2)}) collective-permute-start(f32[4,8,128]{2,1,0:T(8,128)S(1)} %pad_maximum_fusion.1), channel_id=1, source_target_pairs={{0,8},{1,9},{2,10},{3,11},{4,12},{5,13},{6,14},{7,15},{8,16},{9,17... | collective-permute-start | bytes 49160 | tf_op jit(solution)/shard_map/ppermute | solution.py:45
  69.8 4.1 %collective-permute-start.22 = (f32[4,8,128]{2,1,0:T(8,128)S(1)}, f32[4,8,128]{2,1,0:T(8,128)S(1)}, u32[]{:S(2)}, u32[]{:S(2)}) collective-permute-start(f32[4,8,128]{2,1,0:T(8,128)S(1)} %pad_maximum_fusion.1), channel_id=1, source_target_pairs={{0,16},{1,17},{2,18},{3,19},{4,20},{5,21},{6,22},{7,23},{8,24},{9,... | collective-permute-start | bytes 49160 | tf_op jit(solution)/shard_map/ppermute | solution.py:45
  73.9 3.8 %collective-permute-start.27 = (f32[4,4,128]{2,1,0:T(4,128)S(1)}, f32[4,4,128]{2,1,0:T(4,128)S(1)}, u32[]{:S(2)}, u32[]{:S(2)}) collective-permute-start(f32[4,4,128]{2,1,0:T(4,128)S(1)} %exponential_multiply_fusion.refs_0_), channel_id=1, source_target_pairs={{0,32},{1,33},{2,34},{3,35},{4,36},{5,37},{6,38},{7,39},{8,40},{9,... | collective-permute-start | bytes 24584 | tf_op jit(solution)/shard_map/core/ppermute | solution.py:41

commit v5 on v4

--- a/solution.py
+++ b/solution.py
@@ -114,18 +114,21 @@
             cut = slice(t * LANES, (t + 1) * LANES)
             top = jnp.max(jnp.maximum(scores[0][cut], scores[1][cut]), axis=1, keepdims=True)
             powers = [jnp.exp(score[cut] - top) for score in scores]
-            for c, power in enumerate(powers):
-                staged[c, u, cut, :] = power.astype(jnp.bfloat16)
+            staged[u, cut, :] = powers[0].astype(jnp.bfloat16)
+            copy = pltpu.make_async_copy(
+                staged.at[u, pl.ds(t * LANES, LANES)],
+                ours_ref.at[u, pl.ds(t * LANES, LANES)],
+                part_sems.at[u, t],
+            )
+            copy.start()
+            copies.append(copy)
+            sent_ref[u, cut, :cent] = powers[1].astype(jnp.bfloat16)
             total = jnp.sum(powers[0] + powers[1], axis=1, keepdims=True)
             flat = jnp.where(lane == 0, top, total).T
             turn = half * (size // LANES) + t
             row = jnp.where(core == 0, mids[0][turn], mids[1][turn])
             stat_ref[last, pl.ds(row, 1), :] = flat[0:1, :]
             stat_ref[last, pl.ds(SIDE + row, 1), :] = flat[1:2, :]
-        for c, there in enumerate((ours_ref.at[u], sent_ref.at[u, :, pl.ds(0, cent)])):
-            copy = pltpu.make_async_copy(staged.at[c, u], there, part_sems.at[c, u])
-            copy.start()
-            copies.append(copy)
     for copy in copies:
         copy.wait()
 
@@ -133,20 +136,19 @@
 def score_rows(units, rows, cents, biases, local, scale):
     size, width = rows[0].shape
     cent = cents[0].shape[0]
-    hbm = pl.BlockSpec(memory_space=pl.ANY)
     vmem = pl.BlockSpec(memory_space=pltpu.VMEM)
     return pl.pallas_call(
         functools.partial(score_kernel, scale, units),
         out_shape=(
             pltpu.HBM((2, size, cent), jnp.bfloat16),
-            pltpu.HBM((2, size, cent + width), jnp.bfloat16),
+            pltpu.VMEM((2, size, cent + width), jnp.bfloat16),
             jax.ShapeDtypeStruct(local.shape, jnp.float32),
         ),
         in_specs=[vmem] * 7,
-        out_specs=(hbm, hbm, vmem),
+        out_specs=(pl.BlockSpec(memory_space=pl.ANY), vmem, vmem),
         scratch_shapes=[
-            pltpu.VMEM((2, 2, size, cent), jnp.bfloat16),
-            pltpu.SemaphoreType.DMA((2, 2)),
+            pltpu.VMEM((2, size, cent), jnp.bfloat16),
+            pltpu.SemaphoreType.DMA((2, size // LANES)),
             pltpu.SemaphoreType.DMA((2,)),
         ],
         compiler_params=pltpu.CompilerParams(vmem_limit_bytes=14 * 2**20),
@@ -164,7 +166,9 @@
     calls = len(spots) // 2
     factors, refs = refs[:2], refs[2:]
     ours, sent, got, refs = refs[:calls], refs[calls : 2 * calls], refs[2 * calls : 3 * calls], refs[3 * calls :]
-    out_ref, sums_ref, loads_ref, parts, blocks, staged, rounded, sems, part_sems, block_sems = refs
+    out_ref, sums_ref, loads_ref, *refs = refs
+    parts, blocks, staged, rounded, sums, sems, part_sems, block_sems, sum_sems = refs
+    order = [*range(SIDE, pieces), *range(SIDE)]
     tiles = SIDE
     cent = sums_ref.shape[0]
     half = parts.shape[1] // 2
@@ -208,8 +212,8 @@
     found = [sources(p) for p in place]
 
     def body(core):
-        def sends(i):
-            slot = i % SLOTS
+        def sends(n):
+            i, slot = order[n], n % SLOTS
             kind = core if i < SIDE else 1 - core
             last = found[kind][0][i % SIDE]
             for x_lo in range(2):
@@ -220,24 +224,30 @@
                         there = out_ref.at[x_lo, 1, j, :, last]
                     yield pltpu.make_async_copy(staged.at[slot, x_lo, j], there, sems.at[slot])
 
-        def add_sums(i, part):
+        def sum_copy(part):
+            width = blocks.shape[2] // SPLIT
+            cols = pl.ds(part * width, width)
+            return pltpu.make_async_copy(sums.at[:, cols], sums_ref.at[:, cols], sum_sems.at[part])
+
+        def add_sums(n, part):
+            i = order[n]
             width = blocks.shape[2] // SPLIT
             cols = slice(part * width, (part + 1) * width)
             part_sums = lax.dot_general(
-                rounded[i % 2],
+                rounded[n % 2],
                 block_of(i, cols),
                 (((0,), (0,)), ((), ())),
                 preferred_element_type=jnp.float32,
             )
-            if i == 0:
-                sums_ref[:, cols] = part_sums
-            elif i + 1 < pieces:
-                sums_ref[:, cols] += part_sums
+            if n == 0:
+                sums[:, cols] = part_sums
+            elif n + 1 < pieces:
+                sums[:, cols] += part_sums
             else:
-                sums_ref[:, cols] = (sums_ref[:, cols] + part_sums) * (1.0 / math.sqrt(total_rows))
-
-        def weigh(i, t):
-            slot = i % SLOTS
+                sums[:, cols] = (sums[:, cols] + part_sums) * (1.0 / math.sqrt(total_rows))
+
+        def weigh(n, t):
+            i, slot = order[n], n % SLOTS
             kind = core if i < SIDE else 1 - core
             mid = found[kind][1][t]
             part = slice(t * LANES, (t + 1) * LANES)
@@ -252,28 +262,31 @@
                         staged[slot, p % 2, j, mid, p // 2] = chunk
                     else:
                         staged[slot, mid & 1, j, p, mid >> 1] = chunk
-            rounded[i % 2, part, :] = weight.astype(jnp.bfloat16)
+            rounded[n % 2, part, :] = weight.astype(jnp.bfloat16)
             return jnp.sum(weight.reshape(LANES // 8, 8, cent), axis=0)
 
         load = jnp.zeros((8, cent), jnp.float32)
-        for i in range(pieces):
-            if i >= SLOTS:
-                for copy in sends(i - SLOTS):
+        for n in range(pieces):
+            if n >= SLOTS:
+                for copy in sends(n - SLOTS):
                     copy.wait()
-            for copy in fetches(i):
+            for copy in fetches(order[n]):
                 copy.wait()
             for t in range(tiles):
-                load = load + weigh(i, t)
-                if i and (t + 1) % (tiles // SPLIT) == 0:
-                    add_sums(i - 1, t // (tiles // SPLIT))
-            for copy in sends(i):
+                load = load + weigh(n, t)
+                if n and (t + 1) % (tiles // SPLIT) == 0:
+                    add_sums(n - 1, t // (tiles // SPLIT))
+            for copy in sends(n):
                 copy.start()
         for part in range(SPLIT):
             add_sums(pieces - 1, part)
+            sum_copy(part).start()
         loads_ref[...] = jnp.sum(load, axis=0, keepdims=True) * (1.0 / total_rows)
-        for i in range(pieces - SLOTS, pieces):
-            for copy in sends(i):
+        for n in range(pieces - SLOTS, pieces):
+            for copy in sends(n):
                 copy.wait()
+        for part in range(SPLIT):
+            sum_copy(part).wait()
 
     for core in range(2):
 
@@ -298,15 +311,17 @@
         in_specs=[vmem] * 2
         + [hbm] * (len(ours) + len(sent))
         + [vmem] * len(got),
-        out_specs=(hbm, vmem, vmem),
+        out_specs=(hbm, hbm, vmem),
         scratch_shapes=[
             pltpu.VMEM((SIDE, height, cent), jnp.bfloat16),
             pltpu.VMEM((SIDE, height, width), jnp.bfloat16),
             pltpu.VMEM((SLOTS, 2, 2, 4, 2, 16, cent), jnp.float32),
             pltpu.VMEM((2, height, cent), jnp.bfloat16),
+            pltpu.VMEM((cent, width), jnp.float32),
             pltpu.SemaphoreType.DMA((SLOTS,)),
             pltpu.SemaphoreType.DMA((SIDE, 2)),
             pltpu.SemaphoreType.DMA((SIDE, 2)),
+            pltpu.SemaphoreType.DMA((SPLIT,)),
         ],
         compiler_params=pltpu.CompilerParams(vmem_limit_bytes=20 * 2**20),
         name="weights",
@@ -353,9 +368,10 @@
     with jax.named_scope("last"):
         before_a, after_b = shift(own_a, axes, 1), shift(own_b, axes, -1)
         before_b, after_a = shift(own_b, axes, 1), shift(own_a, axes, -1)
+    local = score(((0, 0), (0, 1)), (own_a, own_b), local)
+    after_b, local = lax.optimization_barrier((after_b, local))
     with jax.named_scope("across"):
         across_a, across_b = shift(before_a, axes, 1), shift(after_b, axes, -1)
-    local = score(((0, 0), (0, 1)), (own_a, own_b), local)
     local = score(((1, 0), (2, 1)), (before_a, after_b), local)
     before_b, after_a, local = lax.optimization_barrier((before_b, after_a, local))
     local = score(((1, 1), (2, 0)), (before_b, after_a), local)

time: 87.4 us -> 85.1 us (0.974)
  Pallas kernels: 20.4 us -> 17.5 us
  waiting for transfers between devices: 22.8 us -> 25 us
  starting transfers between devices: 41.1 us -> 39.5 us
    ppermute x21, waiting for transfers between devices: 22 us -> 24.2 us  [shift(): return lax.ppermute(value, AXES, along(*axes, by))]
    ppermute x7, starting transfers between devices: 12 us -> 10.4 us  [to_core(): return lax.ppermute(value, AXES, pairs)]
    pallas_call x1, Pallas kernels: 9.3 us -> 7.8 us  [weight_all(): pl.pallas_call(functools.partial(weight_kernel, spots, float(total_rows))...]
    pallas_call x4, Pallas kernels: 11.1 us -> 9.71 us  [score_rows(): pl.pallas_call(functools.partial(score_kernel, scale, units), out_shape=(...]
  transfers between devices with their start and end apart: 28 -> 28, of which waited for: 13 -> 15; matrix products, arithmetic and copies ran while one was open for 2% -> 2% of each run, Pallas kernels for 10% -> 9%
where the time goes in v5:
time: 85.1 us; the launch traced here: 84.9 us
  starting transfers between devices  39.5 us (46%)
  waiting for transfers between devices  25 us (29%)
  Pallas kernels  17.5 us (21%)
  between operations  1.07 us (1%)
  local copies, waits for them, and re-layouts  0.99 us (1%)
    ppermute x21, starting transfers between devices, shift(): return lax.ppermute(value, AXES, along(*axes, by))  29.1 us
    ppermute x21, waiting for transfers between devices, shift(): return lax.ppermute(value, AXES, along(*axes, by))  24.2 us
    ppermute x7, starting transfers between devices, to_core(): return lax.ppermute(value, AXES, pairs)  10.4 us
    pallas_call x4, Pallas kernels, score_rows(): pl.pallas_call(functools.partial(score_kernel, scale, units), out_shape=(...  9.71 us
    pallas_call x1, Pallas kernels, weight_all(): pl.pallas_call(functools.partial(weight_kernel, spots, float(total_rows))...  7.8 us
  transfers between devices with their start and end apart: 28, of which 15 were waited for; matrix products, arithmetic and copies ran while one was open for 2% of the time, Pallas kernels for 9%

profile of v5, /device:TPU:1, one launch (start us, length us, event | category | flops | bytes accessed | tf_op | source)
XLA Modules:
  0.0 84.9 jit_solution(8768050596324021270)
XLA Ops:
  0.6 1.5 %collective-permute-start.3 = (bf16[512,1024]{1,0:T(8,128)(2,1)}, bf16[512,1024]{1,0:T(8,128)(2,1)S(1)}, u32[]{:S(2)}, u32[]{:S(2)}) collective-permute-start(bf16[512,1024]{1,0:T(8,128)(2,1)} %cent_a.3), channel_id=1, source_target_pairs={{0,32},{1,33},{2,34},{3,35},{4,36},{5,37},{6,38},{7,39},{8,40},{9,... | collective-permute-start | bytes 3145736 | tf_op jit(solution)/shard_map/core/ppermute | solution.py:41
  2.1 3.8 %collective-permute-start.2 = (bf16[32,1024]{1,0:T(8,128)(2,1)}, bf16[32,1024]{1,0:T(8,128)(2,1)S(1)}, u32[]{:S(2)}, u32[]{:S(2)}) collective-permute-start(bf16[32,1024]{1,0:T(8,128)(2,1)} %bitcast.23), channel_id=1, source_target_pairs={{0,65},{1,64},{2,67},{3,66},{4,69},{5,68},{6,71},{7,70},{8,73},{9,... | collective-permute-start | bytes 196616 | tf_op jit(solution)/shard_map/ppermute | solution.py:45
  6.0 1.3 %collective-permute-start = (bf16[32,1024]{1,0:T(8,128)(2,1)}, bf16[32,1024]{1,0:T(8,128)(2,1)S(1)}, u32[]{:S(2)}, u32[]{:S(2)}) collective-permute-start(bf16[32,1024]{1,0:T(8,128)(2,1)} %bitcast.25), channel_id=1, source_target_pairs={{0,1},{1,0},{2,3},{3,2},{4,5},{5,4},{6,7},{7,6},{8,9},{9,8},{10,11... | collective-permute-start | bytes 196616 | tf_op jit(solution)/shard_map/ppermute | solution.py:45
  7.3 0.7 convert_multiply_fusion
  8.0 0.1 collective-permute-start.4
  8.1 0.9 %bitcast_dynamic-update-slice_fusion.3 = bf16[4,32,1024]{2,1,0:T(8,128)(2,1)S(1)} fusion(bf16[4,32,1024]{2,1,0:T(8,128)(2,1)S(1)} %broadcast_in_dim.19, s32[]{:T(128)S(6)} %select_n.32, bf16[1,32,1024]{2,1,0:T(8,128)(2,1)} %bitcast.26), kind=kLoop, calls=%fused_computation.3 | loop fusion | bytes 131076 | tf_op jit(solution)/shard_map/jit(dynamic_update_index_in_dim)/dynamic_update_slice | solution.py:59
  8.9 2.0 %collective-permute-done = bf16[32,1024]{1,0:T(8,128)(2,1)S(1)} collective-permute-done((bf16[32,1024]{1,0:T(8,128)(2,1)}, bf16[32,1024]{1,0:T(8,128)(2,1)S(1)}, u32[]{:S(2)}, u32[]{:S(2)}) %collective-permute-start) | collective-permute-done | bytes 65568 | tf_op jit(solution)/shard_map/ppermute | solution.py:45
  10.9 0.3 collective-permute-done.1
  11.2 0.0 collective-permute-done.2
  11.3 0.0 collective-permute-done.4.bias_b
  11.3 1.3 %collective-permute-start.8 = (bf16[128,1024]{1,0:T(8,128)(2,1)S(1)}, bf16[128,1024]{1,0:T(8,128)(2,1)S(1)}, u32[]{:S(2)}, u32[]{:S(2)}) collective-permute-start(bf16[128,1024]{1,0:T(8,128)(2,1)S(1)} %bitcast.19), channel_id=1, source_target_pairs={{0,2},{1,3},{2,4},{3,5},{4,6},{5,7},{6,0},{7,1},{8,10},{9,11},{10,... | collective-permute-start | bytes 786440 | tf_op jit(solution)/shard_map/mid/ppermute | solution.py:45
  12.6 2.5 %collective-permute-start.9 = (bf16[128,1024]{1,0:T(8,128)(2,1)S(1)}, bf16[128,1024]{1,0:T(8,128)(2,1)S(1)}, u32[]{:S(2)}, u32[]{:S(2)}) collective-permute-start(bf16[128,1024]{1,0:T(8,128)(2,1)S(1)} %bitcast.20), channel_id=1, source_target_pairs={{0,4},{1,5},{2,6},{3,7},{4,0},{5,1},{6,2},{7,3},{8,12},{9,13},{10,... | collective-permute-start | bytes 786440 | tf_op jit(solution)/shard_map/mid/ppermute | solution.py:45
  15.0 1.2 %collective-permute-start.5 = (bf16[128,1024]{1,0:T(8,128)(2,1)S(1)}, bf16[128,1024]{1,0:T(8,128)(2,1)S(1)}, u32[]{:S(2)}, u32[]{:S(2)}) collective-permute-start(bf16[128,1024]{1,0:T(8,128)(2,1)S(1)} %bitcast.21), channel_id=1, source_target_pairs={{0,6},{1,7},{2,0},{3,1},{4,2},{5,3},{6,4},{7,5},{8,14},{9,15},{10,... | collective-permute-start | bytes 786440 | tf_op jit(solution)/shard_map/mid/ppermute | solution.py:45
  16.2 1.9 %collective-permute-done.8 = bf16[128,1024]{1,0:T(8,128)(2,1)S(1)} collective-permute-done((bf16[128,1024]{1,0:T(8,128)(2,1)S(1)}, bf16[128,1024]{1,0:T(8,128)(2,1)S(1)}, u32[]{:S(2)}, u32[]{:S(2)}) %collective-permute-start.8) | collective-permute-done | bytes 262176 | tf_op jit(solution)/shard_map/mid/ppermute | solution.py:45
  18.1 3.8 %collective-permute-done.9 = bf16[128,1024]{1,0:T(8,128)(2,1)S(1)} collective-permute-done((bf16[128,1024]{1,0:T(8,128)(2,1)S(1)}, bf16[128,1024]{1,0:T(8,128)(2,1)S(1)}, u32[]{:S(2)}, u32[]{:S(2)}) %collective-permute-start.9) | collective-permute-done | bytes 262176 | tf_op jit(solution)/shard_map/mid/ppermute | solution.py:45
  21.9 2.5 %collective-permute-start.10 = (bf16[256,1024]{1,0:T(8,128)(2,1)S(1)}, bf16[256,1024]{1,0:T(8,128)(2,1)S(1)}, u32[]{:S(2)}, u32[]{:S(2)}) collective-permute-start(bf16[256,1024]{1,0:T(8,128)(2,1)S(1)} %constant_dynamic-update-slice_fusion.2.rows_b), channel_id=1, source_target_pairs={{0,24},{1,25},{2,26},{3,27},{4,28},{5,29},{6,30},{7,31},{8,0},{9,1... | collective-permute-start | bytes 1572872 | tf_op jit(solution)/shard_map/last/ppermute | solution.py:45
  24.4 0.1 collective-permute-start.6
  24.5 2.7 %collective-permute-start.13 = (bf16[256,1024]{1,0:T(8,128)(2,1)S(1)}, bf16[256,1024]{1,0:T(8,128)(2,1)S(1)}, u32[]{:S(2)}, u32[]{:S(2)}) collective-permute-start(bf16[256,1024]{1,0:T(8,128)(2,1)S(1)} %constant_dynamic-update-slice_fusion.rows_a), channel_id=1, source_target_pairs={{0,24},{1,25},{2,26},{3,27},{4,28},{5,29},{6,30},{7,31},{8,0},{9,1... | collective-permute-start | bytes 1572872 | tf_op jit(solution)/shard_map/last/ppermute | solution.py:45
  27.2 2.5 %scores.4 = (bf16[2,256,512]{2,1,0:T(8,128)(2,1)}, bf16[2,256,1536]{2,1,0:T(8,128)(2,1)S(1)}, f32[4,8,128]{2,1,0:T(8,128)S(1)}) custom-call(bf16[256,1024]{1,0:T(8,128)(2,1)S(1)} %constant_dynamic-update-slice_fusion.rows_a, bf16[256,1024]{1,0:T(8,128)(2,1)S(1)} %constant_dynamic-update-slice_fusion.2.rows_b, bf16[512,1024]{1,0:T(8,128)(2,1)S(1)} %copy-done.4, ...), custom_call_target="tpu_custom_call" | custom-call | flops 1073741824 | bytes 4194304 | tf_op jit(solution)/shard_map/scores/pallas_call | solution.py:140
  29.7 0.9 %collective-permute-done.10.rows_b = bf16[256,1024]{1,0:T(8,128)(2,1)S(1)} collective-permute-done((bf16[256,1024]{1,0:T(8,128)(2,1)S(1)}, bf16[256,1024]{1,0:T(8,128)(2,1)S(1)}, u32[]{:S(2)}, u32[]{:S(2)}) %collective-permute-start.10) | collective-permute-done | bytes 524320 | tf_op jit(solution)/shard_map/last/ppermute | solution.py:45
  30.5 3.5 %collective-permute-done.6.rows_a = bf16[256,1024]{1,0:T(8,128)(2,1)S(1)} collective-permute-done((bf16[256,1024]{1,0:T(8,128)(2,1)S(1)}, bf16[256,1024]{1,0:T(8,128)(2,1)S(1)}, u32[]{:S(2)}, u32[]{:S(2)}) %collective-permute-start.6) | collective-permute-done | bytes 524320 | tf_op jit(solution)/shard_map/last/ppermute | solution.py:45
  34.0 2.7 %collective-permute-start.11 = (bf16[256,1024]{1,0:T(8,128)(2,1)S(1)}, bf16[256,1024]{1,0:T(8,128)(2,1)S(1)}, u32[]{:S(2)}, u32[]{:S(2)}) collective-permute-start(bf16[256,1024]{1,0:T(8,128)(2,1)S(1)} %collective-permute-done.10.rows_b), channel_id=1, source_target_pairs={{0,24},{1,25},{2,26},{3,27},{4,28},{5,29},{6,30},{7,31},{8,0},{9,1... | collective-permute-start | bytes 1572872 | tf_op jit(solution)/shard_map/across/ppermute | solution.py:45
  36.7 2.4 %scores.5 = (bf16[2,256,512]{2,1,0:T(8,128)(2,1)}, bf16[2,256,1536]{2,1,0:T(8,128)(2,1)S(1)}, f32[4,8,128]{2,1,0:T(8,128)S(1)}) custom-call(bf16[256,1024]{1,0:T(8,128)(2,1)S(1)} %collective-permute-done.6.rows_a, bf16[256,1024]{1,0:T(8,128)(2,1)S(1)} %collective-permute-done.10.rows_b, bf16[512,1024]{1,0:T(8,128)(2,1)S(1)} %copy-done.4, ...), custom_call_target="tpu_custom_call" | custom-call | flops 1073741824 | bytes 4194304 | tf_op jit(solution)/shard_map/scores/pallas_call | solution.py:140
  39.2 0.5 collective-permute-done.12.rows_a
  39.7 2.4 %scores.6 = (bf16[2,256,512]{2,1,0:T(8,128)(2,1)}, bf16[2,256,1536]{2,1,0:T(8,128)(2,1)S(1)}, f32[4,8,128]{2,1,0:T(8,128)S(1)}) custom-call(bf16[256,1024]{1,0:T(8,128)(2,1)S(1)} %collective-permute-done.12.rows_a, bf16[256,1024]{1,0:T(8,128)(2,1)S(1)} %collective-permute-done.13.rows_b, bf16[512,1024]{1,0:T(8,128)(2,1)S(1)} %copy-done.4, ...), custom_call_target="tpu_custom_call" | custom-call | flops 1073741824 | bytes 4194304 | tf_op jit(solution)/shard_map/scores/pallas_call | solution.py:140
  42.1 3.2 %collective-permute-done.7.rows_a = bf16[256,1024]{1,0:T(8,128)(2,1)S(1)} collective-permute-done((bf16[256,1024]{1,0:T(8,128)(2,1)S(1)}, bf16[256,1024]{1,0:T(8,128)(2,1)S(1)}, u32[]{:S(2)}, u32[]{:S(2)}) %collective-permute-start.7) | collective-permute-done | bytes 524320 | tf_op jit(solution)/shard_map/across/ppermute | solution.py:45
  45.3 2.4 %scores.7 = (bf16[2,256,512]{2,1,0:T(8,128)(2,1)}, bf16[2,256,1536]{2,1,0:T(8,128)(2,1)S(1)}, f32[4,8,128]{2,1,0:T(8,128)S(1)}) custom-call(bf16[256,1024]{1,0:T(8,128)(2,1)S(1)} %collective-permute-done.7.rows_a, bf16[256,1024]{1,0:T(8,128)(2,1)S(1)} %collective-permute-done.11.rows_b, bf16[512,1024]{1,0:T(8,128)(2,1)S(1)} %copy-done.4, ...), custom_call_target="tpu_custom_call" | custom-call | flops 1073741824 | bytes 4194304 | tf_op jit(solution)/shard_map/scores/pallas_call | solution.py:140
  47.7 2.4 %collective-permute-start.16 = (f32[4,8,128]{2,1,0:T(8,128)S(1)}, f32[4,8,128]{2,1,0:T(8,128)S(1)}, u32[]{:S(2)}, u32[]{:S(2)}) collective-permute-start(f32[4,8,128]{2,1,0:T(8,128)S(1)} %get-tuple-element.66), channel_id=1, source_target_pairs={{0,65},{1,64},{2,67},{3,66},{4,69},{5,68},{6,71},{7,70},{8,73},{9,... | collective-permute-start | bytes 49160 | tf_op jit(solution)/shard_map/ppermute | solution.py:45
  50.1 0.0 collective-permute-start.15
  50.1 1.4 %collective-permute-start.14 = (f32[4,8,128]{2,1,0:T(8,128)S(1)}, f32[4,8,128]{2,1,0:T(8,128)S(1)}, u32[]{:S(2)}, u32[]{:S(2)}) collective-permute-start(f32[4,8,128]{2,1,0:T(8,128)S(1)} %get-tuple-element.66), channel_id=1, source_target_pairs={{0,1},{1,0},{2,3},{3,2},{4,5},{5,4},{6,7},{7,6},{8,9},{9,8},{10,11... | collective-permute-start | bytes 49160 | tf_op jit(solution)/shard_map/ppermute | solution.py:45
  51.5 2.4 %collective-permute-done.15 = f32[4,8,128]{2,1,0:T(8,128)S(1)} collective-permute-done((f32[4,8,128]{2,1,0:T(8,128)S(1)}, f32[4,8,128]{2,1,0:T(8,128)S(1)}, u32[]{:S(2)}, u32[]{:S(2)}) %collective-permute-start.15) | collective-permute-done | bytes 16416 | tf_op jit(solution)/shard_map/ppermute | solution.py:45
  53.9 0.3 collective-permute-done.14
  54.2 5.6 %collective-permute-start.20 = (bf16[2,256,1536]{2,1,0:T(8,128)(2,1)S(1)}, bf16[2,256,1536]{2,1,0:T(8,128)(2,1)S(1)}, u32[]{:S(2)}, u32[]{:S(2)}) collective-permute-start(bf16[2,256,1536]{2,1,0:T(8,128)(2,1)S(1)} %get-tuple-element.86.refs_6_), channel_id=1, source_target_pairs={{0,32},{1,33},{2,34},{3,35},{4,36},{5,37},{6,38},{7,39},{8,40},{9,... | collective-permute-start | bytes 4718600 | tf_op jit(solution)/shard_map/core/ppermute | solution.py:41
  59.8 0.1 collective-permute-start.21
  59.9 3.0 %collective-permute-start.19 = (f32[4,8,128]{2,1,0:T(8,128)S(1)}, f32[4,8,128]{2,1,0:T(8,128)S(1)}, u32[]{:S(2)}, u32[]{:S(2)}) collective-permute-start(f32[4,8,128]{2,1,0:T(8,128)S(1)} %pad_maximum_fusion), channel_id=1, source_target_pairs={{0,6},{1,7},{2,0},{3,1},{4,2},{5,3},{6,4},{7,5},{8,14},{9,15},{10,... | collective-permute-start | bytes 49160 | tf_op jit(solution)/shard_map/ppermute | solution.py:45
  62.9 1.2 %collective-permute-start.17 = (f32[4,8,128]{2,1,0:T(8,128)S(1)}, f32[4,8,128]{2,1,0:T(8,128)S(1)}, u32[]{:S(2)}, u32[]{:S(2)}) collective-permute-start(f32[4,8,128]{2,1,0:T(8,128)S(1)} %pad_maximum_fusion), channel_id=1, source_target_pairs={{0,4},{1,5},{2,6},{3,7},{4,0},{5,1},{6,2},{7,3},{8,12},{9,13},{10,... | collective-permute-start | bytes 49160 | tf_op jit(solution)/shard_map/ppermute | solution.py:45
  64.1 2.9 %collective-permute-done.18 = f32[4,8,128]{2,1,0:T(8,128)S(1)} collective-permute-done((f32[4,8,128]{2,1,0:T(8,128)S(1)}, f32[4,8,128]{2,1,0:T(8,128)S(1)}, u32[]{:S(2)}, u32[]{:S(2)}) %collective-permute-start.18) | collective-permute-done | bytes 16416 | tf_op jit(solution)/shard_map/ppermute | solution.py:45
  67.0 0.2 collective-permute-done.17
  67.3 0.5 collective-permute-start.25
  67.8 0.1 collective-permute-start.26
  67.9 1.0 %collective-permute-start.24 = (f32[4,8,128]{2,1,0:T(8,128)S(1)}, f32[4,8,128]{2,1,0:T(8,128)S(1)}, u32[]{:S(2)}, u32[]{:S(2)}) collective-permute-start(f32[4,8,128]{2,1,0:T(8,128)S(1)} %pad_maximum_fusion.1), channel_id=1, source_target_pairs={{0,24},{1,25},{2,26},{3,27},{4,28},{5,29},{6,30},{7,31},{8,0},{9,1... | collective-permute-start | bytes 49160 | tf_op jit(solution)/shard_map/ppermute | solution.py:45
  68.9 0.4 collective-permute-start.23
  69.3 1.7 %collective-permute-start.22 = (f32[4,8,128]{2,1,0:T(8,128)S(1)}, f32[4,8,128]{2,1,0:T(8,128)S(1)}, u32[]{:S(2)}, u32[]{:S(2)}) collective-permute-start(f32[4,8,128]{2,1,0:T(8,128)S(1)} %pad_maximum_fusion.1), channel_id=1, source_target_pairs={{0,16},{1,17},{2,18},{3,19},{4,20},{5,21},{6,22},{7,23},{8,24},{9,... | collective-permute-start | bytes 49160 | tf_op jit(solution)/shard_map/ppermute | solution.py:45
  71.1 1.6 %collective-permute-done.23 = f32[4,8,128]{2,1,0:T(8,128)S(1)} collective-permute-done((f32[4,8,128]{2,1,0:T(8,128)S(1)}, f32[4,8,128]{2,1,0:T(8,128)S(1)}, u32[]{:S(2)}, u32[]{:S(2)}) %collective-permute-start.23) | collective-permute-done | bytes 16416 | tf_op jit(solution)/shard_map/ppermute | solution.py:45
  72.7 0.7 collective-permute-done.22
  73.5 2.6 %collective-permute-start.27 = (f32[4,4,128]{2,1,0:T(4,128)S(1)}, f32[4,4,128]{2,1,0:T(4,128)S(1)}, u32[]{:S(2)}, u32[]{:S(2)}) collective-permute-start(f32[4,4,128]{2,1,0:T(4,128)S(1)} %exponential_multiply_fusion.refs_0_), channel_id=1, source_target_pairs={{0,32},{1,33},{2,34},{3,35},{4,36},{5,37},{6,38},{7,39},{8,40},{9,... | collective-permute-start | bytes 24584 | tf_op jit(solution)/shard_map/core/ppermute | solution.py:41
  76.1 0.8 collective-permute-done.27.refs_1_
  76.9 7.8 %weights.1 = (f32[2,2,2,4,4,2,16,512]{7,6,5,4,3,2,1,0:T(8,128)}, f32[512,1024]{1,0:T(8,128)}, f32[1,512]{1,0:T(1,128)}) custom-call(f32[4,4,128]{2,1,0:T(4,128)S(1)} %exponential_multiply_fusion.refs_0_, f32[4,4,128]{2,1,0:T(4,128)S(1)} %collective-permute-done.27.refs_1_, bf16[2,256,512]{2,1,0:T(8,128)(2,1)} %get-tuple-element.82.refs_2_, ...), custom_call_target="tpu_custom_call" | custom-call | tf_op jit(solution)/shard_map/weights/pallas_call | solution.py:304
  (41 shorter events, 0.3 us)
Async XLA Ops:
  0.6 26.6 %copy-start.4 = (bf16[512,1024]{1,0:T(8,128)(2,1)S(1)}, bf16[512,1024]{1,0:T(8,128)(2,1)}, u32[]{:S(2)}) copy-start(bf16[512,1024]{1,0:T(8,128)(2,1)} %cent_a.3) | copy-start | bytes 3145732
  0.6 10.6 %collective-permute-start.3 = (bf16[512,1024]{1,0:T(8,128)(2,1)}, bf16[512,1024]{1,0:T(8,128)(2,1)S(1)}, u32[]{:S(2)}, u32[]{:S(2)}) collective-permute-start(bf16[512,1024]{1,0:T(8,128)(2,1)} %cent_a.3), channel_id=1, source_target_pairs={{0,32},{1,33},{2,34},{3,35},{4,36},{5,37},{6,38},{7,39},{8,40},{9,... | collective-permute-start | bytes 3145736 | tf_op jit(solution)/shard_map/core/ppermute | solution.py:41
  2.1 9.1 %collective-permute-start.2 = (bf16[32,1024]{1,0:T(8,128)(2,1)}, bf16[32,1024]{1,0:T(8,128)(2,1)S(1)}, u32[]{:S(2)}, u32[]{:S(2)}) collective-permute-start(bf16[32,1024]{1,0:T(8,128)(2,1)} %bitcast.23), channel_id=1, source_target_pairs={{0,65},{1,64},{2,67},{3,66},{4,69},{5,68},{6,71},{7,70},{8,73},{9,... | collective-permute-start | bytes 196616 | tf_op jit(solution)/shard_map/ppermute | solution.py:45
  6.0 5.2 %collective-permute-start.1 = (bf16[32,1024]{1,0:T(8,128)(2,1)}, bf16[32,1024]{1,0:T(8,128)(2,1)S(1)}, u32[]{:S(2)}, u32[]{:S(2)}) collective-permute-start(bf16[32,1024]{1,0:T(8,128)(2,1)} %bitcast.24), channel_id=1, source_target_pairs={{0,64},{1,65},{2,66},{3,67},{4,68},{5,69},{6,70},{7,71},{8,72},{9,... | collective-permute-start | bytes 196616 | tf_op jit(solution)/shard_map/ppermute | solution.py:45
  6.0 4.9 %collective-permute-start = (bf16[32,1024]{1,0:T(8,128)(2,1)}, bf16[32,1024]{1,0:T(8,128)(2,1)S(1)}, u32[]{:S(2)}, u32[]{:S(2)}) collective-permute-start(bf16[32,1024]{1,0:T(8,128)(2,1)} %bitcast.25), channel_id=1, source_target_pairs={{0,1},{1,0},{2,3},{3,2},{4,5},{5,4},{6,7},{7,6},{8,9},{9,8},{10,11... | collective-permute-start | bytes 196616 | tf_op jit(solution)/shard_map/ppermute | solution.py:45
  8.0 3.3 %collective-permute-start.4 = (f32[1,512]{1,0:T(1,128)S(1)}, f32[1,512]{1,0:T(1,128)S(1)}, u32[]{:S(2)}, u32[]{:S(2)}) collective-permute-start(f32[1,512]{1,0:T(1,128)S(1)} %bitcast.14), channel_id=1, source_target_pairs={{0,32},{1,33},{2,34},{3,35},{4,36},{5,37},{6,38},{7,39},{8,40},{9,... | collective-permute-start | bytes 6152 | tf_op jit(solution)/shard_map/core/ppermute | solution.py:41
  11.3 6.8 %collective-permute-start.8 = (bf16[128,1024]{1,0:T(8,128)(2,1)S(1)}, bf16[128,1024]{1,0:T(8,128)(2,1)S(1)}, u32[]{:S(2)}, u32[]{:S(2)}) collective-permute-start(bf16[128,1024]{1,0:T(8,128)(2,1)S(1)} %bitcast.19), channel_id=1, source_target_pairs={{0,2},{1,3},{2,4},{3,5},{4,6},{5,7},{6,0},{7,1},{8,10},{9,11},{10,... | collective-permute-start | bytes 786440 | tf_op jit(solution)/shard_map/mid/ppermute | solution.py:45
  12.6 9.3 %collective-permute-start.9 = (bf16[128,1024]{1,0:T(8,128)(2,1)S(1)}, bf16[128,1024]{1,0:T(8,128)(2,1)S(1)}, u32[]{:S(2)}, u32[]{:S(2)}) collective-permute-start(bf16[128,1024]{1,0:T(8,128)(2,1)S(1)} %bitcast.20), channel_id=1, source_target_pairs={{0,4},{1,5},{2,6},{3,7},{4,0},{5,1},{6,2},{7,3},{8,12},{9,13},{10,... | collective-permute-start | bytes 786440 | tf_op jit(solution)/shard_map/mid/ppermute | solution.py:45
  15.0 9.4 %collective-permute-start.5 = (bf16[128,1024]{1,0:T(8,128)(2,1)S(1)}, bf16[128,1024]{1,0:T(8,128)(2,1)S(1)}, u32[]{:S(2)}, u32[]{:S(2)}) collective-permute-start(bf16[128,1024]{1,0:T(8,128)(2,1)S(1)} %bitcast.21), channel_id=1, source_target_pairs={{0,6},{1,7},{2,0},{3,1},{4,2},{5,3},{6,4},{7,5},{8,14},{9,15},{10,... | collective-permute-start | bytes 786440 | tf_op jit(solution)/shard_map/mid/ppermute | solution.py:45
  21.9 8.6 %collective-permute-start.10 = (bf16[256,1024]{1,0:T(8,128)(2,1)S(1)}, bf16[256,1024]{1,0:T(8,128)(2,1)S(1)}, u32[]{:S(2)}, u32[]{:S(2)}) collective-permute-start(bf16[256,1024]{1,0:T(8,128)(2,1)S(1)} %constant_dynamic-update-slice_fusion.2.rows_b), channel_id=1, source_target_pairs={{0,24},{1,25},{2,26},{3,27},{4,28},{5,29},{6,30},{7,31},{8,0},{9,1... | collective-permute-start | bytes 1572872 | tf_op jit(solution)/shard_map/last/ppermute | solution.py:45
  24.4 9.6 %collective-permute-start.6 = (bf16[256,1024]{1,0:T(8,128)(2,1)S(1)}, bf16[256,1024]{1,0:T(8,128)(2,1)S(1)}, u32[]{:S(2)}, u32[]{:S(2)}) collective-permute-start(bf16[256,1024]{1,0:T(8,128)(2,1)S(1)} %constant_dynamic-update-slice_fusion.rows_a), channel_id=1, source_target_pairs={{0,8},{1,9},{2,10},{3,11},{4,12},{5,13},{6,14},{7,15},{8,16},{9,17... | collective-permute-start | bytes 1572872 | tf_op jit(solution)/shard_map/last/ppermute | solution.py:45
  24.5 14.6 %collective-permute-start.13 = (bf16[256,1024]{1,0:T(8,128)(2,1)S(1)}, bf16[256,1024]{1,0:T(8,128)(2,1)S(1)}, u32[]{:S(2)}, u32[]{:S(2)}) collective-permute-start(bf16[256,1024]{1,0:T(8,128)(2,1)S(1)} %constant_dynamic-update-slice_fusion.rows_a), channel_id=1, source_target_pairs={{0,24},{1,25},{2,26},{3,27},{4,28},{5,29},{6,30},{7,31},{8,0},{9,1... | collective-permute-start | bytes 1572872 | tf_op jit(solution)/shard_map/last/ppermute | solution.py:45
  27.2 12.5 %collective-permute-start.12 = (bf16[256,1024]{1,0:T(8,128)(2,1)S(1)}, bf16[256,1024]{1,0:T(8,128)(2,1)S(1)}, u32[]{:S(2)}, u32[]{:S(2)}) collective-permute-start(bf16[256,1024]{1,0:T(8,128)(2,1)S(1)} %constant_dynamic-update-slice_fusion.2.rows_b), channel_id=1, source_target_pairs={{0,8},{1,9},{2,10},{3,11},{4,12},{5,13},{6,14},{7,15},{8,16},{9,17... | collective-permute-start | bytes 1572872 | tf_op jit(solution)/shard_map/last/ppermute | solution.py:45
  29.7 24.6 %copy-start = (bf16[2,256,1536]{2,1,0:T(8,128)(2,1)}, bf16[2,256,1536]{2,1,0:T(8,128)(2,1)S(1)}, u32[]{:S(2)}) copy-start(bf16[2,256,1536]{2,1,0:T(8,128)(2,1)S(1)} %get-tuple-element.86.refs_6_) | copy-start | bytes 4718596
  34.0 11.2 %collective-permute-start.7 = (bf16[256,1024]{1,0:T(8,128)(2,1)S(1)}, bf16[256,1024]{1,0:T(8,128)(2,1)S(1)}, u32[]{:S(2)}, u32[]{:S(2)}) collective-permute-start(bf16[256,1024]{1,0:T(8,128)(2,1)S(1)} %collective-permute-done.6.rows_a), channel_id=1, source_target_pairs={{0,8},{1,9},{2,10},{3,11},{4,12},{5,13},{6,14},{7,15},{8,16},{9,17... | collective-permute-start | bytes 1572872 | tf_op jit(solution)/shard_map/across/ppermute | solution.py:45
  34.0 11.2 %collective-permute-start.11 = (bf16[256,1024]{1,0:T(8,128)(2,1)S(1)}, bf16[256,1024]{1,0:T(8,128)(2,1)S(1)}, u32[]{:S(2)}, u32[]{:S(2)}) collective-permute-start(bf16[256,1024]{1,0:T(8,128)(2,1)S(1)} %collective-permute-done.10.rows_b), channel_id=1, source_target_pairs={{0,24},{1,25},{2,26},{3,27},{4,28},{5,29},{6,30},{7,31},{8,0},{9,1... | collective-permute-start | bytes 1572872 | tf_op jit(solution)/shard_map/across/ppermute | solution.py:45
  39.1 20.7 %copy-start.1 = (bf16[2,256,1536]{2,1,0:T(8,128)(2,1)}, bf16[2,256,1536]{2,1,0:T(8,128)(2,1)S(1)}, u32[]{:S(2)}) copy-start(bf16[2,256,1536]{2,1,0:T(8,128)(2,1)S(1)} %get-tuple-element.87.refs_7_) | copy-start | bytes 4718596
  42.1 25.2 %copy-start.2 = (bf16[2,256,1536]{2,1,0:T(8,128)(2,1)}, bf16[2,256,1536]{2,1,0:T(8,128)(2,1)S(1)}, u32[]{:S(2)}) copy-start(bf16[2,256,1536]{2,1,0:T(8,128)(2,1)S(1)} %get-tuple-element.88.refs_8_) | copy-start | bytes 4718596
  47.7 29.2 %copy-start.3 = (bf16[2,256,1536]{2,1,0:T(8,128)(2,1)}, bf16[2,256,1536]{2,1,0:T(8,128)(2,1)S(1)}, u32[]{:S(2)}) copy-start(bf16[2,256,1536]{2,1,0:T(8,128)(2,1)S(1)} %get-tuple-element.89.refs_9_) | copy-start | bytes 4718596
  47.7 3.8 %collective-permute-start.16 = (f32[4,8,128]{2,1,0:T(8,128)S(1)}, f32[4,8,128]{2,1,0:T(8,128)S(1)}, u32[]{:S(2)}, u32[]{:S(2)}) collective-permute-start(f32[4,8,128]{2,1,0:T(8,128)S(1)} %get-tuple-element.66), channel_id=1, source_target_pairs={{0,65},{1,64},{2,67},{3,66},{4,69},{5,68},{6,71},{7,70},{8,73},{9,... | collective-permute-start | bytes 49160 | tf_op jit(solution)/shard_map/ppermute | solution.py:45
  50.1 3.8 %collective-permute-start.15 = (f32[4,8,128]{2,1,0:T(8,128)S(1)}, f32[4,8,128]{2,1,0:T(8,128)S(1)}, u32[]{:S(2)}, u32[]{:S(2)}) collective-permute-start(f32[4,8,128]{2,1,0:T(8,128)S(1)} %get-tuple-element.66), channel_id=1, source_target_pairs={{0,64},{1,65},{2,66},{3,67},{4,68},{5,69},{6,70},{7,71},{8,72},{9,... | collective-permute-start | bytes 49160 | tf_op jit(solution)/shard_map/ppermute | solution.py:45
  50.1 4.1 %collective-permute-start.14 = (f32[4,8,128]{2,1,0:T(8,128)S(1)}, f32[4,8,128]{2,1,0:T(8,128)S(1)}, u32[]{:S(2)}, u32[]{:S(2)}) collective-permute-start(f32[4,8,128]{2,1,0:T(8,128)S(1)} %get-tuple-element.66), channel_id=1, source_target_pairs={{0,1},{1,0},{2,3},{3,2},{4,5},{5,4},{6,7},{7,6},{8,9},{9,8},{10,11... | collective-permute-start | bytes 49160 | tf_op jit(solution)/shard_map/ppermute | solution.py:45
  54.2 13.0 %collective-permute-start.20 = (bf16[2,256,1536]{2,1,0:T(8,128)(2,1)S(1)}, bf16[2,256,1536]{2,1,0:T(8,128)(2,1)S(1)}, u32[]{:S(2)}, u32[]{:S(2)}) collective-permute-start(bf16[2,256,1536]{2,1,0:T(8,128)(2,1)S(1)} %get-tuple-element.86.refs_6_), channel_id=1, source_target_pairs={{0,32},{1,33},{2,34},{3,35},{4,36},{5,37},{6,38},{7,39},{8,40},{9,... | collective-permute-start | bytes 4718600 | tf_op jit(solution)/shard_map/core/ppermute | solution.py:41
  59.8 7.4 %collective-permute-start.21 = (bf16[2,256,1536]{2,1,0:T(8,128)(2,1)S(1)}, bf16[2,256,1536]{2,1,0:T(8,128)(2,1)S(1)}, u32[]{:S(2)}, u32[]{:S(2)}) collective-permute-start(bf16[2,256,1536]{2,1,0:T(8,128)(2,1)S(1)} %get-tuple-element.87.refs_7_), channel_id=1, source_target_pairs={{0,32},{1,33},{2,34},{3,35},{4,36},{5,37},{6,38},{7,39},{8,40},{9,... | collective-permute-start | bytes 4718600 | tf_op jit(solution)/shard_map/core/ppermute | solution.py:41
  59.9 4.1 %collective-permute-start.19 = (f32[4,8,128]{2,1,0:T(8,128)S(1)}, f32[4,8,128]{2,1,0:T(8,128)S(1)}, u32[]{:S(2)}, u32[]{:S(2)}) collective-permute-start(f32[4,8,128]{2,1,0:T(8,128)S(1)} %pad_maximum_fusion), channel_id=1, source_target_pairs={{0,6},{1,7},{2,0},{3,1},{4,2},{5,3},{6,4},{7,5},{8,14},{9,15},{10,... | collective-permute-start | bytes 49160 | tf_op jit(solution)/shard_map/ppermute | solution.py:45
  62.9 4.1 %collective-permute-start.18 = (f32[4,8,128]{2,1,0:T(8,128)S(1)}, f32[4,8,128]{2,1,0:T(8,128)S(1)}, u32[]{:S(2)}, u32[]{:S(2)}) collective-permute-start(f32[4,8,128]{2,1,0:T(8,128)S(1)} %pad_maximum_fusion), channel_id=1, source_target_pairs={{0,2},{1,3},{2,4},{3,5},{4,6},{5,7},{6,0},{7,1},{8,10},{9,11},{10,... | collective-permute-start | bytes 49160 | tf_op jit(solution)/shard_map/ppermute | solution.py:45
  62.9 4.3 %collective-permute-start.17 = (f32[4,8,128]{2,1,0:T(8,128)S(1)}, f32[4,8,128]{2,1,0:T(8,128)S(1)}, u32[]{:S(2)}, u32[]{:S(2)}) collective-permute-start(f32[4,8,128]{2,1,0:T(8,128)S(1)} %pad_maximum_fusion), channel_id=1, source_target_pairs={{0,4},{1,5},{2,6},{3,7},{4,0},{5,1},{6,2},{7,3},{8,12},{9,13},{10,... | collective-permute-start | bytes 49160 | tf_op jit(solution)/shard_map/ppermute | solution.py:45
  67.3 6.2 %collective-permute-start.25 = (bf16[2,256,1536]{2,1,0:T(8,128)(2,1)S(1)}, bf16[2,256,1536]{2,1,0:T(8,128)(2,1)S(1)}, u32[]{:S(2)}, u32[]{:S(2)}) collective-permute-start(bf16[2,256,1536]{2,1,0:T(8,128)(2,1)S(1)} %get-tuple-element.88.refs_8_), channel_id=1, source_target_pairs={{0,32},{1,33},{2,34},{3,35},{4,36},{5,37},{6,38},{7,39},{8,40},{9,... | collective-permute-start | bytes 4718600 | tf_op jit(solution)/shard_map/core/ppermute | solution.py:41
  67.8 5.7 %collective-permute-start.26 = (bf16[2,256,1536]{2,1,0:T(8,128)(2,1)S(1)}, bf16[2,256,1536]{2,1,0:T(8,128)(2,1)S(1)}, u32[]{:S(2)}, u32[]{:S(2)}) collective-permute-start(bf16[2,256,1536]{2,1,0:T(8,128)(2,1)S(1)} %get-tuple-element.89.refs_9_), channel_id=1, source_target_pairs={{0,32},{1,33},{2,34},{3,35},{4,36},{5,37},{6,38},{7,39},{8,40},{9,... | collective-permute-start | bytes 4718600 | tf_op jit(solution)/shard_map/core/ppermute | solution.py:41
  67.9 3.2 %collective-permute-start.24 = (f32[4,8,128]{2,1,0:T(8,128)S(1)}, f32[4,8,128]{2,1,0:T(8,128)S(1)}, u32[]{:S(2)}, u32[]{:S(2)}) collective-permute-start(f32[4,8,128]{2,1,0:T(8,128)S(1)} %pad_maximum_fusion.1), channel_id=1, source_target_pairs={{0,24},{1,25},{2,26},{3,27},{4,28},{5,29},{6,30},{7,31},{8,0},{9,1... | collective-permute-start | bytes 49160 | tf_op jit(solution)/shard_map/ppermute | solution.py:45
  68.9 3.8 %collective-permute-start.23 = (f32[4,8,128]{2,1,0:T(8,128)S(1)}, f32[4,8,128]{2,1,0:T(8,128)S(1)}, u32[]{:S(2)}, u32[]{:S(2)}) collective-permute-start(f32[4,8,128]{2,1,0:T(8,128)S(1)} %pad_maximum_fusion.1), channel_id=1, source_target_pairs={{0,8},{1,9},{2,10},{3,11},{4,12},{5,13},{6,14},{7,15},{8,16},{9,17... | collective-permute-start | bytes 49160 | tf_op jit(solution)/shard_map/ppermute | solution.py:45
  69.3 4.1 %collective-permute-start.22 = (f32[4,8,128]{2,1,0:T(8,128)S(1)}, f32[4,8,128]{2,1,0:T(8,128)S(1)}, u32[]{:S(2)}, u32[]{:S(2)}) collective-permute-start(f32[4,8,128]{2,1,0:T(8,128)S(1)} %pad_maximum_fusion.1), channel_id=1, source_target_pairs={{0,16},{1,17},{2,18},{3,19},{4,20},{5,21},{6,22},{7,23},{8,24},{9,... | collective-permute-start | bytes 49160 | tf_op jit(solution)/shard_map/ppermute | solution.py:45
  73.5 3.4 %collective-permute-start.27 = (f32[4,4,128]{2,1,0:T(4,128)S(1)}, f32[4,4,128]{2,1,0:T(4,128)S(1)}, u32[]{:S(2)}, u32[]{:S(2)}) collective-permute-start(f32[4,4,128]{2,1,0:T(4,128)S(1)} %exponential_multiply_fusion.refs_0_), channel_id=1, source_target_pairs={{0,32},{1,33},{2,34},{3,35},{4,36},{5,37},{6,38},{7,39},{8,40},{9,... | collective-permute-start | bytes 24584 | tf_op jit(solution)/shard_map/core/ppermute | solution.py:41

commit v6 on v5

--- a/solution.py
+++ b/solution.py
@@ -45,7 +45,7 @@
     return lax.ppermute(value, AXES, along(*axes, by))
 
 
-COST = 1
+COST = 4
 SWAPS = ((), (0, 1), (2, 3))
 SLOTS = 3
 SPLIT = 2

time: 85.1 us -> 84.7 us (level)
  no operation moved by 1% of the time
where the time goes in v6:
time: 84.7 us; the launch traced here: 84.5 us
  starting transfers between devices  39.9 us (47%)
  waiting for transfers between devices  24.3 us (29%)
  Pallas kernels  17.5 us (21%)
  between operations  1.07 us (1%)
  local copies, waits for them, and re-layouts  0.99 us (1%)
    ppermute x21, starting transfers between devices, shift(): return lax.ppermute(value, AXES, along(*axes, by))  29.8 us
    ppermute x21, waiting for transfers between devices, shift(): return lax.ppermute(value, AXES, along(*axes, by))  23.4 us
    ppermute x7, starting transfers between devices, to_core(): return lax.ppermute(value, AXES, pairs)  10 us
    pallas_call x4, Pallas kernels, score_rows(): pl.pallas_call(functools.partial(score_kernel, scale, units), out_shape=(...  9.67 us
    pallas_call x1, Pallas kernels, weight_all(): pl.pallas_call(functools.partial(weight_kernel, spots, float(total_rows))...  7.8 us
  transfers between devices with their start and end apart: 28, of which 15 were waited for; matrix products, arithmetic and copies ran while one was open for 2% of the time, Pallas kernels for 9%

profile of v6, /device:TPU:1, one launch (start us, length us, event | category | flops | bytes accessed | tf_op | source)
XLA Modules:
  0.0 84.5 jit_solution(13897732239418788448)
XLA Ops:
  0.6 1.5 %collective-permute-start.3 = (bf16[512,1024]{1,0:T(8,128)(2,1)}, bf16[512,1024]{1,0:T(8,128)(2,1)S(1)}, u32[]{:S(2)}, u32[]{:S(2)}) collective-permute-start(bf16[512,1024]{1,0:T(8,128)(2,1)} %cent_a.3), channel_id=1, source_target_pairs={{0,32},{1,33},{2,34},{3,35},{4,36},{5,37},{6,38},{7,39},{8,40},{9,... | collective-permute-start | bytes 3145736 | tf_op jit(solution)/shard_map/core/ppermute | solution.py:41
  2.1 3.8 %collective-permute-start.2 = (bf16[32,1024]{1,0:T(8,128)(2,1)}, bf16[32,1024]{1,0:T(8,128)(2,1)S(1)}, u32[]{:S(2)}, u32[]{:S(2)}) collective-permute-start(bf16[32,1024]{1,0:T(8,128)(2,1)} %bitcast.23), channel_id=1, source_target_pairs={{0,65},{1,64},{2,67},{3,66},{4,69},{5,68},{6,71},{7,70},{8,73},{9,... | collective-permute-start | bytes 196616 | tf_op jit(solution)/shard_map/ppermute | solution.py:45
  6.0 0.0 collective-permute-start.1
  6.0 1.3 %collective-permute-start = (bf16[32,1024]{1,0:T(8,128)(2,1)}, bf16[32,1024]{1,0:T(8,128)(2,1)S(1)}, u32[]{:S(2)}, u32[]{:S(2)}) collective-permute-start(bf16[32,1024]{1,0:T(8,128)(2,1)} %bitcast.25), channel_id=1, source_target_pairs={{0,1},{1,0},{2,3},{3,2},{4,5},{5,4},{6,7},{7,6},{8,9},{9,8},{10,11... | collective-permute-start | bytes 196616 | tf_op jit(solution)/shard_map/ppermute | solution.py:45
  7.3 0.7 convert_multiply_fusion
  8.0 0.1 collective-permute-start.4
  8.1 0.9 %bitcast_dynamic-update-slice_fusion.3 = bf16[4,32,1024]{2,1,0:T(8,128)(2,1)S(1)} fusion(bf16[4,32,1024]{2,1,0:T(8,128)(2,1)S(1)} %broadcast_in_dim.19, s32[]{:T(128)S(6)} %select_n.32, bf16[1,32,1024]{2,1,0:T(8,128)(2,1)} %bitcast.26), kind=kLoop, calls=%fused_computation.3 | loop fusion | bytes 131076 | tf_op jit(solution)/shard_map/jit(dynamic_update_index_in_dim)/dynamic_update_slice | solution.py:59
  8.9 2.0 %collective-permute-done = bf16[32,1024]{1,0:T(8,128)(2,1)S(1)} collective-permute-done((bf16[32,1024]{1,0:T(8,128)(2,1)}, bf16[32,1024]{1,0:T(8,128)(2,1)S(1)}, u32[]{:S(2)}, u32[]{:S(2)}) %collective-permute-start) | collective-permute-done | bytes 65568 | tf_op jit(solution)/shard_map/ppermute | solution.py:45
  10.9 0.3 collective-permute-done.1
  11.3 0.0 collective-permute-done.3.cent_b
  11.3 1.3 %collective-permute-start.8 = (bf16[128,1024]{1,0:T(8,128)(2,1)S(1)}, bf16[128,1024]{1,0:T(8,128)(2,1)S(1)}, u32[]{:S(2)}, u32[]{:S(2)}) collective-permute-start(bf16[128,1024]{1,0:T(8,128)(2,1)S(1)} %bitcast.19), channel_id=1, source_target_pairs={{0,2},{1,3},{2,4},{3,5},{4,6},{5,7},{6,0},{7,1},{8,10},{9,11},{10,... | collective-permute-start | bytes 786440 | tf_op jit(solution)/shard_map/mid/ppermute | solution.py:45
  12.6 2.5 %collective-permute-start.9 = (bf16[128,1024]{1,0:T(8,128)(2,1)S(1)}, bf16[128,1024]{1,0:T(8,128)(2,1)S(1)}, u32[]{:S(2)}, u32[]{:S(2)}) collective-permute-start(bf16[128,1024]{1,0:T(8,128)(2,1)S(1)} %bitcast.20), channel_id=1, source_target_pairs={{0,4},{1,5},{2,6},{3,7},{4,0},{5,1},{6,2},{7,3},{8,12},{9,13},{10,... | collective-permute-start | bytes 786440 | tf_op jit(solution)/shard_map/mid/ppermute | solution.py:45
  15.0 1.2 %collective-permute-start.5 = (bf16[128,1024]{1,0:T(8,128)(2,1)S(1)}, bf16[128,1024]{1,0:T(8,128)(2,1)S(1)}, u32[]{:S(2)}, u32[]{:S(2)}) collective-permute-start(bf16[128,1024]{1,0:T(8,128)(2,1)S(1)} %bitcast.21), channel_id=1, source_target_pairs={{0,6},{1,7},{2,0},{3,1},{4,2},{5,3},{6,4},{7,5},{8,14},{9,15},{10,... | collective-permute-start | bytes 786440 | tf_op jit(solution)/shard_map/mid/ppermute | solution.py:45
  16.2 1.9 %collective-permute-done.8 = bf16[128,1024]{1,0:T(8,128)(2,1)S(1)} collective-permute-done((bf16[128,1024]{1,0:T(8,128)(2,1)S(1)}, bf16[128,1024]{1,0:T(8,128)(2,1)S(1)}, u32[]{:S(2)}, u32[]{:S(2)}) %collective-permute-start.8) | collective-permute-done | bytes 262176 | tf_op jit(solution)/shard_map/mid/ppermute | solution.py:45
  18.1 3.8 %collective-permute-done.9 = bf16[128,1024]{1,0:T(8,128)(2,1)S(1)} collective-permute-done((bf16[128,1024]{1,0:T(8,128)(2,1)S(1)}, bf16[128,1024]{1,0:T(8,128)(2,1)S(1)}, u32[]{:S(2)}, u32[]{:S(2)}) %collective-permute-start.9) | collective-permute-done | bytes 262176 | tf_op jit(solution)/shard_map/mid/ppermute | solution.py:45
  21.9 2.5 %collective-permute-start.10 = (bf16[256,1024]{1,0:T(8,128)(2,1)S(1)}, bf16[256,1024]{1,0:T(8,128)(2,1)S(1)}, u32[]{:S(2)}, u32[]{:S(2)}) collective-permute-start(bf16[256,1024]{1,0:T(8,128)(2,1)S(1)} %constant_dynamic-update-slice_fusion.2.rows_b), channel_id=1, source_target_pairs={{0,24},{1,25},{2,26},{3,27},{4,28},{5,29},{6,30},{7,31},{8,0},{9,1... | collective-permute-start | bytes 1572872 | tf_op jit(solution)/shard_map/last/ppermute | solution.py:45
  24.4 0.1 collective-permute-start.6
  24.5 2.7 %collective-permute-start.13 = (bf16[256,1024]{1,0:T(8,128)(2,1)S(1)}, bf16[256,1024]{1,0:T(8,128)(2,1)S(1)}, u32[]{:S(2)}, u32[]{:S(2)}) collective-permute-start(bf16[256,1024]{1,0:T(8,128)(2,1)S(1)} %constant_dynamic-update-slice_fusion.rows_a), channel_id=1, source_target_pairs={{0,24},{1,25},{2,26},{3,27},{4,28},{5,29},{6,30},{7,31},{8,0},{9,1... | collective-permute-start | bytes 1572872 | tf_op jit(solution)/shard_map/last/ppermute | solution.py:45
  27.2 2.5 %scores.4 = (bf16[2,256,512]{2,1,0:T(8,128)(2,1)}, bf16[2,256,1536]{2,1,0:T(8,128)(2,1)S(1)}, f32[4,8,128]{2,1,0:T(8,128)S(1)}) custom-call(bf16[256,1024]{1,0:T(8,128)(2,1)S(1)} %constant_dynamic-update-slice_fusion.rows_a, bf16[256,1024]{1,0:T(8,128)(2,1)S(1)} %constant_dynamic-update-slice_fusion.2.rows_b, bf16[512,1024]{1,0:T(8,128)(2,1)S(1)} %copy-done.4, ...), custom_call_target="tpu_custom_call" | custom-call | flops 4294967296 | bytes 16777216 | tf_op jit(solution)/shard_map/scores/pallas_call | solution.py:140
  29.7 0.9 %collective-permute-done.10.rows_b = bf16[256,1024]{1,0:T(8,128)(2,1)S(1)} collective-permute-done((bf16[256,1024]{1,0:T(8,128)(2,1)S(1)}, bf16[256,1024]{1,0:T(8,128)(2,1)S(1)}, u32[]{:S(2)}, u32[]{:S(2)}) %collective-permute-start.10) | collective-permute-done | bytes 524320 | tf_op jit(solution)/shard_map/last/ppermute | solution.py:45
  30.5 3.4 %collective-permute-start.11 = (bf16[256,1024]{1,0:T(8,128)(2,1)S(1)}, bf16[256,1024]{1,0:T(8,128)(2,1)S(1)}, u32[]{:S(2)}, u32[]{:S(2)}) collective-permute-start(bf16[256,1024]{1,0:T(8,128)(2,1)S(1)} %collective-permute-done.10.rows_b), channel_id=1, source_target_pairs={{0,24},{1,25},{2,26},{3,27},{4,28},{5,29},{6,30},{7,31},{8,0},{9,1... | collective-permute-start | bytes 1572872 | tf_op jit(solution)/shard_map/across/ppermute | solution.py:45
  33.9 0.1 collective-permute-done.6.rows_a
  34.0 2.4 %scores.5 = (bf16[2,256,512]{2,1,0:T(8,128)(2,1)}, bf16[2,256,1536]{2,1,0:T(8,128)(2,1)S(1)}, f32[4,8,128]{2,1,0:T(8,128)S(1)}) custom-call(bf16[256,1024]{1,0:T(8,128)(2,1)S(1)} %collective-permute-done.6.rows_a, bf16[256,1024]{1,0:T(8,128)(2,1)S(1)} %collective-permute-done.10.rows_b, bf16[512,1024]{1,0:T(8,128)(2,1)S(1)} %copy-done.4, ...), custom_call_target="tpu_custom_call" | custom-call | flops 4294967296 | bytes 16777216 | tf_op jit(solution)/shard_map/scores/pallas_call | solution.py:140
  36.5 3.2 %collective-permute-done.12.rows_a = bf16[256,1024]{1,0:T(8,128)(2,1)S(1)} collective-permute-done((bf16[256,1024]{1,0:T(8,128)(2,1)S(1)}, bf16[256,1024]{1,0:T(8,128)(2,1)S(1)}, u32[]{:S(2)}, u32[]{:S(2)}) %collective-permute-start.12) | collective-permute-done | bytes 524320 | tf_op jit(solution)/shard_map/last/ppermute | solution.py:45
  39.7 2.4 %scores.6 = (bf16[2,256,512]{2,1,0:T(8,128)(2,1)}, bf16[2,256,1536]{2,1,0:T(8,128)(2,1)S(1)}, f32[4,8,128]{2,1,0:T(8,128)S(1)}) custom-call(bf16[256,1024]{1,0:T(8,128)(2,1)S(1)} %collective-permute-done.12.rows_a, bf16[256,1024]{1,0:T(8,128)(2,1)S(1)} %collective-permute-done.13.rows_b, bf16[512,1024]{1,0:T(8,128)(2,1)S(1)} %copy-done.4, ...), custom_call_target="tpu_custom_call" | custom-call | flops 4294967296 | bytes 16777216 | tf_op jit(solution)/shard_map/scores/pallas_call | solution.py:140
  42.1 3.2 %collective-permute-done.7.rows_a = bf16[256,1024]{1,0:T(8,128)(2,1)S(1)} collective-permute-done((bf16[256,1024]{1,0:T(8,128)(2,1)S(1)}, bf16[256,1024]{1,0:T(8,128)(2,1)S(1)}, u32[]{:S(2)}, u32[]{:S(2)}) %collective-permute-start.7) | collective-permute-done | bytes 524320 | tf_op jit(solution)/shard_map/across/ppermute | solution.py:45
  45.3 2.4 %scores.7 = (bf16[2,256,512]{2,1,0:T(8,128)(2,1)}, bf16[2,256,1536]{2,1,0:T(8,128)(2,1)S(1)}, f32[4,8,128]{2,1,0:T(8,128)S(1)}) custom-call(bf16[256,1024]{1,0:T(8,128)(2,1)S(1)} %collective-permute-done.7.rows_a, bf16[256,1024]{1,0:T(8,128)(2,1)S(1)} %collective-permute-done.11.rows_b, bf16[512,1024]{1,0:T(8,128)(2,1)S(1)} %copy-done.4, ...), custom_call_target="tpu_custom_call" | custom-call | flops 4294967296 | bytes 16777216 | tf_op jit(solution)/shard_map/scores/pallas_call | solution.py:140
  47.7 2.4 %collective-permute-start.16 = (f32[4,8,128]{2,1,0:T(8,128)S(1)}, f32[4,8,128]{2,1,0:T(8,128)S(1)}, u32[]{:S(2)}, u32[]{:S(2)}) collective-permute-start(f32[4,8,128]{2,1,0:T(8,128)S(1)} %get-tuple-element.66), channel_id=1, source_target_pairs={{0,65},{1,64},{2,67},{3,66},{4,69},{5,68},{6,71},{7,70},{8,73},{9,... | collective-permute-start | bytes 49160 | tf_op jit(solution)/shard_map/ppermute | solution.py:45
  50.1 0.0 collective-permute-start.15
  50.1 1.4 %collective-permute-start.14 = (f32[4,8,128]{2,1,0:T(8,128)S(1)}, f32[4,8,128]{2,1,0:T(8,128)S(1)}, u32[]{:S(2)}, u32[]{:S(2)}) collective-permute-start(f32[4,8,128]{2,1,0:T(8,128)S(1)} %get-tuple-element.66), channel_id=1, source_target_pairs={{0,1},{1,0},{2,3},{3,2},{4,5},{5,4},{6,7},{7,6},{8,9},{9,8},{10,11... | collective-permute-start | bytes 49160 | tf_op jit(solution)/shard_map/ppermute | solution.py:45
  51.5 2.4 %collective-permute-done.15 = f32[4,8,128]{2,1,0:T(8,128)S(1)} collective-permute-done((f32[4,8,128]{2,1,0:T(8,128)S(1)}, f32[4,8,128]{2,1,0:T(8,128)S(1)}, u32[]{:S(2)}, u32[]{:S(2)}) %collective-permute-start.15) | collective-permute-done | bytes 16416 | tf_op jit(solution)/shard_map/ppermute | solution.py:45
  53.9 0.3 collective-permute-done.14
  54.2 5.6 %collective-permute-start.20 = (bf16[2,256,1536]{2,1,0:T(8,128)(2,1)S(1)}, bf16[2,256,1536]{2,1,0:T(8,128)(2,1)S(1)}, u32[]{:S(2)}, u32[]{:S(2)}) collective-permute-start(bf16[2,256,1536]{2,1,0:T(8,128)(2,1)S(1)} %get-tuple-element.86.refs_6_), channel_id=1, source_target_pairs={{0,32},{1,33},{2,34},{3,35},{4,36},{5,37},{6,38},{7,39},{8,40},{9,... | collective-permute-start | bytes 4718600 | tf_op jit(solution)/shard_map/core/ppermute | solution.py:41
  59.8 0.1 collective-permute-start.21
  59.9 3.0 %collective-permute-start.19 = (f32[4,8,128]{2,1,0:T(8,128)S(1)}, f32[4,8,128]{2,1,0:T(8,128)S(1)}, u32[]{:S(2)}, u32[]{:S(2)}) collective-permute-start(f32[4,8,128]{2,1,0:T(8,128)S(1)} %pad_maximum_fusion), channel_id=1, source_target_pairs={{0,6},{1,7},{2,0},{3,1},{4,2},{5,3},{6,4},{7,5},{8,14},{9,15},{10,... | collective-permute-start | bytes 49160 | tf_op jit(solution)/shard_map/ppermute | solution.py:45
  62.8 1.2 %collective-permute-start.17 = (f32[4,8,128]{2,1,0:T(8,128)S(1)}, f32[4,8,128]{2,1,0:T(8,128)S(1)}, u32[]{:S(2)}, u32[]{:S(2)}) collective-permute-start(f32[4,8,128]{2,1,0:T(8,128)S(1)} %pad_maximum_fusion), channel_id=1, source_target_pairs={{0,4},{1,5},{2,6},{3,7},{4,0},{5,1},{6,2},{7,3},{8,12},{9,13},{10,... | collective-permute-start | bytes 49160 | tf_op jit(solution)/shard_map/ppermute | solution.py:45
  64.0 2.9 %collective-permute-done.18 = f32[4,8,128]{2,1,0:T(8,128)S(1)} collective-permute-done((f32[4,8,128]{2,1,0:T(8,128)S(1)}, f32[4,8,128]{2,1,0:T(8,128)S(1)}, u32[]{:S(2)}, u32[]{:S(2)}) %collective-permute-start.18) | collective-permute-done | bytes 16416 | tf_op jit(solution)/shard_map/ppermute | solution.py:45
  66.9 0.2 collective-permute-done.17
  67.2 0.5 collective-permute-start.25
  67.7 0.1 collective-permute-start.26
  67.8 1.0 %collective-permute-start.24 = (f32[4,8,128]{2,1,0:T(8,128)S(1)}, f32[4,8,128]{2,1,0:T(8,128)S(1)}, u32[]{:S(2)}, u32[]{:S(2)}) collective-permute-start(f32[4,8,128]{2,1,0:T(8,128)S(1)} %pad_maximum_fusion.1), channel_id=1, source_target_pairs={{0,24},{1,25},{2,26},{3,27},{4,28},{5,29},{6,30},{7,31},{8,0},{9,1... | collective-permute-start | bytes 49160 | tf_op jit(solution)/shard_map/ppermute | solution.py:45
  68.9 0.4 collective-permute-start.23
  69.3 1.7 %collective-permute-start.22 = (f32[4,8,128]{2,1,0:T(8,128)S(1)}, f32[4,8,128]{2,1,0:T(8,128)S(1)}, u32[]{:S(2)}, u32[]{:S(2)}) collective-permute-start(f32[4,8,128]{2,1,0:T(8,128)S(1)} %pad_maximum_fusion.1), channel_id=1, source_target_pairs={{0,16},{1,17},{2,18},{3,19},{4,20},{5,21},{6,22},{7,23},{8,24},{9,... | collective-permute-start | bytes 49160 | tf_op jit(solution)/shard_map/ppermute | solution.py:45
  71.0 1.6 %collective-permute-done.23 = f32[4,8,128]{2,1,0:T(8,128)S(1)} collective-permute-done((f32[4,8,128]{2,1,0:T(8,128)S(1)}, f32[4,8,128]{2,1,0:T(8,128)S(1)}, u32[]{:S(2)}, u32[]{:S(2)}) %collective-permute-start.23) | collective-permute-done | bytes 16416 | tf_op jit(solution)/shard_map/ppermute | solution.py:45
  72.7 0.7 collective-permute-done.22
  73.5 2.2 %collective-permute-start.27 = (f32[4,4,128]{2,1,0:T(4,128)S(1)}, f32[4,4,128]{2,1,0:T(4,128)S(1)}, u32[]{:S(2)}, u32[]{:S(2)}) collective-permute-start(f32[4,4,128]{2,1,0:T(4,128)S(1)} %exponential_multiply_fusion.refs_0_), channel_id=1, source_target_pairs={{0,32},{1,33},{2,34},{3,35},{4,36},{5,37},{6,38},{7,39},{8,40},{9,... | collective-permute-start | bytes 24584 | tf_op jit(solution)/shard_map/core/ppermute | solution.py:41
  75.7 0.8 collective-permute-done.27.refs_1_
  76.5 7.8 %weights.1 = (f32[2,2,2,4,4,2,16,512]{7,6,5,4,3,2,1,0:T(8,128)}, f32[512,1024]{1,0:T(8,128)}, f32[1,512]{1,0:T(1,128)}) custom-call(f32[4,4,128]{2,1,0:T(4,128)S(1)} %exponential_multiply_fusion.refs_0_, f32[4,4,128]{2,1,0:T(4,128)S(1)} %collective-permute-done.27.refs_1_, bf16[2,256,512]{2,1,0:T(8,128)(2,1)} %get-tuple-element.82.refs_2_, ...), custom_call_target="tpu_custom_call" | custom-call | tf_op jit(solution)/shard_map/weights/pallas_call | solution.py:304
  (41 shorter events, 0.3 us)
Async XLA Ops:
  0.6 26.6 %copy-start.4 = (bf16[512,1024]{1,0:T(8,128)(2,1)S(1)}, bf16[512,1024]{1,0:T(8,128)(2,1)}, u32[]{:S(2)}) copy-start(bf16[512,1024]{1,0:T(8,128)(2,1)} %cent_a.3) | copy-start | bytes 3145732
  0.6 10.6 %collective-permute-start.3 = (bf16[512,1024]{1,0:T(8,128)(2,1)}, bf16[512,1024]{1,0:T(8,128)(2,1)S(1)}, u32[]{:S(2)}, u32[]{:S(2)}) collective-permute-start(bf16[512,1024]{1,0:T(8,128)(2,1)} %cent_a.3), channel_id=1, source_target_pairs={{0,32},{1,33},{2,34},{3,35},{4,36},{5,37},{6,38},{7,39},{8,40},{9,... | collective-permute-start | bytes 3145736 | tf_op jit(solution)/shard_map/core/ppermute | solution.py:41
  2.1 9.1 %collective-permute-start.2 = (bf16[32,1024]{1,0:T(8,128)(2,1)}, bf16[32,1024]{1,0:T(8,128)(2,1)S(1)}, u32[]{:S(2)}, u32[]{:S(2)}) collective-permute-start(bf16[32,1024]{1,0:T(8,128)(2,1)} %bitcast.23), channel_id=1, source_target_pairs={{0,65},{1,64},{2,67},{3,66},{4,69},{5,68},{6,71},{7,70},{8,73},{9,... | collective-permute-start | bytes 196616 | tf_op jit(solution)/shard_map/ppermute | solution.py:45
  6.0 5.2 %collective-permute-start.1 = (bf16[32,1024]{1,0:T(8,128)(2,1)}, bf16[32,1024]{1,0:T(8,128)(2,1)S(1)}, u32[]{:S(2)}, u32[]{:S(2)}) collective-permute-start(bf16[32,1024]{1,0:T(8,128)(2,1)} %bitcast.24), channel_id=1, source_target_pairs={{0,64},{1,65},{2,66},{3,67},{4,68},{5,69},{6,70},{7,71},{8,72},{9,... | collective-permute-start | bytes 196616 | tf_op jit(solution)/shard_map/ppermute | solution.py:45
  6.0 4.9 %collective-permute-start = (bf16[32,1024]{1,0:T(8,128)(2,1)}, bf16[32,1024]{1,0:T(8,128)(2,1)S(1)}, u32[]{:S(2)}, u32[]{:S(2)}) collective-permute-start(bf16[32,1024]{1,0:T(8,128)(2,1)} %bitcast.25), channel_id=1, source_target_pairs={{0,1},{1,0},{2,3},{3,2},{4,5},{5,4},{6,7},{7,6},{8,9},{9,8},{10,11... | collective-permute-start | bytes 196616 | tf_op jit(solution)/shard_map/ppermute | solution.py:45
  8.0 3.3 %collective-permute-start.4 = (f32[1,512]{1,0:T(1,128)S(1)}, f32[1,512]{1,0:T(1,128)S(1)}, u32[]{:S(2)}, u32[]{:S(2)}) collective-permute-start(f32[1,512]{1,0:T(1,128)S(1)} %bitcast.14), channel_id=1, source_target_pairs={{0,32},{1,33},{2,34},{3,35},{4,36},{5,37},{6,38},{7,39},{8,40},{9,... | collective-permute-start | bytes 6152 | tf_op jit(solution)/shard_map/core/ppermute | solution.py:41
  11.3 6.8 %collective-permute-start.8 = (bf16[128,1024]{1,0:T(8,128)(2,1)S(1)}, bf16[128,1024]{1,0:T(8,128)(2,1)S(1)}, u32[]{:S(2)}, u32[]{:S(2)}) collective-permute-start(bf16[128,1024]{1,0:T(8,128)(2,1)S(1)} %bitcast.19), channel_id=1, source_target_pairs={{0,2},{1,3},{2,4},{3,5},{4,6},{5,7},{6,0},{7,1},{8,10},{9,11},{10,... | collective-permute-start | bytes 786440 | tf_op jit(solution)/shard_map/mid/ppermute | solution.py:45
  12.6 9.3 %collective-permute-start.9 = (bf16[128,1024]{1,0:T(8,128)(2,1)S(1)}, bf16[128,1024]{1,0:T(8,128)(2,1)S(1)}, u32[]{:S(2)}, u32[]{:S(2)}) collective-permute-start(bf16[128,1024]{1,0:T(8,128)(2,1)S(1)} %bitcast.20), channel_id=1, source_target_pairs={{0,4},{1,5},{2,6},{3,7},{4,0},{5,1},{6,2},{7,3},{8,12},{9,13},{10,... | collective-permute-start | bytes 786440 | tf_op jit(solution)/shard_map/mid/ppermute | solution.py:45
  15.0 9.4 %collective-permute-start.5 = (bf16[128,1024]{1,0:T(8,128)(2,1)S(1)}, bf16[128,1024]{1,0:T(8,128)(2,1)S(1)}, u32[]{:S(2)}, u32[]{:S(2)}) collective-permute-start(bf16[128,1024]{1,0:T(8,128)(2,1)S(1)} %bitcast.21), channel_id=1, source_target_pairs={{0,6},{1,7},{2,0},{3,1},{4,2},{5,3},{6,4},{7,5},{8,14},{9,15},{10,... | collective-permute-start | bytes 786440 | tf_op jit(solution)/shard_map/mid/ppermute | solution.py:45
  21.9 8.6 %collective-permute-start.10 = (bf16[256,1024]{1,0:T(8,128)(2,1)S(1)}, bf16[256,1024]{1,0:T(8,128)(2,1)S(1)}, u32[]{:S(2)}, u32[]{:S(2)}) collective-permute-start(bf16[256,1024]{1,0:T(8,128)(2,1)S(1)} %constant_dynamic-update-slice_fusion.2.rows_b), channel_id=1, source_target_pairs={{0,24},{1,25},{2,26},{3,27},{4,28},{5,29},{6,30},{7,31},{8,0},{9,1... | collective-permute-start | bytes 1572872 | tf_op jit(solution)/shard_map/last/ppermute | solution.py:45
  24.4 9.6 %collective-permute-start.6 = (bf16[256,1024]{1,0:T(8,128)(2,1)S(1)}, bf16[256,1024]{1,0:T(8,128)(2,1)S(1)}, u32[]{:S(2)}, u32[]{:S(2)}) collective-permute-start(bf16[256,1024]{1,0:T(8,128)(2,1)S(1)} %constant_dynamic-update-slice_fusion.rows_a), channel_id=1, source_target_pairs={{0,8},{1,9},{2,10},{3,11},{4,12},{5,13},{6,14},{7,15},{8,16},{9,17... | collective-permute-start | bytes 1572872 | tf_op jit(solution)/shard_map/last/ppermute | solution.py:45
  24.5 12.0 %collective-permute-start.13 = (bf16[256,1024]{1,0:T(8,128)(2,1)S(1)}, bf16[256,1024]{1,0:T(8,128)(2,1)S(1)}, u32[]{:S(2)}, u32[]{:S(2)}) collective-permute-start(bf16[256,1024]{1,0:T(8,128)(2,1)S(1)} %constant_dynamic-update-slice_fusion.rows_a), channel_id=1, source_target_pairs={{0,24},{1,25},{2,26},{3,27},{4,28},{5,29},{6,30},{7,31},{8,0},{9,1... | collective-permute-start | bytes 1572872 | tf_op jit(solution)/shard_map/last/ppermute | solution.py:45
  27.2 12.5 %collective-permute-start.12 = (bf16[256,1024]{1,0:T(8,128)(2,1)S(1)}, bf16[256,1024]{1,0:T(8,128)(2,1)S(1)}, u32[]{:S(2)}, u32[]{:S(2)}) collective-permute-start(bf16[256,1024]{1,0:T(8,128)(2,1)S(1)} %constant_dynamic-update-slice_fusion.2.rows_b), channel_id=1, source_target_pairs={{0,8},{1,9},{2,10},{3,11},{4,12},{5,13},{6,14},{7,15},{8,16},{9,17... | collective-permute-start | bytes 1572872 | tf_op jit(solution)/shard_map/last/ppermute | solution.py:45
  29.7 24.5 %copy-start = (bf16[2,256,1536]{2,1,0:T(8,128)(2,1)}, bf16[2,256,1536]{2,1,0:T(8,128)(2,1)S(1)}, u32[]{:S(2)}) copy-start(bf16[2,256,1536]{2,1,0:T(8,128)(2,1)S(1)} %get-tuple-element.86.refs_6_) | copy-start | bytes 4718596
  30.5 14.7 %collective-permute-start.11 = (bf16[256,1024]{1,0:T(8,128)(2,1)S(1)}, bf16[256,1024]{1,0:T(8,128)(2,1)S(1)}, u32[]{:S(2)}, u32[]{:S(2)}) collective-permute-start(bf16[256,1024]{1,0:T(8,128)(2,1)S(1)} %collective-permute-done.10.rows_b), channel_id=1, source_target_pairs={{0,24},{1,25},{2,26},{3,27},{4,28},{5,29},{6,30},{7,31},{8,0},{9,1... | collective-permute-start | bytes 1572872 | tf_op jit(solution)/shard_map/across/ppermute | solution.py:45
  34.0 11.2 %collective-permute-start.7 = (bf16[256,1024]{1,0:T(8,128)(2,1)S(1)}, bf16[256,1024]{1,0:T(8,128)(2,1)S(1)}, u32[]{:S(2)}, u32[]{:S(2)}) collective-permute-start(bf16[256,1024]{1,0:T(8,128)(2,1)S(1)} %collective-permute-done.6.rows_a), channel_id=1, source_target_pairs={{0,8},{1,9},{2,10},{3,11},{4,12},{5,13},{6,14},{7,15},{8,16},{9,17... | collective-permute-start | bytes 1572872 | tf_op jit(solution)/shard_map/across/ppermute | solution.py:45
  36.5 23.3 %copy-start.1 = (bf16[2,256,1536]{2,1,0:T(8,128)(2,1)}, bf16[2,256,1536]{2,1,0:T(8,128)(2,1)S(1)}, u32[]{:S(2)}) copy-start(bf16[2,256,1536]{2,1,0:T(8,128)(2,1)S(1)} %get-tuple-element.87.refs_7_) | copy-start | bytes 4718596
  42.1 25.2 %copy-start.2 = (bf16[2,256,1536]{2,1,0:T(8,128)(2,1)}, bf16[2,256,1536]{2,1,0:T(8,128)(2,1)S(1)}, u32[]{:S(2)}) copy-start(bf16[2,256,1536]{2,1,0:T(8,128)(2,1)S(1)} %get-tuple-element.88.refs_8_) | copy-start | bytes 4718596
  47.7 28.8 %copy-start.3 = (bf16[2,256,1536]{2,1,0:T(8,128)(2,1)}, bf16[2,256,1536]{2,1,0:T(8,128)(2,1)S(1)}, u32[]{:S(2)}) copy-start(bf16[2,256,1536]{2,1,0:T(8,128)(2,1)S(1)} %get-tuple-element.89.refs_9_) | copy-start | bytes 4718596
  47.7 3.8 %collective-permute-start.16 = (f32[4,8,128]{2,1,0:T(8,128)S(1)}, f32[4,8,128]{2,1,0:T(8,128)S(1)}, u32[]{:S(2)}, u32[]{:S(2)}) collective-permute-start(f32[4,8,128]{2,1,0:T(8,128)S(1)} %get-tuple-element.66), channel_id=1, source_target_pairs={{0,65},{1,64},{2,67},{3,66},{4,69},{5,68},{6,71},{7,70},{8,73},{9,... | collective-permute-start | bytes 49160 | tf_op jit(solution)/shard_map/ppermute | solution.py:45
  50.1 3.8 %collective-permute-start.15 = (f32[4,8,128]{2,1,0:T(8,128)S(1)}, f32[4,8,128]{2,1,0:T(8,128)S(1)}, u32[]{:S(2)}, u32[]{:S(2)}) collective-permute-start(f32[4,8,128]{2,1,0:T(8,128)S(1)} %get-tuple-element.66), channel_id=1, source_target_pairs={{0,64},{1,65},{2,66},{3,67},{4,68},{5,69},{6,70},{7,71},{8,72},{9,... | collective-permute-start | bytes 49160 | tf_op jit(solution)/shard_map/ppermute | solution.py:45
  50.1 4.1 %collective-permute-start.14 = (f32[4,8,128]{2,1,0:T(8,128)S(1)}, f32[4,8,128]{2,1,0:T(8,128)S(1)}, u32[]{:S(2)}, u32[]{:S(2)}) collective-permute-start(f32[4,8,128]{2,1,0:T(8,128)S(1)} %get-tuple-element.66), channel_id=1, source_target_pairs={{0,1},{1,0},{2,3},{3,2},{4,5},{5,4},{6,7},{7,6},{8,9},{9,8},{10,11... | collective-permute-start | bytes 49160 | tf_op jit(solution)/shard_map/ppermute | solution.py:45
  54.2 13.0 %collective-permute-start.20 = (bf16[2,256,1536]{2,1,0:T(8,128)(2,1)S(1)}, bf16[2,256,1536]{2,1,0:T(8,128)(2,1)S(1)}, u32[]{:S(2)}, u32[]{:S(2)}) collective-permute-start(bf16[2,256,1536]{2,1,0:T(8,128)(2,1)S(1)} %get-tuple-element.86.refs_6_), channel_id=1, source_target_pairs={{0,32},{1,33},{2,34},{3,35},{4,36},{5,37},{6,38},{7,39},{8,40},{9,... | collective-permute-start | bytes 4718600 | tf_op jit(solution)/shard_map/core/ppermute | solution.py:41
  59.8 7.4 %collective-permute-start.21 = (bf16[2,256,1536]{2,1,0:T(8,128)(2,1)S(1)}, bf16[2,256,1536]{2,1,0:T(8,128)(2,1)S(1)}, u32[]{:S(2)}, u32[]{:S(2)}) collective-permute-start(bf16[2,256,1536]{2,1,0:T(8,128)(2,1)S(1)} %get-tuple-element.87.refs_7_), channel_id=1, source_target_pairs={{0,32},{1,33},{2,34},{3,35},{4,36},{5,37},{6,38},{7,39},{8,40},{9,... | collective-permute-start | bytes 4718600 | tf_op jit(solution)/shard_map/core/ppermute | solution.py:41
  59.9 4.1 %collective-permute-start.19 = (f32[4,8,128]{2,1,0:T(8,128)S(1)}, f32[4,8,128]{2,1,0:T(8,128)S(1)}, u32[]{:S(2)}, u32[]{:S(2)}) collective-permute-start(f32[4,8,128]{2,1,0:T(8,128)S(1)} %pad_maximum_fusion), channel_id=1, source_target_pairs={{0,6},{1,7},{2,0},{3,1},{4,2},{5,3},{6,4},{7,5},{8,14},{9,15},{10,... | collective-permute-start | bytes 49160 | tf_op jit(solution)/shard_map/ppermute | solution.py:45
  62.8 4.1 %collective-permute-start.18 = (f32[4,8,128]{2,1,0:T(8,128)S(1)}, f32[4,8,128]{2,1,0:T(8,128)S(1)}, u32[]{:S(2)}, u32[]{:S(2)}) collective-permute-start(f32[4,8,128]{2,1,0:T(8,128)S(1)} %pad_maximum_fusion), channel_id=1, source_target_pairs={{0,2},{1,3},{2,4},{3,5},{4,6},{5,7},{6,0},{7,1},{8,10},{9,11},{10,... | collective-permute-start | bytes 49160 | tf_op jit(solution)/shard_map/ppermute | solution.py:45
  62.8 4.3 %collective-permute-start.17 = (f32[4,8,128]{2,1,0:T(8,128)S(1)}, f32[4,8,128]{2,1,0:T(8,128)S(1)}, u32[]{:S(2)}, u32[]{:S(2)}) collective-permute-start(f32[4,8,128]{2,1,0:T(8,128)S(1)} %pad_maximum_fusion), channel_id=1, source_target_pairs={{0,4},{1,5},{2,6},{3,7},{4,0},{5,1},{6,2},{7,3},{8,12},{9,13},{10,... | collective-permute-start | bytes 49160 | tf_op jit(solution)/shard_map/ppermute | solution.py:45
  67.2 6.2 %collective-permute-start.25 = (bf16[2,256,1536]{2,1,0:T(8,128)(2,1)S(1)}, bf16[2,256,1536]{2,1,0:T(8,128)(2,1)S(1)}, u32[]{:S(2)}, u32[]{:S(2)}) collective-permute-start(bf16[2,256,1536]{2,1,0:T(8,128)(2,1)S(1)} %get-tuple-element.88.refs_8_), channel_id=1, source_target_pairs={{0,32},{1,33},{2,34},{3,35},{4,36},{5,37},{6,38},{7,39},{8,40},{9,... | collective-permute-start | bytes 4718600 | tf_op jit(solution)/shard_map/core/ppermute | solution.py:41
  67.7 5.7 %collective-permute-start.26 = (bf16[2,256,1536]{2,1,0:T(8,128)(2,1)S(1)}, bf16[2,256,1536]{2,1,0:T(8,128)(2,1)S(1)}, u32[]{:S(2)}, u32[]{:S(2)}) collective-permute-start(bf16[2,256,1536]{2,1,0:T(8,128)(2,1)S(1)} %get-tuple-element.89.refs_9_), channel_id=1, source_target_pairs={{0,32},{1,33},{2,34},{3,35},{4,36},{5,37},{6,38},{7,39},{8,40},{9,... | collective-permute-start | bytes 4718600 | tf_op jit(solution)/shard_map/core/ppermute | solution.py:41
  67.8 3.2 %collective-permute-start.24 = (f32[4,8,128]{2,1,0:T(8,128)S(1)}, f32[4,8,128]{2,1,0:T(8,128)S(1)}, u32[]{:S(2)}, u32[]{:S(2)}) collective-permute-start(f32[4,8,128]{2,1,0:T(8,128)S(1)} %pad_maximum_fusion.1), channel_id=1, source_target_pairs={{0,24},{1,25},{2,26},{3,27},{4,28},{5,29},{6,30},{7,31},{8,0},{9,1... | collective-permute-start | bytes 49160 | tf_op jit(solution)/shard_map/ppermute | solution.py:45
  68.9 3.8 %collective-permute-start.23 = (f32[4,8,128]{2,1,0:T(8,128)S(1)}, f32[4,8,128]{2,1,0:T(8,128)S(1)}, u32[]{:S(2)}, u32[]{:S(2)}) collective-permute-start(f32[4,8,128]{2,1,0:T(8,128)S(1)} %pad_maximum_fusion.1), channel_id=1, source_target_pairs={{0,8},{1,9},{2,10},{3,11},{4,12},{5,13},{6,14},{7,15},{8,16},{9,17... | collective-permute-start | bytes 49160 | tf_op jit(solution)/shard_map/ppermute | solution.py:45
  69.3 4.1 %collective-permute-start.22 = (f32[4,8,128]{2,1,0:T(8,128)S(1)}, f32[4,8,128]{2,1,0:T(8,128)S(1)}, u32[]{:S(2)}, u32[]{:S(2)}) collective-permute-start(f32[4,8,128]{2,1,0:T(8,128)S(1)} %pad_maximum_fusion.1), channel_id=1, source_target_pairs={{0,16},{1,17},{2,18},{3,19},{4,20},{5,21},{6,22},{7,23},{8,24},{9,... | collective-permute-start | bytes 49160 | tf_op jit(solution)/shard_map/ppermute | solution.py:45
  73.5 3.0 %collective-permute-start.27 = (f32[4,4,128]{2,1,0:T(4,128)S(1)}, f32[4,4,128]{2,1,0:T(4,128)S(1)}, u32[]{:S(2)}, u32[]{:S(2)}) collective-permute-start(f32[4,4,128]{2,1,0:T(4,128)S(1)} %exponential_multiply_fusion.refs_0_), channel_id=1, source_target_pairs={{0,32},{1,33},{2,34},{3,35},{4,36},{5,37},{6,38},{7,39},{8,40},{9,... | collective-permute-start | bytes 24584 | tf_op jit(solution)/shard_map/core/ppermute | solution.py:41
